TPU v7x, 128 devices: a whole 4x4x4 slice. The times are simulated.
128 devices in a mesh: lists: 8 (over x, core), score: 16 (over y, z).
Axes of the slice: x: 4, y: 4, z: 4, core: 2. Of those that a mesh axis runs over, the one named last changes fastest.
Arguments:
- queries: bfloat16 [512, 32, 128], P('score', 'lists'), may hold values from -0.59765625 to 0.59765625
- centroids: bfloat16 [65536, 128], P('lists'), may hold values from -3 to 3
- codes: bfloat16 [4096, 128, 128], P(('lists', 'score')), may hold values from -6 to 6
- scales: float32 [4096, 128], P(('lists', 'score')), may hold values from 0.1 to 1
- centroid_ids: int32 [4096, 128], P(('lists', 'score')), may hold values from 0 to 8191
- lengths: int32 [4096], P(('lists', 'score')), may hold values from 1 to 128
- owners: int32 [8, 512, 8], P('lists', 'score'), may hold values from 0 to 127, all different within a row; in each aligned block of 32 rows (0 to 31, 32 to 63, ..., all dimensions but the last counted through in order) at most 4 rows name the same one
- slots: int32 [8, 512, 8], P('lists', 'score'), may hold values from 0 to 31
Outputs:
- scores: float32 [8, 512, 8], P('lists', 'score')
- relevance: float32 [512, 65536], P('score', 'lists')
Inputs may be any that keep to these rules, and one draw needn't show every extreme that they name: Within the 32 rows of one device (aligned blocks of 32 rows, the first two dimensions taken together in order) no owner is named more than 4 times; each row names 8 different owners. Owner d holds blocks d * 32 to d * 32 + 31. `centroid_ids`: A row among the 8192 centroids of the block's lists shard.
All inputs are finite; a program needn't handle non-finite values.
Results may differ from a plain program's by a relative error of at most 0.00034.
Values may be sent and summed in bfloat16 or wider, within the bound.
No kernel may reach another device: no remote copies, remote signals or barrier semaphores. Data moves between devices by JAX's collectives and lax.ppermute only.
A program may use at most 128 MiB of HBM per device.

v0:
```python
import math

import jax
import jax.numpy as jnp
from jax import lax
from jax.sharding import PartitionSpec as P


def laid_out(tiles, dim):
    shape = list(tiles.shape[1:])
    shape[dim] *= tiles.shape[0]
    return jnp.moveaxis(tiles, 0, dim).reshape(shape)


def sent_to_all(value, axis):
    peers = lax.axis_size(axis)
    return lax.all_to_all(
        jnp.broadcast_to(value[None], (peers, *value.shape)), axis, 0, 0, tiled=True
    )


def gathered_copies(value, axis, dim):
    return laid_out(sent_to_all(value, axis), dim)


def rebuild_held(codes, scales, centroid_ids, centroids):
    held = codes.shape[0]
    slot_len = codes.shape[1]
    width = codes.shape[2]
    base = (
        jnp.take(centroids, centroid_ids.reshape(-1), axis=0)
        .astype(jnp.float32)
        .reshape(held, slot_len, width)
    )
    vectors = base + scales[..., None] * codes.astype(jnp.float32)
    return vectors.astype(jnp.bfloat16).reshape(held, slot_len * width)


def pick_blocks(held_vectors, lengths, wanted):
    held = held_vectors.shape[0]
    picker = wanted[:, None] == jnp.arange(held, dtype=jnp.int32)[None, :]
    picked = jnp.dot(
        picker.astype(jnp.bfloat16), held_vectors, preferred_element_type=jnp.float32
    ).astype(jnp.bfloat16)
    picked_len = jnp.sum(jnp.where(picker, lengths[None, :], 0), axis=1)
    return (picked, picked_len)


def maxsim_total(inner, valid_count, token_count):
    spots = jnp.arange(inner.shape[-1], dtype=jnp.int32)
    keep = spots < valid_count[..., None, None]
    best = jnp.max(jnp.where(keep, inner, -1e30), axis=-1)
    return jnp.sum(best, axis=-1) / token_count


def per_device(queries, centroids, codes, scales, centroid_ids, lengths, owners, slots):
    gathered = gathered_copies(queries, "lists", 1)
    query_rows, token_count, width = gathered.shape
    slot_len = codes.shape[1]
    cent_rows = centroids.shape[0]
    group = math.gcd(cent_rows, 4096)
    flat = gathered.reshape(query_rows * token_count, width)
    grouped = centroids.reshape(cent_rows // group, group, width)

    def relate(block_rows):
        inner = lax.dot_general(
            flat, block_rows, (((1,), (1,)), ((), ())), preferred_element_type=jnp.float32
        )
        return jnp.max(inner.reshape(query_rows, token_count, group), axis=1)

    relevance = jnp.transpose(lax.map(relate, grouped), (1, 0, 2)).reshape(query_rows, cent_rows)
    held_vectors = rebuild_held(codes, scales, centroid_ids, centroids)
    owner_flat = owners[0].reshape(-1)
    local_flat = slots[0].reshape(-1)
    count = owner_flat.shape[0]
    per_query = owners.shape[2]
    devices = lax.axis_size("lists") * lax.axis_size("score")
    capacity = max(4, 2 * -(-count // devices))
    total_slots = devices * capacity
    matches = (owner_flat[:, None] == jnp.arange(devices, dtype=jnp.int32)[None, :]).astype(
        jnp.float32
    )
    positions = jnp.arange(count, dtype=jnp.int32)
    before = (positions[:, None] > positions[None, :]).astype(jnp.float32)
    prior = jnp.dot(
        before, matches, precision=lax.Precision.HIGHEST, preferred_element_type=jnp.float32
    )
    earlier = jnp.sum(prior * matches, axis=1).astype(jnp.int32)
    placed = owner_flat * capacity + earlier
    slot_match = placed[None, :] == jnp.arange(total_slots, dtype=jnp.int32)[:, None]
    request = jnp.sum(jnp.where(slot_match, local_flat[None, :], 0), axis=1).reshape(
        devices, capacity
    )
    slot_pick = slot_match.astype(jnp.bfloat16)
    row_pick = (
        (positions // per_query)[:, None] == jnp.arange(query_rows, dtype=jnp.int32)[None, :]
    ).astype(jnp.bfloat16)
    selector = jnp.dot(slot_pick, row_pick, preferred_element_type=jnp.float32).astype(jnp.bfloat16)
    outgoing = jnp.dot(
        selector,
        gathered.reshape(query_rows, token_count * width),
        preferred_element_type=jnp.float32,
    )
    outgoing = outgoing.astype(jnp.bfloat16).reshape(devices, capacity, token_count, width)
    wanted = lax.all_to_all(request, ("lists", "score"), split_axis=0, concat_axis=0, tiled=True)
    asked = lax.all_to_all(outgoing, ("lists", "score"), split_axis=0, concat_axis=0, tiled=True)
    vectors, valid = pick_blocks(held_vectors, lengths, wanted.reshape(-1))
    vectors = vectors.reshape(wanted.shape + (slot_len, width))
    valid = valid.reshape(wanted.shape)
    inner = jnp.einsum("sctd,scpd->sctp", asked, vectors, preferred_element_type=jnp.float32)
    returned = lax.all_to_all(
        maxsim_total(inner, valid, token_count),
        ("lists", "score"),
        split_axis=0,
        concat_axis=0,
        tiled=True,
    )
    scores = returned.reshape(-1)[placed].reshape(query_rows, per_query)
    return (scores[None], relevance)


def solution(mesh):
    placed = (
        P("score", "lists", None),
        P("lists", None),
        P(("lists", "score"), None, None),
        P(("lists", "score"), None),
        P(("lists", "score"), None),
        P(("lists", "score")),
        P("lists", "score", None),
        P("lists", "score", None),
    )
    return jax.shard_map(
        per_device,
        mesh=mesh,
        in_specs=placed,
        out_specs=(P("lists", "score", None), P("score", "lists")),
        check_vma=False,
    )
```

profile of v0, /device:TPU:1, one launch (start us, length us, event | category | flops | bytes accessed | tf_op | source)
XLA Modules:
  0.0 128.7 jit_solution(7946354007883582360)
XLA Ops:
  0.6 1.5 %broadcast_in_dim.79 = bf16[8,32,4,128]{3,2,1,0:T(4,128)(2,1)} broadcast(bf16[32,4,128]{2,1,0:T(4,128)(2,1)} %param.10), dimensions={1,2,3} | broadcast | bytes 294912 | tf_op jit(solution)/shard_map/broadcast_in_dim | solution.py:18
  2.2 5.8 %all-to-all-start.1 = ((bf16[8,32,4,128]{3,2,1,0:T(4,128)(2,1)}), bf16[8,32,4,128]{3,2,1,0:T(4,128)(2,1)S(1)}, u32[]{:S(2)}, u32[]{:S(2)}) async-start(bf16[8,32,4,128]{3,2,1,0:T(4,128)(2,1)} %broadcast_in_dim.79), calls=%async_computation.1 | async-start | bytes 524288 | tf_op jit(solution)/shard_map/all_to_all | solution.py:17
  8.0 0.8 copy.39
  8.7 0.1 reshape_squeeze.3
  8.8 0.2 fusion.8
  9.1 0.8 copy.40
  9.8 0.1 broadcast_in_dim.73
  9.9 0.2 select_reduce_fusion.1
  10.1 0.7 all_to_all.16
  10.8 3.6 %all-to-all-done.1 = bf16[8,32,4,128]{3,2,1,0:T(4,128)(2,1)S(1)} async-done(((bf16[8,32,4,128]{3,2,1,0:T(4,128)(2,1)}), bf16[8,32,4,128]{3,2,1,0:T(4,128)(2,1)S(1)}, u32[]{:S(2)}, u32[]{:S(2)}) %all-to-all-start.1) | async-done | bytes 262176 | tf_op jit(solution)/shard_map/all_to_all | solution.py:17
  14.5 9.2 %all-to-all-start = ((s32[128,1,4]{2,1,0:T(1,128)}), s32[128,1,4]{2,1,0:T(1,128)S(1)}, u32[]{:S(2)}, u32[]{:S(2)}) async-start(s32[128,1,4]{2,1,0:T(1,128)} %bitcast.4), calls=%async_computation | async-start | bytes 131072 | tf_op jit(solution)/shard_map/all_to_all | solution.py:105
  23.6 0.1 copy.42
  23.7 0.0 copy-start.2
  23.8 0.2 reshape_reshape.6
  23.9 3.5 %fusion.7 = bf16[64,8,32,128]{3,1,2,0:T(8,128)(2,1)} fusion(bf16[32,4096]{1,0:T(8,128)(2,1)S(1)} %reshape_reshape.6, s32[256]{0:T(256)S(1)} %get-tuple-element.44, s32[256]{0:T(256)S(1)} %get-tuple-element.43), kind=kOutput, calls=%fused_computation.12 | convolution fusion | flops 144859136 | bytes 4458496 | tf_op jit(solution)/shard_map/dot_general | solution.py:99
  27.4 5.4 %copy.51 = bf16[64,8,32,128]{3,2,1,0:T(8,128)(2,1)} copy(bf16[64,8,32,128]{3,1,2,0:T(8,128)(2,1)} %fusion.7) | data formatting | bytes 8388608
  32.8 0.0 copy-done.2
  32.8 0.4 all-to-all-done
  33.2 0.0 copy-start.5
  33.2 0.0 copy-start.3
  33.2 0.0 copy-start
  33.2 9.8 %all-to-all-start.2 = ((bf16[128,4,32,128]{3,2,1,0:T(8,128)(2,1)}), bf16[128,4,32,128]{3,2,1,0:T(8,128)(2,1)}, u32[]{:S(2)}, u32[]{:S(2)}) async-start(bf16[128,4,32,128]{3,2,1,0:T(8,128)(2,1)} %bitcast.50), calls=%async_computation.2 | async-start | bytes 8388608 | tf_op jit(solution)/shard_map/all_to_all | solution.py:106
  43.1 0.0 copy-done.5
  43.1 0.1 copy.45
  43.2 0.1 mul.42
  43.3 0.0 copy-done.3
  43.3 0.0 copy-done
  43.3 0.0 copy-start.4
  43.3 15.0 %gather_fusion = bf16[4096,128]{1,0:T(8,128)(2,1)} fusion(bf16[8192,128]{1,0:T(8,128)(2,1)S(1)} %copy-done, s32[4096]{0:T(1024)S(1)} %broadcast_clamp_fusion), kind=kCustom, calls=%fused_computation | custom fusion | bytes 2113536 | tf_op jit(solution)/shard_map/jit(_take)/gather | solution.py:31
  58.4 0.0 copy-done.4
  58.4 3.2 %add_convert_fusion = bf16[32,128,128]{2,1,0:T(8,128)(2,1)S(1)} fusion(bf16[32,128,128]{2,1,0:T(8,128)(2,1)} %param.12, f32[32,128]{1,0:T(8,128)S(1)} %copy-done.4, bf16[32,128,128]{2,1,0:T(8,128)(2,1)} %bitcast.52, pred[32,128]{1,0:T(8,128)(4,1)S(1)} %compare_and_fusion), kind=kLoop, calls=%fused_computation.13 | loop fusion | flops 3145728 | bytes 3166208 | tf_op jit(solution)/shard_map/convert_element_type | solution.py:36
  61.6 0.5 broadcast.130
  62.1 0.8 reduce.6
  62.9 0.1 eq.60
  63.0 5.0 %fusion.6 = bf16[64,8,128,128]{3,1,2,0:T(8,128)(2,1)S(1)} fusion(bf16[4,8,128,128]{3,2,1,0:T(8,128)(2,1)S(1)} %bitcast.51, s32[512]{0:T(512)S(1)} %eq.60), kind=kOutput, calls=%fused_computation.10 | convolution fusion | flops 545275904 | bytes 17827840 | tf_op jit(solution)/shard_map/dot_general | solution.py:42
  68.0 0.0 copy-start.6
  68.0 8.4 %copy.53 = bf16[64,8,128,128]{3,2,1,0:T(8,128)(2,1)} copy(bf16[64,8,128,128]{3,1,2,0:T(8,128)(2,1)S(1)} %fusion.6) | data formatting | bytes 33554432
  76.3 0.0 copy-done.6
  76.4 0.1 select_reduce_fusion.2
  76.4 0.1 lt.57
  76.6 0.2 iota_compare_fusion.4
  76.8 18.3 %all-to-all-done.2 = bf16[128,4,32,128]{3,2,1,0:T(8,128)(2,1)} async-done(((bf16[128,4,32,128]{3,2,1,0:T(8,128)(2,1)}), bf16[128,4,32,128]{3,2,1,0:T(8,128)(2,1)}, u32[]{:S(2)}, u32[]{:S(2)}) %all-to-all-start.2) | async-done | bytes 4194336 | tf_op jit(solution)/shard_map/all_to_all | solution.py:106
  95.1 0.0 copy-start.1
  95.1 13.3 %select_reduce_fusion = f32[128,4,32]{2,1,0:T(4,128)S(1)} fusion(pred[128,4,128]{2,1,0:T(4,128)(4,1)S(1)} %iota_compare_fusion.4, bf16[128,4,32,128]{3,2,1,0:T(8,128)(2,1)} %all-to-all-done.2, bf16[128,4,128,128]{3,2,1,0:T(8,128)(2,1)} %bitcast.48), kind=kOutput, calls=%fused_computation.9 | convolution fusion | flops 541048832 | bytes 21102592 | tf_op jit(solution)/shard_map/sctd,scpd->sctp/dot_general | solution.py:110
  108.4 0.2 reduce_sum.39
  108.6 0.1 copy.54
  108.6 0.8 copy.44
  109.4 5.5 %all-to-all-start.3 = ((f32[128,1,4]{2,1,0:T(1,128)}), f32[128,1,4]{2,1,0:T(1,128)S(1)}, u32[]{:S(2)}, u32[]{:S(2)}) async-start(f32[128,1,4]{2,1,0:T(1,128)} %copy.44), calls=%async_computation.3 | async-start | bytes 131072 | tf_op jit(solution)/shard_map/all_to_all | solution.py:111
  114.9 0.0 copy-done.1
  114.9 6.8 %while.10 = (s32[]{:T(128)}, f32[2,32,4096]{2,1,0:T(8,128)S(1)}, bf16[2,4096,128]{2,1,0:T(8,128)(2,1)S(1)}, bf16[1024,128]{1,0:T(8,128)(2,1)}, s32[]{:T(128)}) while((s32[]{:T(128)}, f32[2,32,4096]{2,1,0:T(8,128)S(1)}, bf16[2,4096,128]{2,1,0:T(8,128)(2,1)S(1)}, bf16[1024,128]{1,0:T(8,128)(2,1)}, s32[]{:T(128)}) %tuple.33), condition=%wide.region_7.8_spmd, body=%wide.region_5.7_spmd.sunk | while | flops 1077805056 | bytes 2883653 | solution.py:71
  115.0 3.3 %bitcast_reduce_fusion.2 = f32[32,4096]{1,0:T(8,128)S(1)} fusion(bf16[1024,128]{1,0:T(8,128)(2,1)} %get-tuple-element.83, bf16[2,4096,128]{2,1,0:T(8,128)(2,1)S(1)} %get-tuple-element.82, s32[]{:T(128)} %get-tuple-element.75), kind=kOutput, calls=%fused_computation.2.clone.1 | convolution fusion | flops 1077805056 | bytes 1835012 | tf_op jit(solution)/shard_map/while/body/eval_jaxpr/dot_general | solution.py:66
  118.4 3.3 %bitcast_reduce_fusion.2 = f32[32,4096]{1,0:T(8,128)S(1)} fusion(bf16[1024,128]{1,0:T(8,128)(2,1)} %get-tuple-element.83, bf16[2,4096,128]{2,1,0:T(8,128)(2,1)S(1)} %get-tuple-element.82, s32[]{:T(128)} %get-tuple-element.75), kind=kOutput, calls=%fused_computation.2.clone.1 | convolution fusion | flops 1077805056 | bytes 1835012 | tf_op jit(solution)/shard_map/while/body/eval_jaxpr/dot_general | solution.py:66
  121.8 1.0 copy.50
  122.8 1.7 %all-to-all-done.3 = f32[128,1,4]{2,1,0:T(1,128)S(1)} async-done(((f32[128,1,4]{2,1,0:T(1,128)}), f32[128,1,4]{2,1,0:T(1,128)S(1)}, u32[]{:S(2)}, u32[]{:S(2)}) %all-to-all-start.3) | async-done | bytes 2080 | tf_op jit(solution)/shard_map/all_to_all | solution.py:111
  124.5 0.5 broadcast.131
  125.0 0.8 reduce.7
  125.8 0.1 reshape.157
  125.9 1.9 %gather_fusion.1 = f32[256]{0:T(256)S(1)} fusion(f32[512]{0:T(512)S(1)} %reshape.157, s32[1024]{0:T(1024)S(1)} %pad_clamp_fusion), kind=kCustom, calls=%fused_computation.1 | custom fusion | bytes 3072 | tf_op jit(solution)/shard_map/gather | solution.py:118
  127.9 0.1 broadcast_in_dim_reshape.2
  128.0 0.7 copy.48
  (12 shorter events, 0.2 us)
Async XLA Ops:
  2.2 12.3 %all-to-all-start.1 = ((bf16[8,32,4,128]{3,2,1,0:T(4,128)(2,1)}), bf16[8,32,4,128]{3,2,1,0:T(4,128)(2,1)S(1)}, u32[]{:S(2)}, u32[]{:S(2)}) async-start(bf16[8,32,4,128]{3,2,1,0:T(4,128)(2,1)} %broadcast_in_dim.79), calls=%async_computation.1 | async-start | bytes 524288 | tf_op jit(solution)/shard_map/all_to_all | solution.py:17
  14.5 18.8 %all-to-all-start = ((s32[128,1,4]{2,1,0:T(1,128)}), s32[128,1,4]{2,1,0:T(1,128)S(1)}, u32[]{:S(2)}, u32[]{:S(2)}) async-start(s32[128,1,4]{2,1,0:T(1,128)} %bitcast.4), calls=%async_computation | async-start | bytes 131072 | tf_op jit(solution)/shard_map/all_to_all | solution.py:105
  23.7 9.0 %copy-start.2 = (bf16[32,8,4,128]{3,2,1,0:T(4,128)(2,1)}, bf16[32,8,4,128]{3,2,1,0:T(4,128)(2,1)S(1)}, u32[]{:S(2)}) copy-start(bf16[32,8,4,128]{3,2,1,0:T(4,128)(2,1)S(1)} %copy.42) | copy-start | bytes 786436
  33.2 9.9 %copy-start.5 = (s32[1,32,8]{1,2,0:T(8,128)S(1)}, s32[1,32,8]{1,2,0:T(8,128)}, u32[]{:S(2)}) copy-start(s32[1,32,8]{1,2,0:T(8,128)} %param.16) | copy-start | bytes 3076
  33.2 10.0 %copy-start.3 = (s32[32,128]{1,0:T(8,128)S(1)}, s32[32,128]{1,0:T(8,128)}, u32[]{:S(2)}) copy-start(s32[32,128]{1,0:T(8,128)} %param.14) | copy-start | bytes 49156
  33.2 10.1 %copy-start = (bf16[8192,128]{1,0:T(8,128)(2,1)S(1)}, bf16[8192,128]{1,0:T(8,128)(2,1)}, u32[]{:S(2)}) copy-start(bf16[8192,128]{1,0:T(8,128)(2,1)} %param.11) | copy-start | bytes 6291460
  33.2 61.8 %all-to-all-start.2 = ((bf16[128,4,32,128]{3,2,1,0:T(8,128)(2,1)}), bf16[128,4,32,128]{3,2,1,0:T(8,128)(2,1)}, u32[]{:S(2)}, u32[]{:S(2)}) async-start(bf16[128,4,32,128]{3,2,1,0:T(8,128)(2,1)} %bitcast.50), calls=%async_computation.2 | async-start | bytes 8388608 | tf_op jit(solution)/shard_map/all_to_all | solution.py:106
  43.3 15.1 %copy-start.4 = (f32[32,128]{1,0:T(8,128)S(1)}, f32[32,128]{1,0:T(8,128)}, u32[]{:S(2)}) copy-start(f32[32,128]{1,0:T(8,128)} %param.13) | copy-start | bytes 49156
  68.0 8.4 %copy-start.6 = (s32[32]{0:T(128)S(1)}, s32[32]{0:T(128)}, u32[]{:S(2)}) copy-start(s32[32]{0:T(128)} %param.15) | copy-start | bytes 388
  95.1 19.9 %copy-start.1 = (f32[2,32,4096]{2,1,0:T(8,128)S(1)}, f32[2,32,4096]{2,1,0:T(8,128)}, u32[]{:S(2)}) copy-start(f32[2,32,4096]{2,1,0:T(8,128)} %custom-call.4) | copy-start | bytes 3145732
  109.4 15.1 %all-to-all-start.3 = ((f32[128,1,4]{2,1,0:T(1,128)}), f32[128,1,4]{2,1,0:T(1,128)S(1)}, u32[]{:S(2)}, u32[]{:S(2)}) async-start(f32[128,1,4]{2,1,0:T(1,128)} %copy.44), calls=%async_computation.3 | async-start | bytes 131072 | tf_op jit(solution)/shard_map/all_to_all | solution.py:111
where the time goes:
time: 129 us
  local copies, waits for them, and re-layouts  39.2 us (30%)
  starting transfers between devices  30.3 us (23%)
  matrix products  28.6 us (22%)
  waiting for transfers between devices  24.1 us (19%)
  other arithmetic  5.49 us (4%)
    all_to_all x1, waiting for transfers between devices, per_device(): lax.all_to_all(outgoing, ('lists', 'score'), split_axis=0, concat_axis=0,...  18.3 us
    unnamed x20, local copies, waits for them, and re-layouts  16 us
    gather x1, local copies, waits for them, and re-layouts, rebuild_held(): jnp.take(centroids, centroid_ids.reshape(-1), axis=0).astype(jnp.float32)  15 us
    dot_general x1, matrix products, per_device(): jnp.einsum('sctd,scpd->sctp', asked, vectors, preferred_element_type=jnp....  13.3 us
    all_to_all x1, starting transfers between devices, per_device(): lax.all_to_all(outgoing, ('lists', 'score'), split_axis=0, concat_axis=0,...  9.81 us
    all_to_all x1, starting transfers between devices, per_device(): lax.all_to_all(request, ('lists', 'score'), split_axis=0, concat_axis=0,...  9.18 us
    dot_general x2, matrix products, relate(): lax.dot_general(flat, block_rows, (((1,), (1,)), ((), ())), preferred_ele...  6.68 us
    all_to_all x1, starting transfers between devices, sent_to_all(): lax.all_to_all(jnp.broadcast_to(value[None], (peers, *value.shape)), axis...  5.8 us
  transfers between devices with their start and end apart: 4, of which 4 were waited for; matrix products, arithmetic and copies ran while one was open for 41% of the time, Pallas kernels for 0%

commit v1 on v0

v1 whole, which is shorter than its diff:
```python
import jax
import jax.numpy as jnp
from jax import lax
from jax.experimental import pallas as pl
from jax.experimental.pallas import tpu as pltpu
from jax.sharding import PartitionSpec as P

AXES = ("lists", "score")
SIDE = 4
CORES = 2
DEVICES = 128
CAP = 4
SMEM = pltpu.SMEM
VMEM = pltpu.VMEM


def device_of(x, core, y, z):
    x, y, z = x % SIDE, y % SIDE, z % SIDE
    return ((x * CORES + core) * SIDE + y) * SIDE + z


def moved(value, step):
    pairs = []
    for x in range(SIDE):
        for core in range(CORES):
            for y in range(SIDE):
                for z in range(SIDE):
                    pairs.append((device_of(x, core, y, z), device_of(*step(x, core, y, z))))
    return lax.ppermute(value, AXES, pairs)


def along_x(k):
    return lambda x, core, y, z: (x + k, core, y, z)


def along_first(k):
    return lambda x, core, y, z: (x, core, y + k, z) if core == 0 else (x, core, y, z + k)


def along_second(k):
    return lambda x, core, y, z: (x, core, y, z + k) if core == 0 else (x, core, y + k, z)


def other_core(x, core, y, z):
    return (x, 1 - core, y, z)


def rebuild_kernel(ids_ref, cent_ref, scale_ref, code_ref, out_ref, table, base):
    b = pl.program_id(0)

    @pl.when(b == 0)
    def _():
        table[...] = cent_ref[...].astype(jnp.float32)

    rows = base.shape[0]
    for p in range(rows):
        base[pl.ds(p, 1), :] = table[pl.ds(ids_ref[b, p], 1), :]
    scale = jnp.transpose(jnp.broadcast_to(scale_ref[0], (rows, rows)))
    out_ref[0] = (base[...] + scale * code_ref[0].astype(jnp.float32)).astype(jnp.bfloat16)


def rebuild(codes, scales, centroid_ids, centroids):
    held, rows, width = codes.shape
    return pl.pallas_call(
        rebuild_kernel,
        grid=(held,),
        out_shape=jax.ShapeDtypeStruct(codes.shape, jnp.bfloat16),
        in_specs=[
            pl.BlockSpec(memory_space=SMEM),
            pl.BlockSpec(centroids.shape, lambda b: (0, 0)),
            pl.BlockSpec((1, 1, rows), lambda b: (b, 0, 0)),
            pl.BlockSpec((1, rows, width), lambda b: (b, 0, 0)),
        ],
        out_specs=pl.BlockSpec((1, rows, width), lambda b: (b, 0, 0)),
        scratch_shapes=[
            VMEM(centroids.shape, jnp.float32),
            VMEM((rows, width), jnp.float32),
        ],
        compiler_params=pltpu.CompilerParams(vmem_limit_bytes=32 << 20),
        cost_estimate=pl.CostEstimate(flops=12000000, bytes_accessed=20000000, transcendentals=0),
        name="rebuild",
    )(centroid_ids, centroids, scales.reshape(held, 1, rows), codes)


UNROLL = 8


def maxsim_kernel(
    where_ref, lengths_ref, own_ref, other_ref, held_ref, out_ref, meta, table, rows_ref, work, sem
):
    groups = SIDE * SIDE
    per = own_ref.shape[0] // groups
    queries = per - 1
    sources = groups * SIDE
    me, my_x, my_core, my_y, my_z = (where_ref[i] for i in range(5))
    for half, ref in enumerate((own_ref, other_ref)):
        for i in range(groups):
            meta[pl.ds((half * groups + i) * 16, 16), :] = ref[i * per + queries].astype(jnp.float32)
    count = 2 * sources
    lane = lax.broadcasted_iota(jnp.int32, (count, 128), 1)
    parts = [meta[pl.ds(row, count, stride=4), :] for row in range(4)]
    hit, slot = jnp.zeros((count, 128), jnp.float32), jnp.zeros((count, 128), jnp.float32)
    for owner, place in ((parts[0], parts[2]), (parts[1], parts[3])):
        mine = owner == me.astype(jnp.float32)
        hit += jnp.where(mine, 1.0, 0.0)
        slot += jnp.where(mine, place, 0.0)
    for shift in (64, 32):
        hit = hit + pltpu.roll(hit, shift, 1)
        slot = slot + pltpu.roll(slot, shift, 1)
    row_id = lax.broadcasted_iota(jnp.int32, (128, 128), 0)
    lane_id = lax.broadcasted_iota(jnp.int32, (128, 128), 1)
    earlier = jnp.where((row_id < queries) & (row_id < lane_id), 1.0, 0.0).astype(jnp.bfloat16)
    prior = jnp.dot(hit.astype(jnp.bfloat16), earlier, preferred_element_type=jnp.float32)
    inside = jnp.where(lane < queries, hit, 0.0)
    code = lane.astype(jnp.float32) * 32.0 + slot
    packed = jnp.where(lane == CAP, jnp.sum(inside, axis=1, keepdims=True), 0.0)
    for rank in range(CAP):
        chosen = jnp.where((inside > 0.5) & (prior == float(rank)), code, 0.0)
        packed = packed + jnp.where(lane == rank, jnp.sum(chosen, axis=1, keepdims=True), 0.0)
    flat = jnp.transpose(packed)[:8].astype(jnp.int32)
    u = lax.broadcasted_iota(jnp.int32, (8, 128), 1)
    line = lax.broadcasted_iota(jnp.int32, (8, 128), 0)
    half = u >> 6
    at = (u >> 2) & 15
    kx = u & 3
    first, second = at & 3, at >> 2
    turned = first * 4 + second
    own_at = jnp.where(half == 0, at, turned)
    other_at = jnp.where(half == 0, turned, at)
    core = my_core ^ half
    dy = jnp.where(core == 0, first, second)
    dz = jnp.where(core == 0, second, first)
    source = (((((my_x - kx) & 3) * 2 + core) * 4) + ((my_y - dy) & 3)) * 4 + ((my_z - dz) & 3)
    table[...] = jnp.where(
        line == 5,
        own_at * per,
        jnp.where(line == 6, other_at * per, jnp.where(line == 7, source * CAP, flat)),
    )
    copy = pltpu.make_async_copy(table, rows_ref, sem)
    copy.start()
    copy.wait()

    def gather_list(step, start):
        for i in range(4):
            src = step * 4 + i
            for rank in range(CAP):
                work[start + rank] = rows_ref[rank, src] + (src << 10) + (rank << 17)
            start = start + rows_ref[CAP, src]
        return start

    total = lax.fori_loop(0, 2 * sources // 4, gather_list, 0)
    for i in range(UNROLL):
        work[total + i] = CAP << 17
    spots = lax.broadcasted_iota(jnp.int32, (32, 128), 1)
    buffer = out_ref

    def one(n):
        item = work[n]
        place = item & 31
        query = (item >> 5) & 31
        src = (item >> 10) & 127
        rank = item >> 17
        token = jnp.concatenate(
            [own_ref[rows_ref[5, src] + query], other_ref[rows_ref[6, src] + query]], axis=0
        )
        inner = lax.dot_general(
            token, held_ref[place], (((1,), (1,)), ((), ())), preferred_element_type=jnp.float32
        )
        kept = jnp.where(spots < lengths_ref[place], inner, -1e30)
        best = jnp.max(kept, axis=1, keepdims=True)
        value = jnp.sum(best, axis=0, keepdims=True) * (1.0 / 32.0)
        dest = jnp.where(rank == CAP, DEVICES * CAP, rows_ref[7, src] + rank)
        return dest, value

    def steps(step, carry):
        done = [one(step * UNROLL + i) for i in range(UNROLL)]
        for dest, value in done:
            buffer[pl.ds(dest, 1), :] = jnp.broadcast_to(value, (1, 128))
        return carry

    lax.fori_loop(0, (total + UNROLL - 1) // UNROLL, steps, 0)


def maxsim(where, lengths, own, other, held):
    rows = DEVICES * CAP + 8
    return pl.pallas_call(
        maxsim_kernel,
        out_shape=jax.ShapeDtypeStruct((rows, 128), jnp.float32),
        in_specs=[pl.BlockSpec(memory_space=SMEM)] * 2 + [pl.BlockSpec(memory_space=VMEM)] * 3,
        out_specs=pl.BlockSpec(memory_space=VMEM),
        scratch_shapes=[
            VMEM((DEVICES * 4, 128), jnp.float32),
            VMEM((8, 128), jnp.int32),
            SMEM((8, 128), jnp.int32),
            SMEM((DEVICES * CAP + 16,), jnp.int32),
            pltpu.SemaphoreType.DMA,
        ],
        compiler_params=pltpu.CompilerParams(vmem_limit_bytes=32 << 20),
        cost_estimate=pl.CostEstimate(flops=12000000, bytes_accessed=20000000, transcendentals=0),
        name="maxsim",
    )(where, lengths, own, other, held)


def final_kernel(owner_ref, back_ref, out_ref):
    queries, per = owner_ref.shape
    lane = lax.broadcasted_iota(jnp.int32, (queries, 128), 1)
    named = [lane == owner_ref[:, c : c + 1] for c in range(per)]
    match = jnp.zeros((queries, 128), jnp.float32)
    for mine in named:
        match += jnp.where(mine, 1.0, 0.0)
    row = lax.broadcasted_iota(jnp.int32, (queries, queries), 0)
    col = lax.broadcasted_iota(jnp.int32, (queries, queries), 1)
    prior = jnp.dot(
        jnp.where(col < row, 1.0, 0.0).astype(jnp.bfloat16),
        match.astype(jnp.bfloat16),
        preferred_element_type=jnp.float32,
    )
    back = jnp.transpose(back_ref[...])
    chosen = jnp.zeros((queries, 128), jnp.float32)
    for rank in range(CAP):
        chosen = jnp.where(prior == float(rank), back[rank : rank + 1, :], chosen)
    spot = lax.broadcasted_iota(jnp.int32, (queries, per), 1)
    out = jnp.zeros((queries, per), jnp.float32)
    for c in range(per):
        value = jnp.sum(jnp.where(named[c], chosen, 0.0), axis=1, keepdims=True)
        out = jnp.where(spot == c, value, out)
    out_ref[...] = out


def final(owners, back):
    return pl.pallas_call(
        final_kernel,
        out_shape=jax.ShapeDtypeStruct(owners.shape, jnp.float32),
        in_specs=[pl.BlockSpec(memory_space=VMEM)] * 2,
        out_specs=pl.BlockSpec(memory_space=VMEM),
        name="final",
    )(owners, back)


def relevance_of(tokens, centroids):
    token_count, query_rows, width = tokens.shape
    inner = lax.dot_general(
        tokens.reshape(token_count * query_rows, width),
        centroids,
        (((1,), (1,)), ((), ())),
        preferred_element_type=jnp.float32,
    )
    return jnp.max(inner.reshape(token_count, query_rows, -1), axis=0)


def per_device(queries, centroids, codes, scales, centroid_ids, lengths, owners, slots):
    query_rows = queries.shape[0]
    owner, slot = owners[0], slots[0]
    meta = jnp.concatenate([owner.T.reshape(2, 128), slot.T.reshape(2, 128)], axis=0)
    first = jnp.concatenate([queries, meta.astype(jnp.bfloat16)[None]], axis=0)
    by_x = jnp.stack([first] + [moved(first, along_x(k)) for k in range(1, SIDE)], axis=1)
    by_x = by_x.reshape(query_rows + 1, SIDE * 4, 128)
    second = jnp.stack([by_x] + [moved(by_x, along_first(k)) for k in range(1, SIDE)], axis=0)
    pieces = [second] + [moved(second, along_second(k)) for k in range(1, SIDE)]
    peers = [moved(piece, other_core) for piece in pieces]
    own = jnp.concatenate(pieces, axis=0).reshape(-1, SIDE * 4, 128)
    other = jnp.concatenate(peers, axis=0).reshape(-1, SIDE * 4, 128)

    lists, score = lax.axis_index("lists"), lax.axis_index("score")
    where = jnp.stack(
        [lists * 16 + score, lists // 2, lists % 2, score // SIDE, score % SIDE]
    ).astype(jnp.int32)
    held = rebuild(codes, scales, centroid_ids, centroids)
    totals = maxsim(where, lengths, own, other, held)
    outgoing = totals[: DEVICES * CAP, 0].reshape(DEVICES, 1, CAP)
    back = lax.all_to_all(outgoing, AXES, split_axis=0, concat_axis=0, tiled=True)
    back = jnp.pad(back.reshape(DEVICES, CAP), ((0, 0), (0, 128 - CAP)))
    scores = final(owner, back)
    tokens = jnp.concatenate([by_x[:query_rows], peers[0][0, :query_rows]], axis=1)
    relevance = relevance_of(jnp.swapaxes(tokens, 0, 1), centroids)
    return (scores[None], relevance)


def solution(mesh):
    placed = (
        P("score", "lists", None),
        P("lists", None),
        P(("lists", "score"), None, None),
        P(("lists", "score"), None),
        P(("lists", "score"), None),
        P(("lists", "score")),
        P("lists", "score", None),
        P("lists", "score", None),
    )
    return jax.shard_map(
        per_device,
        mesh=mesh,
        in_specs=placed,
        out_specs=(P("lists", "score", None), P("score", "lists")),
        check_vma=False,
    )
```

time: 129 us -> 93 us (0.72)
  local copies, waits for them, and re-layouts: 39.2 us -> 8.71 us
  matrix products: 28.6 us -> 5.76 us
  Pallas kernels: 0 us -> 21.3 us
  waiting for transfers between devices: 24.1 us -> 10.9 us
  starting transfers between devices: 30.3 us -> 42.7 us
  other arithmetic: 5.49 us -> 2.72 us
    ppermute x0 -> x13, starting transfers between devices: none -> 28.3 us  [moved(): return lax.ppermute(value, AXES, pairs)]
    dot_general x6 -> x1, matrix products: 28.6 us -> 5.76 us  [relevance_of(): lax.dot_general(tokens.reshape(token_count * query_rows, width), centroid...]
    pallas_call x0 -> x3, Pallas kernels: none -> 21.3 us  [the longest x1 14.2 us: maxsim(): pl.pallas_call(maxsim_kernel, out_shape=jax.ShapeDtypeStruct((rows, 128),...]
    all_to_all x4 -> x1, waiting for transfers between devices: 24.1 us -> 3.79 us  [per_device(): lax.all_to_all(outgoing, AXES, split_axis=0, concat_axis=0, tiled=True)]
    gather x2 -> x0, local copies, waits for them, and re-layouts: 17 us -> none  [the longest x1 15 us: rebuild_held(): jnp.take(centroids, centroid_ids.reshape(-1), axis=0).astype(jnp.float32)]
    all_to_all x4 -> x1, starting transfers between devices: 30.3 us -> 14.4 us  [per_device(): lax.all_to_all(outgoing, AXES, split_axis=0, concat_axis=0, tiled=True)]
    unnamed x20 -> x23, local copies, waits for them, and re-layouts: 16 us -> 6.66 us
    ppermute x0 -> x13, waiting for transfers between devices: none -> 7.11 us  [moved(): return lax.ppermute(value, AXES, pairs)]
  transfers between devices with their start and end apart: 4 -> 14, of which waited for: 4 -> 6; matrix products, arithmetic and copies ran while one was open for 41% -> 8% of each run, Pallas kernels for 0% -> 6%
where the time goes in v1:
time: 93 us
  starting transfers between devices  42.7 us (46%)
  Pallas kernels  21.3 us (23%)
  waiting for transfers between devices  10.9 us (12%)
  local copies, waits for them, and re-layouts  8.71 us (9%)
  matrix products  5.76 us (6%)
  other arithmetic  2.72 us (3%)
    ppermute x13, starting transfers between devices, moved(): return lax.ppermute(value, AXES, pairs)  28.3 us
    all_to_all x1, starting transfers between devices, per_device(): lax.all_to_all(outgoing, AXES, split_axis=0, concat_axis=0, tiled=True)  14.4 us
    pallas_call x1, Pallas kernels, maxsim(): pl.pallas_call(maxsim_kernel, out_shape=jax.ShapeDtypeStruct((rows, 128),...  14.2 us
    ppermute x13, waiting for transfers between devices, moved(): return lax.ppermute(value, AXES, pairs)  7.11 us
    unnamed x23, local copies, waits for them, and re-layouts  6.66 us
    dot_general x1, matrix products, relevance_of(): lax.dot_general(tokens.reshape(token_count * query_rows, width), centroid...  5.76 us
    pallas_call x1, Pallas kernels, rebuild(): pl.pallas_call(rebuild_kernel, grid=(held,), out_shape=jax.ShapeDtypeStru...  5.28 us
    all_to_all x1, waiting for transfers between devices, per_device(): lax.all_to_all(outgoing, AXES, split_axis=0, concat_axis=0, tiled=True)  3.79 us
  transfers between devices with their start and end apart: 14, of which 6 were waited for; matrix products, arithmetic and copies ran while one was open for 8% of the time, Pallas kernels for 6%

profile of v1, /device:TPU:1, one launch (start us, length us, event | category | flops | bytes accessed | tf_op | source)
XLA Modules:
  0.0 93.0 jit_solution(2439044616813431814)
XLA Ops:
  0.6 0.8 copy.25
  1.4 0.0 copy-start.6
  1.4 0.1 copy.26
  1.5 0.1 concatenate.28
  1.6 0.7 convert_bitcast_fusion.1
  2.3 0.1 concatenate.29
  2.4 0.8 maximum_maximum_fusion
  3.1 2.1 %collective-permute-start = (bf16[33,4,128]{2,1,0:T(4,128)(2,1)S(1)}, bf16[33,4,128]{2,1,0:T(4,128)(2,1)S(1)}, u32[]{:S(2)}, u32[]{:S(2)}) collective-permute-start(bf16[33,4,128]{2,1,0:T(4,128)(2,1)S(1)} %maximum_maximum_fusion), channel_id=1, source_target_pairs={{0,32},{1,33},{2,34},{3,35},{4,36},{5,37},{6,38},{7,39},{8,40},{9,... | collective-permute-start | bytes 101384 | tf_op jit(solution)/shard_map/ppermute | solution.py:29
  5.2 2.5 %collective-permute-start.1 = (bf16[33,4,128]{2,1,0:T(4,128)(2,1)S(1)}, bf16[33,4,128]{2,1,0:T(4,128)(2,1)S(1)}, u32[]{:S(2)}, u32[]{:S(2)}) collective-permute-start(bf16[33,4,128]{2,1,0:T(4,128)(2,1)S(1)} %maximum_maximum_fusion), channel_id=1, source_target_pairs={{0,64},{1,65},{2,66},{3,67},{4,68},{5,69},{6,70},{7,71},{8,72},{9,... | collective-permute-start | bytes 101384 | tf_op jit(solution)/shard_map/ppermute | solution.py:29
  7.7 1.2 %collective-permute-start.2 = (bf16[33,4,128]{2,1,0:T(4,128)(2,1)S(1)}, bf16[33,4,128]{2,1,0:T(4,128)(2,1)S(1)}, u32[]{:S(2)}, u32[]{:S(2)}) collective-permute-start(bf16[33,4,128]{2,1,0:T(4,128)(2,1)S(1)} %maximum_maximum_fusion), channel_id=1, source_target_pairs={{0,96},{1,97},{2,98},{3,99},{4,100},{5,101},{6,102},{7,103},{8,104... | collective-permute-start | bytes 101384 | tf_op jit(solution)/shard_map/ppermute | solution.py:29
  8.8 0.8 fusion.4
  9.6 0.0 collective-permute-done
  9.6 0.0 collective-permute-done.1
  9.6 1.1 %collective-permute-done.2 = bf16[33,4,128]{2,1,0:T(4,128)(2,1)S(1)} collective-permute-done((bf16[33,4,128]{2,1,0:T(4,128)(2,1)S(1)}, bf16[33,4,128]{2,1,0:T(4,128)(2,1)S(1)}, u32[]{:S(2)}, u32[]{:S(2)}) %collective-permute-start.2) | collective-permute-done | bytes 33824 | tf_op jit(solution)/shard_map/ppermute | solution.py:29
  10.8 0.1 pad_maximum_fusion.2
  10.9 1.7 %collective-permute-start.3 = (bf16[33,16,128]{2,1,0:T(8,128)(2,1)S(1)}, bf16[33,16,128]{2,1,0:T(8,128)(2,1)S(1)}, u32[]{:S(2)}, u32[]{:S(2)}) collective-permute-start(bf16[33,16,128]{2,1,0:T(8,128)(2,1)S(1)} %bitcast.45), channel_id=1, source_target_pairs={{0,4},{1,5},{2,6},{3,7},{4,8},{5,9},{6,10},{7,11},{8,12},{9,13},{1... | collective-permute-start | bytes 405512 | tf_op jit(solution)/shard_map/ppermute | solution.py:29
  12.7 3.3 %collective-permute-start.4 = (bf16[33,16,128]{2,1,0:T(8,128)(2,1)S(1)}, bf16[33,16,128]{2,1,0:T(8,128)(2,1)S(1)}, u32[]{:S(2)}, u32[]{:S(2)}) collective-permute-start(bf16[33,16,128]{2,1,0:T(8,128)(2,1)S(1)} %bitcast.46), channel_id=1, source_target_pairs={{0,8},{1,9},{2,10},{3,11},{4,12},{5,13},{6,14},{7,15},{8,0},{9,1},... | collective-permute-start | bytes 405512 | tf_op jit(solution)/shard_map/ppermute | solution.py:29
  16.0 0.7 collective-permute-start.5
  16.7 0.1 stack.50.where_ref
  16.8 0.0 copy-start
  16.8 1.6 %copy-done = bf16[8192,128]{1,0:T(8,128)(2,1)S(1)} copy-done((bf16[8192,128]{1,0:T(8,128)(2,1)S(1)}, bf16[8192,128]{1,0:T(8,128)(2,1)}, u32[]{:S(2)}) %copy-start) | copy-done | bytes 2097176
  18.4 0.0 copy-start.2
  18.4 1.2 %copy-done.2 = bf16[32,128,128]{2,1,0:T(8,128)(2,1)S(1)} copy-done((bf16[32,128,128]{2,1,0:T(8,128)(2,1)S(1)}, bf16[32,128,128]{2,1,0:T(8,128)(2,1)}, u32[]{:S(2)}) %copy-start.2) | copy-done | bytes 1048600
  19.6 0.0 copy-start.3
  19.6 0.7 copy-done.3
  20.3 0.0 copy-start.4
  20.3 0.7 copy-done.4
  21.0 5.3 %rebuild.1.held_ref = bf16[32,128,128]{2,1,0:T(8,128)(2,1)S(1)} custom-call(s32[32,128]{1,0:T(8,128)S(1)} %copy-done.3, bf16[8192,128]{1,0:T(8,128)(2,1)S(1)} %copy-done, f32[32,1,128]{2,1,0:T(1,128)S(1)} %bitcast.44, bf16[32,128,128]{2,1,0:T(8,128)(2,1)S(1)} %copy-done.2), custom_call_target="tpu_custom_call" | custom-call | flops 12000000 | bytes 20000000 | tf_op jit(solution)/shard_map/rebuild/pallas_call | solution.py:64
  26.3 0.0 copy-done.6
  26.4 0.0 collective-permute-done.3
  26.4 0.0 collective-permute-done.4
  26.4 0.0 collective-permute-done.5
  26.4 0.1 pad_maximum_fusion.1
  26.5 1.4 %collective-permute-start.6 = (bf16[4,33,16,128]{3,2,1,0:T(8,128)(2,1)S(1)}, bf16[4,33,16,128]{3,2,1,0:T(8,128)(2,1)S(1)}, u32[]{:S(2)}, u32[]{:S(2)}) collective-permute-start(bf16[4,33,16,128]{3,2,1,0:T(8,128)(2,1)S(1)} %pad_maximum_fusion.1), channel_id=1, source_target_pairs={{0,1},{1,2},{2,3},{3,0},{4,5},{5,6},{6,7},{7,4},{8,9},{9,10},{10,1... | collective-permute-start | bytes 1622024 | tf_op jit(solution)/shard_map/ppermute | solution.py:29
  27.9 2.6 %collective-permute-start.7 = (bf16[4,33,16,128]{3,2,1,0:T(8,128)(2,1)S(1)}, bf16[4,33,16,128]{3,2,1,0:T(8,128)(2,1)S(1)}, u32[]{:S(2)}, u32[]{:S(2)}) collective-permute-start(bf16[4,33,16,128]{3,2,1,0:T(8,128)(2,1)S(1)} %pad_maximum_fusion.1), channel_id=1, source_target_pairs={{0,2},{1,3},{2,0},{3,1},{4,6},{5,7},{6,4},{7,5},{8,10},{9,11},{10,... | collective-permute-start | bytes 1622024 | tf_op jit(solution)/shard_map/ppermute | solution.py:29
  30.5 1.1 %collective-permute-start.8 = (bf16[4,33,16,128]{3,2,1,0:T(8,128)(2,1)S(1)}, bf16[4,33,16,128]{3,2,1,0:T(8,128)(2,1)S(1)}, u32[]{:S(2)}, u32[]{:S(2)}) collective-permute-start(bf16[4,33,16,128]{3,2,1,0:T(8,128)(2,1)S(1)} %pad_maximum_fusion.1), channel_id=1, source_target_pairs={{0,3},{1,0},{2,1},{3,2},{4,7},{5,4},{6,5},{7,6},{8,11},{9,8},{10,9... | collective-permute-start | bytes 1622024 | tf_op jit(solution)/shard_map/ppermute | solution.py:29
  31.6 3.9 %collective-permute-start.9 = (bf16[4,33,16,128]{3,2,1,0:T(8,128)(2,1)S(1)}, bf16[4,33,16,128]{3,2,1,0:T(8,128)(2,1)S(1)}, u32[]{:S(2)}, u32[]{:S(2)}) collective-permute-start(bf16[4,33,16,128]{3,2,1,0:T(8,128)(2,1)S(1)} %pad_maximum_fusion.1), channel_id=1, source_target_pairs={{0,16},{1,17},{2,18},{3,19},{4,20},{5,21},{6,22},{7,23},{8,24},{9,... | collective-permute-start | bytes 1622024 | tf_op jit(solution)/shard_map/ppermute | solution.py:29
  35.5 0.9 collective-permute-done.6
  36.4 3.8 %collective-permute-start.10 = (bf16[4,33,16,128]{3,2,1,0:T(8,128)(2,1)S(1)}, bf16[4,33,16,128]{3,2,1,0:T(8,128)(2,1)S(1)}, u32[]{:S(2)}, u32[]{:S(2)}) collective-permute-start(bf16[4,33,16,128]{3,2,1,0:T(8,128)(2,1)S(1)} %collective-permute-done.6), channel_id=1, source_target_pairs={{0,16},{1,17},{2,18},{3,19},{4,20},{5,21},{6,22},{7,23},{8,24},{9,... | collective-permute-start | bytes 1622024 | tf_op jit(solution)/shard_map/ppermute | solution.py:29
  40.2 3.1 %collective-permute-done.7 = bf16[4,33,16,128]{3,2,1,0:T(8,128)(2,1)S(1)} collective-permute-done((bf16[4,33,16,128]{3,2,1,0:T(8,128)(2,1)S(1)}, bf16[4,33,16,128]{3,2,1,0:T(8,128)(2,1)S(1)}, u32[]{:S(2)}, u32[]{:S(2)}) %collective-permute-start.7) | collective-permute-done | bytes 540704 | tf_op jit(solution)/shard_map/ppermute | solution.py:29
  43.3 4.1 %collective-permute-start.11 = (bf16[4,33,16,128]{3,2,1,0:T(8,128)(2,1)S(1)}, bf16[4,33,16,128]{3,2,1,0:T(8,128)(2,1)S(1)}, u32[]{:S(2)}, u32[]{:S(2)}) collective-permute-start(bf16[4,33,16,128]{3,2,1,0:T(8,128)(2,1)S(1)} %collective-permute-done.7), channel_id=1, source_target_pairs={{0,16},{1,17},{2,18},{3,19},{4,20},{5,21},{6,22},{7,23},{8,24},{9,... | collective-permute-start | bytes 1622024 | tf_op jit(solution)/shard_map/ppermute | solution.py:29
  47.5 0.0 collective-permute-done.8
  47.5 0.0 collective-permute-start.12
  47.5 0.0 collective-permute-done.9
  47.6 0.1 constant_dynamic-update-slice_fusion.2
  47.6 0.1 constant_dynamic-update-slice_fusion.1
  47.7 0.1 constant_dynamic-update-slice_fusion
  47.8 0.0 copy-start.5
  47.8 0.0 collective-permute-done.10
  47.8 1.2 %collective-permute-done.11 = bf16[4,33,16,128]{3,2,1,0:T(8,128)(2,1)S(1)} collective-permute-done((bf16[4,33,16,128]{3,2,1,0:T(8,128)(2,1)S(1)}, bf16[4,33,16,128]{3,2,1,0:T(8,128)(2,1)S(1)}, u32[]{:S(2)}, u32[]{:S(2)}) %collective-permute-start.11) | collective-permute-done | bytes 540704 | tf_op jit(solution)/shard_map/ppermute | solution.py:29
  49.0 0.8 collective-permute-done.12
  49.8 0.3 pad_maximum_fusion
  50.1 0.0 copy-done.5
  50.1 0.0 copy-start.1
  50.1 14.2 %maxsim.1 = f32[520,128]{1,0:T(8,128)S(1)} custom-call(s32[5]{0:T(128)S(1)} %stack.50.where_ref, s32[32]{0:T(128)S(1)} %copy-done.5, bf16[528,16,128]{2,1,0:T(8,128)(2,1)S(1)} %bitcast.43, bf16[528,16,128]{2,1,0:T(8,128)(2,1)S(1)} %bitcast.42, bf16[32,128,128]{2,1,0:T(8,128)(2,1)S(1)} %rebuild.1.held_ref), custom_call_target="tpu_custom_call" | custom-call | flops 12000000 | bytes 20000000 | tf_op jit(solution)/shard_map/maxsim/pallas_call | solution.py:186
  64.3 0.1 slice_reduce_fusion
  64.4 0.7 reshape_squeeze.3
  65.2 14.4 %all-to-all-start = ((f32[128,1,4]{2,1,0:T(1,128)}), f32[128,1,4]{2,1,0:T(1,128)S(1)}, u32[]{:S(2)}, u32[]{:S(2)}) async-start(f32[128,1,4]{2,1,0:T(1,128)} %bitcast.21), calls=%async_computation | async-start | bytes 131072 | tf_op jit(solution)/shard_map/all_to_all | solution.py:271
  79.5 0.0 copy-done.1
  79.6 5.8 %convolution_reduce_fusion = f32[32,8192]{1,0:T(8,128)} fusion(bf16[8192,128]{1,0:T(8,128)(2,1)S(1)} %copy-done.1, bf16[32,16,128]{2,0,1:T(8,128)(2,1)S(1)} %bitcast.56, bf16[32,16,128]{2,0,1:T(8,128)(2,1)S(1)} %bitcast.55), kind=kOutput, calls=%fused_computation | convolution fusion | flops 2155741184 | bytes 3407872 | tf_op jit(solution)/shard_map/dot_general | solution.py:242
  85.3 3.8 %all-to-all-done = f32[128,1,4]{2,1,0:T(1,128)S(1)} async-done(((f32[128,1,4]{2,1,0:T(1,128)}), f32[128,1,4]{2,1,0:T(1,128)S(1)}, u32[]{:S(2)}, u32[]{:S(2)}) %all-to-all-start) | async-done | bytes 2080 | tf_op jit(solution)/shard_map/all_to_all | solution.py:271
  89.1 0.6 pad.4.back_ref
  89.7 1.8 %final.1 = f32[32,8]{1,0:T(8,128)} custom-call(s32[32,8]{1,0:T(8,128)} %bitcast.54, f32[128,128]{1,0:T(8,128)} %pad.4.back_ref), custom_call_target="tpu_custom_call" | custom-call | tf_op jit(solution)/shard_map/final/pallas_call | solution.py:231
  91.6 1.4 %copy.32 = f32[1,32,8]{1,2,0:T(8,128)} copy(f32[1,32,8]{2,1,0:T(8,128)} %bitcast.57) | data formatting | bytes 2048
  (10 shorter events, 0.2 us)
Async XLA Ops:
  1.4 24.9 %copy-start.6 = (s32[1,32,8]{2,1,0:T(8,128)}, s32[1,32,8]{2,1,0:T(8,128)S(1)}, u32[]{:S(2)}) copy-start(s32[1,32,8]{2,1,0:T(8,128)S(1)} %copy.25) | copy-start | bytes 3076
  3.1 6.5 %collective-permute-start = (bf16[33,4,128]{2,1,0:T(4,128)(2,1)S(1)}, bf16[33,4,128]{2,1,0:T(4,128)(2,1)S(1)}, u32[]{:S(2)}, u32[]{:S(2)}) collective-permute-start(bf16[33,4,128]{2,1,0:T(4,128)(2,1)S(1)} %maximum_maximum_fusion), channel_id=1, source_target_pairs={{0,32},{1,33},{2,34},{3,35},{4,36},{5,37},{6,38},{7,39},{8,40},{9,... | collective-permute-start | bytes 101384 | tf_op jit(solution)/shard_map/ppermute | solution.py:29
  5.2 4.4 %collective-permute-start.1 = (bf16[33,4,128]{2,1,0:T(4,128)(2,1)S(1)}, bf16[33,4,128]{2,1,0:T(4,128)(2,1)S(1)}, u32[]{:S(2)}, u32[]{:S(2)}) collective-permute-start(bf16[33,4,128]{2,1,0:T(4,128)(2,1)S(1)} %maximum_maximum_fusion), channel_id=1, source_target_pairs={{0,64},{1,65},{2,66},{3,67},{4,68},{5,69},{6,70},{7,71},{8,72},{9,... | collective-permute-start | bytes 101384 | tf_op jit(solution)/shard_map/ppermute | solution.py:29
  7.7 3.1 %collective-permute-start.2 = (bf16[33,4,128]{2,1,0:T(4,128)(2,1)S(1)}, bf16[33,4,128]{2,1,0:T(4,128)(2,1)S(1)}, u32[]{:S(2)}, u32[]{:S(2)}) collective-permute-start(bf16[33,4,128]{2,1,0:T(4,128)(2,1)S(1)} %maximum_maximum_fusion), channel_id=1, source_target_pairs={{0,96},{1,97},{2,98},{3,99},{4,100},{5,101},{6,102},{7,103},{8,104... | collective-permute-start | bytes 101384 | tf_op jit(solution)/shard_map/ppermute | solution.py:29
  10.9 15.5 %collective-permute-start.3 = (bf16[33,16,128]{2,1,0:T(8,128)(2,1)S(1)}, bf16[33,16,128]{2,1,0:T(8,128)(2,1)S(1)}, u32[]{:S(2)}, u32[]{:S(2)}) collective-permute-start(bf16[33,16,128]{2,1,0:T(8,128)(2,1)S(1)} %bitcast.45), channel_id=1, source_target_pairs={{0,4},{1,5},{2,6},{3,7},{4,8},{5,9},{6,10},{7,11},{8,12},{9,13},{1... | collective-permute-start | bytes 405512 | tf_op jit(solution)/shard_map/ppermute | solution.py:29
  12.7 13.8 %collective-permute-start.4 = (bf16[33,16,128]{2,1,0:T(8,128)(2,1)S(1)}, bf16[33,16,128]{2,1,0:T(8,128)(2,1)S(1)}, u32[]{:S(2)}, u32[]{:S(2)}) collective-permute-start(bf16[33,16,128]{2,1,0:T(8,128)(2,1)S(1)} %bitcast.46), channel_id=1, source_target_pairs={{0,8},{1,9},{2,10},{3,11},{4,12},{5,13},{6,14},{7,15},{8,0},{9,1},... | collective-permute-start | bytes 405512 | tf_op jit(solution)/shard_map/ppermute | solution.py:29
  16.0 10.5 %collective-permute-start.5 = (bf16[33,16,128]{2,1,0:T(8,128)(2,1)S(1)}, bf16[33,16,128]{2,1,0:T(8,128)(2,1)S(1)}, u32[]{:S(2)}, u32[]{:S(2)}) collective-permute-start(bf16[33,16,128]{2,1,0:T(8,128)(2,1)S(1)} %bitcast.47), channel_id=1, source_target_pairs={{0,12},{1,13},{2,14},{3,15},{4,0},{5,1},{6,2},{7,3},{8,4},{9,5},{1... | collective-permute-start | bytes 405512 | tf_op jit(solution)/shard_map/ppermute | solution.py:29
  16.8 1.6 %copy-start = (bf16[8192,128]{1,0:T(8,128)(2,1)S(1)}, bf16[8192,128]{1,0:T(8,128)(2,1)}, u32[]{:S(2)}) copy-start(bf16[8192,128]{1,0:T(8,128)(2,1)} %cent_ref.1) | copy-start | bytes 6291460
  18.4 1.2 %copy-start.2 = (bf16[32,128,128]{2,1,0:T(8,128)(2,1)S(1)}, bf16[32,128,128]{2,1,0:T(8,128)(2,1)}, u32[]{:S(2)}) copy-start(bf16[32,128,128]{2,1,0:T(8,128)(2,1)} %code_ref.1) | copy-start | bytes 3145732
  19.6 0.7 copy-start.3
  20.3 0.7 copy-start.4
  26.5 9.8 %collective-permute-start.6 = (bf16[4,33,16,128]{3,2,1,0:T(8,128)(2,1)S(1)}, bf16[4,33,16,128]{3,2,1,0:T(8,128)(2,1)S(1)}, u32[]{:S(2)}, u32[]{:S(2)}) collective-permute-start(bf16[4,33,16,128]{3,2,1,0:T(8,128)(2,1)S(1)} %pad_maximum_fusion.1), channel_id=1, source_target_pairs={{0,1},{1,2},{2,3},{3,0},{4,5},{5,6},{6,7},{7,4},{8,9},{9,10},{10,1... | collective-permute-start | bytes 1622024 | tf_op jit(solution)/shard_map/ppermute | solution.py:29
  27.9 15.4 %collective-permute-start.7 = (bf16[4,33,16,128]{3,2,1,0:T(8,128)(2,1)S(1)}, bf16[4,33,16,128]{3,2,1,0:T(8,128)(2,1)S(1)}, u32[]{:S(2)}, u32[]{:S(2)}) collective-permute-start(bf16[4,33,16,128]{3,2,1,0:T(8,128)(2,1)S(1)} %pad_maximum_fusion.1), channel_id=1, source_target_pairs={{0,2},{1,3},{2,0},{3,1},{4,6},{5,7},{6,4},{7,5},{8,10},{9,11},{10,... | collective-permute-start | bytes 1622024 | tf_op jit(solution)/shard_map/ppermute | solution.py:29
  30.5 17.0 %collective-permute-start.8 = (bf16[4,33,16,128]{3,2,1,0:T(8,128)(2,1)S(1)}, bf16[4,33,16,128]{3,2,1,0:T(8,128)(2,1)S(1)}, u32[]{:S(2)}, u32[]{:S(2)}) collective-permute-start(bf16[4,33,16,128]{3,2,1,0:T(8,128)(2,1)S(1)} %pad_maximum_fusion.1), channel_id=1, source_target_pairs={{0,3},{1,0},{2,1},{3,2},{4,7},{5,4},{6,5},{7,6},{8,11},{9,8},{10,9... | collective-permute-start | bytes 1622024 | tf_op jit(solution)/shard_map/ppermute | solution.py:29
  31.6 15.9 %collective-permute-start.9 = (bf16[4,33,16,128]{3,2,1,0:T(8,128)(2,1)S(1)}, bf16[4,33,16,128]{3,2,1,0:T(8,128)(2,1)S(1)}, u32[]{:S(2)}, u32[]{:S(2)}) collective-permute-start(bf16[4,33,16,128]{3,2,1,0:T(8,128)(2,1)S(1)} %pad_maximum_fusion.1), channel_id=1, source_target_pairs={{0,16},{1,17},{2,18},{3,19},{4,20},{5,21},{6,22},{7,23},{8,24},{9,... | collective-permute-start | bytes 1622024 | tf_op jit(solution)/shard_map/ppermute | solution.py:29
  36.4 11.5 %collective-permute-start.10 = (bf16[4,33,16,128]{3,2,1,0:T(8,128)(2,1)S(1)}, bf16[4,33,16,128]{3,2,1,0:T(8,128)(2,1)S(1)}, u32[]{:S(2)}, u32[]{:S(2)}) collective-permute-start(bf16[4,33,16,128]{3,2,1,0:T(8,128)(2,1)S(1)} %collective-permute-done.6), channel_id=1, source_target_pairs={{0,16},{1,17},{2,18},{3,19},{4,20},{5,21},{6,22},{7,23},{8,24},{9,... | collective-permute-start | bytes 1622024 | tf_op jit(solution)/shard_map/ppermute | solution.py:29
  43.3 5.7 %collective-permute-start.11 = (bf16[4,33,16,128]{3,2,1,0:T(8,128)(2,1)S(1)}, bf16[4,33,16,128]{3,2,1,0:T(8,128)(2,1)S(1)}, u32[]{:S(2)}, u32[]{:S(2)}) collective-permute-start(bf16[4,33,16,128]{3,2,1,0:T(8,128)(2,1)S(1)} %collective-permute-done.7), channel_id=1, source_target_pairs={{0,16},{1,17},{2,18},{3,19},{4,20},{5,21},{6,22},{7,23},{8,24},{9,... | collective-permute-start | bytes 1622024 | tf_op jit(solution)/shard_map/ppermute | solution.py:29
  47.5 2.3 %collective-permute-start.12 = (bf16[4,33,16,128]{3,2,1,0:T(8,128)(2,1)S(1)}, bf16[4,33,16,128]{3,2,1,0:T(8,128)(2,1)S(1)}, u32[]{:S(2)}, u32[]{:S(2)}) collective-permute-start(bf16[4,33,16,128]{3,2,1,0:T(8,128)(2,1)S(1)} %collective-permute-done.8), channel_id=1, source_target_pairs={{0,16},{1,17},{2,18},{3,19},{4,20},{5,21},{6,22},{7,23},{8,24},{9,... | collective-permute-start | bytes 1622024 | tf_op jit(solution)/shard_map/ppermute | solution.py:29
  47.8 2.3 %copy-start.5 = (s32[32]{0:T(128)S(1)}, s32[32]{0:T(128)}, u32[]{:S(2)}) copy-start(s32[32]{0:T(128)} %lengths_ref.1) | copy-start | bytes 388
  50.1 29.5 %copy-start.1 = (bf16[8192,128]{1,0:T(8,128)(2,1)S(1)}, bf16[8192,128]{1,0:T(8,128)(2,1)}, u32[]{:S(2)}) copy-start(bf16[8192,128]{1,0:T(8,128)(2,1)} %cent_ref.1) | copy-start | bytes 6291460
  65.2 24.0 %all-to-all-start = ((f32[128,1,4]{2,1,0:T(1,128)}), f32[128,1,4]{2,1,0:T(1,128)S(1)}, u32[]{:S(2)}, u32[]{:S(2)}) async-start(f32[128,1,4]{2,1,0:T(1,128)} %bitcast.21), calls=%async_computation | async-start | bytes 131072 | tf_op jit(solution)/shard_map/all_to_all | solution.py:271

commit v2 on v1

v2 whole, which is shorter than its diff:
```python
import jax
import jax.numpy as jnp
from jax import lax
from jax.experimental import pallas as pl
from jax.experimental.pallas import tpu as pltpu
from jax.sharding import PartitionSpec as P

AXES = ("lists", "score")
SIDE = 4
CORES = 2
DEVICES = 128
CAP = 4
SMEM = pltpu.SMEM
VMEM = pltpu.VMEM


def device_of(x, core, y, z):
    x, y, z = x % SIDE, y % SIDE, z % SIDE
    return ((x * CORES + core) * SIDE + y) * SIDE + z


def moved(value, step):
    pairs = []
    for x in range(SIDE):
        for core in range(CORES):
            for y in range(SIDE):
                for z in range(SIDE):
                    pairs.append((device_of(x, core, y, z), device_of(*step(x, core, y, z))))
    return lax.ppermute(value, AXES, pairs)


def along_x(k):
    return lambda x, core, y, z: (x + k, core, y, z)


def along_first(k):
    return lambda x, core, y, z: (x, core, y + k, z) if core == 0 else (x, core, y, z + k)


def along_second(k):
    return lambda x, core, y, z: (x, core, y, z + k) if core == 0 else (x, core, y + k, z)


def other_core(x, core, y, z):
    return (x, 1 - core, y, z)


def rebuild_kernel(ids_ref, cent_ref, scale_ref, code_ref, _, out_ref, table, base):
    step = pl.program_id(0)

    @pl.when(step == 0)
    def _():
        table[...] = cent_ref[...].astype(jnp.float32)

    blocks, rows = code_ref.shape[:2]

    def one(b, carry):
        for p in range(rows):
            base[pl.ds(p, 1), :] = table[pl.ds(ids_ref[step * blocks + b, p], 1), :]
        scale = jnp.transpose(jnp.broadcast_to(scale_ref[b], (rows, rows)))
        value = base[...] + scale * code_ref[b].astype(jnp.float32)
        out_ref[b] = value.astype(jnp.bfloat16)
        return carry

    lax.fori_loop(0, blocks, one, 0)


def rebuild(codes, scales, centroid_ids, centroids, after):
    held, rows, width = codes.shape
    step = held // REBUILD_STEPS
    return pl.pallas_call(
        rebuild_kernel,
        grid=(REBUILD_STEPS,),
        out_shape=jax.ShapeDtypeStruct(codes.shape, jnp.bfloat16),
        in_specs=[
            pl.BlockSpec(memory_space=SMEM),
            pl.BlockSpec(centroids.shape, lambda b: (0, 0)),
            pl.BlockSpec((step, 1, rows), lambda b: (b, 0, 0)),
            pl.BlockSpec((step, rows, width), lambda b: (b, 0, 0)),
            pl.BlockSpec(memory_space=pl.ANY),
        ],
        out_specs=pl.BlockSpec((step, rows, width), lambda b: (b, 0, 0)),
        scratch_shapes=[
            VMEM(centroids.shape, jnp.float32),
            VMEM((rows, width), jnp.float32),
        ],
        compiler_params=pltpu.CompilerParams(vmem_limit_bytes=56 << 20),
        cost_estimate=pl.CostEstimate(flops=12000000, bytes_accessed=20000000, transcendentals=0),
        name="rebuild",
    )(centroid_ids, centroids, scales.reshape(held, 1, rows), codes, after)


REBUILD_STEPS = 4
CHUNK = 8
TOGETHER = 8
PLACES = 768
DUMMY_ROW = DEVICES * CAP
ALL = [(k, j, 4 * k + j) for k in range(SIDE) for j in range(SIDE)]
EARLY = [(k, j, 4 * n + j) for n, k in enumerate((0, 1, 3)) for j in (0, 1, 3)]
LATE = [(2, j, j) for j in range(4)] + [(k, 2, 4 + n) for n, k in enumerate((0, 1, 3))]


def as_bf16(mask):
    return jnp.where(mask, 1.0, 0.0).astype(jnp.bfloat16)


def product(a, b):
    return jnp.dot(a.astype(jnp.bfloat16), b, preferred_element_type=jnp.float32)


def by_row(row, values):
    result = jnp.full(row.shape, values[-1], jnp.int32)
    for i, value in enumerate(values[:-1]):
        result = jnp.where(row == i, value, result)
    return result


def request_list(rows, where_ref, own_ref, other_ref, meta):
    per = PER
    queries = per - 1
    me, my_x, my_core, my_y, my_z = (where_ref[i] for i in range(5))
    if len(rows) < 16:
        meta[...] = jnp.full(meta.shape, -1.0, jnp.float32)
    for half, ref in enumerate((own_ref, other_ref)):
        for i, (_, _, at) in enumerate(rows):
            meta[pl.ds((half * 16 + i) * 16, 16), :] = ref[at * per + queries].astype(jnp.float32)
    square = (DEVICES, 128)
    lane = lax.broadcasted_iota(jnp.int32, square, 1)
    line = lax.broadcasted_iota(jnp.int32, square, 0)
    lane_low, lane_high = lane & 31, lane >> 5
    line_low, line_high = line & 31, line >> 5
    same_low = as_bf16(line_low == lane_low)
    same_high = as_bf16(line_high == lane_high)
    parts = [meta[pl.ds(row, DEVICES, stride=4), :] for row in range(4)]
    mine = [parts[i] == me.astype(jnp.float32) for i in range(2)]
    hit = jnp.where(mine[0], 1.0, 0.0) + jnp.where(mine[1], 1.0, 0.0)
    slot = jnp.where(mine[0], parts[2], 0.0) + jnp.where(mine[1], parts[3], 0.0)
    earlier = as_bf16(line_low < lane_low)
    prior = product(hit, earlier)
    hit, slot = product(hit, same_low), product(slot, same_low)
    chosen = (hit > 0.5) & (prior == lane_high.astype(jnp.float32))
    low = lane_low.astype(jnp.float32)
    asked_query = product(jnp.where(chosen, low + 1.0, 0.0), same_high)
    asked_slot = product(jnp.where(chosen, slot, 0.0), same_high)
    wants = (asked_query > 0.5) & (asked_slot == low)
    before = product(jnp.where(lane < line, 1.0, 0.0), as_bf16(wants))
    count = jnp.sum(jnp.where(wants, 1.0, 0.0), axis=0, keepdims=True)
    count = jnp.broadcast_to(count, (8, 128))
    lower_ranks = product(count, as_bf16((line_low == lane_low) & (line_high < lane_high)))
    in_block = product(count, same_low)
    chunks = ((in_block.astype(jnp.int32) + (CHUNK - 1)) // CHUNK).astype(jnp.float32)
    first_chunk = product(chunks, as_bf16((line < 32) & (line < lane_low)))
    all_chunks = product(chunks, as_bf16(line < 32)).astype(jnp.int32)
    spot = before + lower_ranks[:1]
    spot_high = (spot.astype(jnp.int32) // CHUNK).astype(jnp.float32)
    spot_low = spot - spot_high * float(CHUNK)
    high = product(jnp.where(wants, spot_high + first_chunk[:1], 0.0), same_high)
    low_part = product(jnp.where(wants, spot_low, 0.0), same_high)
    spot = jnp.where(asked_query > 0.5, high * float(CHUNK) + low_part, -1.0).astype(jnp.int32)
    fields = [line.astype(jnp.float32), asked_query, asked_slot]
    u_row = lax.broadcasted_iota(jnp.int32, (8, 128), 1).astype(jnp.float32)
    kind = lax.broadcasted_iota(jnp.int32, (8, 128), 0)
    asked = [jnp.transpose(value) for value in fields[1:]]
    to = lax.broadcasted_iota(jnp.int32, (DEVICES, PLACES), 1)
    found = jnp.zeros((8, PLACES), jnp.float32)
    for rank in range(CAP):
        at = 32 * rank
        left = jnp.where(
            kind == 0,
            u_row,
            jnp.where(
                kind == 1,
                asked[0][at : at + 1, :],
                jnp.where(kind == 2, asked[1][at : at + 1, :], float(rank)),
            ),
        )
        found = found + product(left, as_bf16(spot[:, at : at + 1] == to))
    found = found.astype(jnp.int32)
    u, query, slot, rank = (found[i : i + 1, :] for i in range(4))
    half = u >> 6
    at = (u >> 2) & 15
    kx = u & 3
    if len(rows) == 16:
        straight, turned = at, (at & 3) * 4 + (at >> 2)
        first, second = at & 3, at >> 2
    else:
        places = {(k, j): i for k, j, i in rows}
        straight = by_row(at, [i for _, _, i in rows])
        turned = by_row(at, [places[j, k] for k, j, _ in rows])
        first, second = by_row(at, [j for _, j, _ in rows]), by_row(at, [k for k, _, _ in rows])
    own_at = jnp.where(half == 0, straight, turned) * per + query - 1
    other_at = jnp.where(half == 0, turned, straight) * per + query - 1
    core = my_core ^ half
    dy = jnp.where(core == 0, first, second)
    dz = jnp.where(core == 0, second, first)
    source = (((((my_x - kx) & 3) * 2 + core) * 4) + ((my_y - dy) & 3)) * 4 + ((my_z - dz) & 3)
    real = query > 0
    item = jnp.where(real, slot + (own_at << 5) + (other_at << 15), 0)
    goal = jnp.where(real, source + rank * DEVICES, DUMMY_ROW)
    return item, goal, all_chunks[:1]


PER = 33


def maxsim_kernel(
    rows, last, where_ref, lengths_ref, own_ref, other_ref, held_ref, best_in, out_ref, meta, table, work, best, sem
):
    if best is None:
        best = out_ref
    elif best_in is not None:
        best[...] = best_in[...]
    item, goal, all_chunks = request_list(rows, where_ref, own_ref, other_ref, meta)
    table[0:1, :] = item
    table[1:2, :] = goal
    table[2:3, 0:128] = all_chunks
    copy = pltpu.make_async_copy(table, work, sem)
    copy.start()
    copy.wait()
    total = work[2, 0]
    slots_id = lax.broadcasted_iota(jnp.int32, (128, CHUNK * 32), 0)
    group = lax.broadcasted_iota(jnp.int32, (1, 128), 1) >> 5

    def one(chunk):
        tokens = []
        for i in range(CHUNK):
            item = work[0, chunk * CHUNK + i]
            if i == 0:
                block = item & 31
            tokens.append(own_ref[(item >> 5) & 1023])
            tokens.append(other_ref[item >> 15])
        inner = lax.dot_general(
            held_ref[block],
            jnp.concatenate(tokens, axis=0),
            (((1,), (1,)), ((), ())),
            preferred_element_type=jnp.float32,
        )
        kept = jnp.where(slots_id < lengths_ref[block], inner, -1e30)
        return jnp.max(kept, axis=0, keepdims=True)

    def steps(step, carry):
        done = [one(step * TOGETHER + i) for i in range(TOGETHER)]
        for i, value in enumerate(done):
            for j in range(CHUNK):
                part = value[:, j // 4 * 128 : j // 4 * 128 + 128]
                dest = work[1, (step * TOGETHER + i) * CHUNK + j]
                best[pl.ds(dest, 1), :] = jnp.where(group == j % 4, part, 0.0)
        return carry

    lax.fori_loop(0, (total + TOGETHER - 1) // TOGETHER, steps, 0)
    if last:
        lane = lax.broadcasted_iota(jnp.int32, (DEVICES, 128), 1)
        result = jnp.zeros((DEVICES, 128), jnp.float32)
        for rank in range(CAP):
            value = jnp.sum(best[pl.ds(rank * DEVICES, DEVICES), :], axis=1, keepdims=True)
            result = jnp.where(lane == rank, value * (1.0 / 32.0), result)
        out_ref[...] = result


def maxsim(where, lengths, own, other, held, rows=ALL, last=True, best=None):
    def body(*refs):
        refs = list(refs)
        if best is None:
            refs.insert(5, None)
        if not last:
            refs.insert(-1, None)
        maxsim_kernel(rows, last, *refs)

    buffer = (DEVICES * CAP + 8, 128)
    scratch = [
        VMEM((DEVICES * 4, 128), jnp.float32),
        VMEM((8, PLACES), jnp.int32),
        SMEM((8, PLACES), jnp.int32),
    ]
    if last:
        scratch.append(VMEM(buffer, jnp.float32))
    operands = (where, lengths, own, other, held) + (() if best is None else (best,))
    return pl.pallas_call(
        body,
        out_shape=jax.ShapeDtypeStruct((DEVICES, 128) if last else buffer, jnp.float32),
        in_specs=[pl.BlockSpec(memory_space=SMEM)] * 2
        + [pl.BlockSpec(memory_space=VMEM)] * (len(operands) - 2),
        out_specs=pl.BlockSpec(memory_space=VMEM),
        scratch_shapes=scratch + [pltpu.SemaphoreType.DMA],
        compiler_params=pltpu.CompilerParams(vmem_limit_bytes=32 << 20),
        cost_estimate=pl.CostEstimate(flops=12000000, bytes_accessed=20000000, transcendentals=0),
        name="maxsim_late" if last else "maxsim_early",
    )(*operands)


def pack_kernel(query_ref, owner_ref, slot_ref, out_ref):
    queries = query_ref.shape[0]
    out_ref[:queries] = query_ref[...]
    lane = lax.broadcasted_iota(jnp.int32, (1, 128), 1) >> 5
    rows = []
    for ref in (owner_ref, slot_ref):
        wide = ref[...].astype(jnp.float32)
        wide = jnp.concatenate([wide] * 4, axis=1)
        for part in range(2):
            row = jnp.zeros((1, 128), jnp.float32)
            for i in range(4):
                c = part * 4 + i
                row = jnp.where(lane == i, wide[c : c + 1, :], row)
            rows.append(row)
    out_ref[queries] = jnp.concatenate(rows, axis=0).astype(jnp.bfloat16)


def pack(queries, owners, slots):
    rows, tokens, width = queries.shape
    return pl.pallas_call(
        pack_kernel,
        out_shape=jax.ShapeDtypeStruct((rows + 1, tokens, width), jnp.bfloat16),
        in_specs=[pl.BlockSpec(memory_space=VMEM)] * 3,
        out_specs=pl.BlockSpec(memory_space=VMEM),
        name="pack",
    )(queries, owners, slots)


def final_kernel(owner_ref, back_ref, out_ref):
    per, queries = owner_ref.shape
    lane = lax.broadcasted_iota(jnp.int32, (128, queries), 0)
    named = [lane == owner_ref[c : c + 1, :] for c in range(per)]
    match = jnp.zeros((128, queries), jnp.float32)
    for mine in named:
        match += jnp.where(mine, 1.0, 0.0)
    row = lax.broadcasted_iota(jnp.int32, (queries, queries), 0)
    col = lax.broadcasted_iota(jnp.int32, (queries, queries), 1)
    prior = jnp.dot(
        match.astype(jnp.bfloat16), as_bf16(row < col), preferred_element_type=jnp.float32
    )
    back = back_ref[...]
    chosen = jnp.zeros((128, queries), jnp.float32)
    for rank in range(CAP):
        chosen = jnp.where(prior == float(rank), back[:, rank : rank + 1], chosen)
    for c in range(per):
        out_ref[c : c + 1, :] = jnp.sum(jnp.where(named[c], chosen, 0.0), axis=0, keepdims=True)


def final(owners, back):
    return pl.pallas_call(
        final_kernel,
        out_shape=jax.ShapeDtypeStruct(owners.shape, jnp.float32),
        in_specs=[pl.BlockSpec(memory_space=VMEM)] * 2,
        out_specs=pl.BlockSpec(memory_space=VMEM),
        name="final",
    )(owners, back)


def relevance_of(tokens, centroids):
    token_count, query_rows, width = tokens.shape
    inner = lax.dot_general(
        tokens.reshape(token_count * query_rows, width),
        centroids,
        (((1,), (1,)), ((), ())),
        preferred_element_type=jnp.float32,
    )
    return jnp.max(inner.reshape(token_count, query_rows, -1), axis=0)


def per_device(queries, centroids, codes, scales, centroid_ids, lengths, owners, slots):
    query_rows = queries.shape[0]
    owner, slot = owners[0].T, slots[0].T
    first = pack(queries, owner, slot)
    by_x = jnp.stack([first] + [moved(first, along_x(k)) for k in range(1, SIDE)], axis=1)
    by_x = by_x.reshape(query_rows + 1, SIDE * 4, 128)
    second = jnp.stack([by_x] + [moved(by_x, along_first(k)) for k in range(1, SIDE)], axis=0)
    pieces = [second] + [moved(second, along_second(k)) for k in range(1, SIDE)]
    peers = [moved(piece, other_core) for piece in pieces]
    own = jnp.concatenate(pieces, axis=0).reshape(-1, SIDE * 4, 128)
    other = jnp.concatenate(peers, axis=0).reshape(-1, SIDE * 4, 128)

    lists, score = lax.axis_index("lists"), lax.axis_index("score")
    where = jnp.stack(
        [lists * 16 + score, lists // 2, lists % 2, score // SIDE, score % SIDE]
    ).astype(jnp.int32)
    held = rebuild(codes, scales, centroid_ids, centroids, second)
    totals = maxsim(where, lengths, own, other, held)
    outgoing = totals.reshape(DEVICES, 1, 128)
    back = lax.all_to_all(outgoing, AXES, split_axis=0, concat_axis=0, tiled=True)
    scores = final(owner, back.reshape(DEVICES, 128)).T
    tokens = jnp.concatenate([by_x[:query_rows], peers[0][0, :query_rows]], axis=1)
    relevance = relevance_of(jnp.swapaxes(tokens, 0, 1), centroids)
    return (scores[None], relevance)


def solution(mesh):
    placed = (
        P("score", "lists", None),
        P("lists", None),
        P(("lists", "score"), None, None),
        P(("lists", "score"), None),
        P(("lists", "score"), None),
        P(("lists", "score")),
        P("lists", "score", None),
        P("lists", "score", None),
    )
    return jax.shard_map(
        per_device,
        mesh=mesh,
        in_specs=placed,
        out_specs=(P("lists", "score", None), P("score", "lists")),
        check_vma=False,
    )
```

time: 93 us -> 70.2 us (0.75)
  starting transfers between devices: 42.7 us -> 33.6 us
  local copies, waits for them, and re-layouts: 8.71 us -> 1.18 us
  Pallas kernels: 21.3 us -> 16.4 us
  other arithmetic: 2.72 us -> 1.24 us
    all_to_all x1, starting transfers between devices: 14.4 us -> 8.16 us  [per_device(): lax.all_to_all(outgoing, AXES, split_axis=0, concat_axis=0, tiled=True)]
    unnamed x23 -> x16, local copies, waits for them, and re-layouts: 6.66 us -> 0.87 us
    pallas_call x2 -> x3, Pallas kernels: 19.5 us -> 14.7 us  [the longest x1 6.78 us: rebuild(): pl.pallas_call(rebuild_kernel, grid=(REBUILD_STEPS,), out_shape=jax.Shape...]
    ppermute x13, starting transfers between devices: 28.3 us -> 25.5 us  [moved(): return lax.ppermute(value, AXES, pairs)]
  transfers between devices with their start and end apart: 14 -> 14, of which waited for: 6 -> 8; matrix products, arithmetic and copies ran while one was open for 8% -> 9% of each run, Pallas kernels for 6% -> 10%
where the time goes in v2:
time: 70.2 us; the launch traced here: 70.4 us
  starting transfers between devices  33.6 us (48%)
  Pallas kernels  16.4 us (23%)
  waiting for transfers between devices  11.3 us (16%)
  matrix products  5.77 us (8%)
  other arithmetic  1.24 us (2%)
  local copies, waits for them, and re-layouts  1.18 us (2%)
  between operations  0.84 us (1%)
    ppermute x13, starting transfers between devices, moved(): return lax.ppermute(value, AXES, pairs)  25.5 us
    all_to_all x1, starting transfers between devices, per_device(): lax.all_to_all(outgoing, AXES, split_axis=0, concat_axis=0, tiled=True)  8.16 us
    ppermute x13, waiting for transfers between devices, moved(): return lax.ppermute(value, AXES, pairs)  7.55 us
    pallas_call x1, Pallas kernels, rebuild(): pl.pallas_call(rebuild_kernel, grid=(REBUILD_STEPS,), out_shape=jax.Shape...  6.78 us
    pallas_call x1, Pallas kernels, maxsim(): pl.pallas_call(body, out_shape=jax.ShapeDtypeStruct((DEVICES, 128) if las...  6.4 us
    dot_general x1, matrix products, relevance_of(): lax.dot_general(tokens.reshape(token_count * query_rows, width), centroid...  5.77 us
    all_to_all x1, waiting for transfers between devices, per_device(): lax.all_to_all(outgoing, AXES, split_axis=0, concat_axis=0, tiled=True)  3.78 us
    pallas_call x1, Pallas kernels, final(): pl.pallas_call(final_kernel, out_shape=jax.ShapeDtypeStruct(owners.shape,...  1.71 us
  transfers between devices with their start and end apart: 14, of which 8 were waited for; matrix products, arithmetic and copies ran while one was open for 9% of the time, Pallas kernels for 10%

profile of v2, /device:TPU:1, one launch (start us, length us, event | category | flops | bytes accessed | tf_op | source)
XLA Modules:
  0.0 70.4 jit_solution(15927552922378989698)
XLA Ops:
  0.6 1.5 %pack.1 = bf16[33,4,128]{2,1,0:T(4,128)(2,1)} custom-call(bf16[32,4,128]{2,1,0:T(4,128)(2,1)} %query_ref.1, s32[8,32]{1,0:T(8,128)} %bitcast.58, s32[8,32]{1,0:T(8,128)} %bitcast.60), custom_call_target="tpu_custom_call" | custom-call | tf_op jit(solution)/shard_map/pack/pallas_call | solution.py:310
  2.1 2.0 %collective-permute-start = (bf16[33,4,128]{2,1,0:T(4,128)(2,1)}, bf16[33,4,128]{2,1,0:T(4,128)(2,1)S(1)}, u32[]{:S(2)}, u32[]{:S(2)}) collective-permute-start(bf16[33,4,128]{2,1,0:T(4,128)(2,1)} %pack.1), channel_id=1, source_target_pairs={{0,32},{1,33},{2,34},{3,35},{4,36},{5,37},{6,38},{7,39},{8,40},{9,... | collective-permute-start | bytes 101384 | tf_op jit(solution)/shard_map/ppermute | solution.py:29
  4.1 2.5 %collective-permute-start.1 = (bf16[33,4,128]{2,1,0:T(4,128)(2,1)}, bf16[33,4,128]{2,1,0:T(4,128)(2,1)S(1)}, u32[]{:S(2)}, u32[]{:S(2)}) collective-permute-start(bf16[33,4,128]{2,1,0:T(4,128)(2,1)} %pack.1), channel_id=1, source_target_pairs={{0,64},{1,65},{2,66},{3,67},{4,68},{5,69},{6,70},{7,71},{8,72},{9,... | collective-permute-start | bytes 101384 | tf_op jit(solution)/shard_map/ppermute | solution.py:29
  6.6 1.2 %collective-permute-start.2 = (bf16[33,4,128]{2,1,0:T(4,128)(2,1)}, bf16[33,4,128]{2,1,0:T(4,128)(2,1)S(1)}, u32[]{:S(2)}, u32[]{:S(2)}) collective-permute-start(bf16[33,4,128]{2,1,0:T(4,128)(2,1)} %pack.1), channel_id=1, source_target_pairs={{0,96},{1,97},{2,98},{3,99},{4,100},{5,101},{6,102},{7,103},{8,104... | collective-permute-start | bytes 101384 | tf_op jit(solution)/shard_map/ppermute | solution.py:29
  7.8 0.0 collective-permute-done
  7.8 0.9 %collective-permute-done.1 = bf16[33,4,128]{2,1,0:T(4,128)(2,1)S(1)} collective-permute-done((bf16[33,4,128]{2,1,0:T(4,128)(2,1)}, bf16[33,4,128]{2,1,0:T(4,128)(2,1)S(1)}, u32[]{:S(2)}, u32[]{:S(2)}) %collective-permute-start.1) | collective-permute-done | bytes 33824 | tf_op jit(solution)/shard_map/ppermute | solution.py:29
  8.6 1.2 %collective-permute-done.2 = bf16[33,4,128]{2,1,0:T(4,128)(2,1)S(1)} collective-permute-done((bf16[33,4,128]{2,1,0:T(4,128)(2,1)}, bf16[33,4,128]{2,1,0:T(4,128)(2,1)S(1)}, u32[]{:S(2)}, u32[]{:S(2)}) %collective-permute-start.2) | collective-permute-done | bytes 33824 | tf_op jit(solution)/shard_map/ppermute | solution.py:29
  9.9 0.9 %pad_maximum_fusion.2 = bf16[33,4,4,128]{3,2,0,1:T(4,128)(2,1)S(1)} fusion(bf16[33,1,4,128]{3,2,0,1:T(4,128)(2,1)S(1)} %bitcast.56, bf16[33,1,4,128]{3,2,0,1:T(4,128)(2,1)S(1)} %bitcast.55, bf16[33,1,4,128]{3,2,0,1:T(4,128)(2,1)S(1)} %bitcast.54, bf16[33,1,4,128]{3,2,0,1:T(4,128)(2,1)} %bitcast.53), kind=kLoop, calls=%fused_computation.6 | loop fusion | flops 202752 | bytes 270336 | tf_op jit(solution)/shard_map/stack | solution.py:364
  10.8 1.7 %collective-permute-start.3 = (bf16[33,16,128]{2,1,0:T(8,128)(2,1)S(1)}, bf16[33,16,128]{2,1,0:T(8,128)(2,1)S(1)}, u32[]{:S(2)}, u32[]{:S(2)}) collective-permute-start(bf16[33,16,128]{2,1,0:T(8,128)(2,1)S(1)} %bitcast.43), channel_id=1, source_target_pairs={{0,4},{1,5},{2,6},{3,7},{4,8},{5,9},{6,10},{7,11},{8,12},{9,13},{1... | collective-permute-start | bytes 405512 | tf_op jit(solution)/shard_map/ppermute | solution.py:29
  12.5 3.3 %collective-permute-start.4 = (bf16[33,16,128]{2,1,0:T(8,128)(2,1)S(1)}, bf16[33,16,128]{2,1,0:T(8,128)(2,1)S(1)}, u32[]{:S(2)}, u32[]{:S(2)}) collective-permute-start(bf16[33,16,128]{2,1,0:T(8,128)(2,1)S(1)} %bitcast.44), channel_id=1, source_target_pairs={{0,8},{1,9},{2,10},{3,11},{4,12},{5,13},{6,14},{7,15},{8,0},{9,1},... | collective-permute-start | bytes 405512 | tf_op jit(solution)/shard_map/ppermute | solution.py:29
  15.8 0.7 %collective-permute-start.5 = (bf16[33,16,128]{2,1,0:T(8,128)(2,1)S(1)}, bf16[33,16,128]{2,1,0:T(8,128)(2,1)S(1)}, u32[]{:S(2)}, u32[]{:S(2)}) collective-permute-start(bf16[33,16,128]{2,1,0:T(8,128)(2,1)S(1)} %bitcast.45), channel_id=1, source_target_pairs={{0,12},{1,13},{2,14},{3,15},{4,0},{5,1},{6,2},{7,3},{8,4},{9,5},{1... | collective-permute-start | bytes 405512 | tf_op jit(solution)/shard_map/ppermute | solution.py:29
  16.6 0.1 stack.50.refs_0_
  16.8 0.3 collective-permute-done.3
  17.0 2.6 %collective-permute-done.4 = bf16[33,16,128]{2,1,0:T(8,128)(2,1)S(1)} collective-permute-done((bf16[33,16,128]{2,1,0:T(8,128)(2,1)S(1)}, bf16[33,16,128]{2,1,0:T(8,128)(2,1)S(1)}, u32[]{:S(2)}, u32[]{:S(2)}) %collective-permute-start.4) | collective-permute-done | bytes 135200 | tf_op jit(solution)/shard_map/ppermute | solution.py:29
  19.7 0.0 collective-permute-done.5
  19.7 0.1 pad_maximum_fusion.1._
  19.8 0.0 copy-start.2
  19.8 1.7 %collective-permute-start.6 = (bf16[4,33,16,128]{3,2,1,0:T(8,128)(2,1)S(1)}, bf16[4,33,16,128]{3,2,1,0:T(8,128)(2,1)S(1)}, u32[]{:S(2)}, u32[]{:S(2)}) collective-permute-start(bf16[4,33,16,128]{3,2,1,0:T(8,128)(2,1)S(1)} %pad_maximum_fusion.1._), channel_id=1, source_target_pairs={{0,1},{1,2},{2,3},{3,0},{4,5},{5,6},{6,7},{7,4},{8,9},{9,10},{10,1... | collective-permute-start | bytes 1622024 | tf_op jit(solution)/shard_map/ppermute | solution.py:29
  21.4 2.3 %collective-permute-start.7 = (bf16[4,33,16,128]{3,2,1,0:T(8,128)(2,1)S(1)}, bf16[4,33,16,128]{3,2,1,0:T(8,128)(2,1)S(1)}, u32[]{:S(2)}, u32[]{:S(2)}) collective-permute-start(bf16[4,33,16,128]{3,2,1,0:T(8,128)(2,1)S(1)} %pad_maximum_fusion.1._), channel_id=1, source_target_pairs={{0,2},{1,3},{2,0},{3,1},{4,6},{5,7},{6,4},{7,5},{8,10},{9,11},{10,... | collective-permute-start | bytes 1622024 | tf_op jit(solution)/shard_map/ppermute | solution.py:29
  23.8 1.4 %collective-permute-start.8 = (bf16[4,33,16,128]{3,2,1,0:T(8,128)(2,1)S(1)}, bf16[4,33,16,128]{3,2,1,0:T(8,128)(2,1)S(1)}, u32[]{:S(2)}, u32[]{:S(2)}) collective-permute-start(bf16[4,33,16,128]{3,2,1,0:T(8,128)(2,1)S(1)} %pad_maximum_fusion.1._), channel_id=1, source_target_pairs={{0,3},{1,0},{2,1},{3,2},{4,7},{5,4},{6,5},{7,6},{8,11},{9,8},{10,9... | collective-permute-start | bytes 1622024 | tf_op jit(solution)/shard_map/ppermute | solution.py:29
  25.1 4.0 %collective-permute-start.9 = (bf16[4,33,16,128]{3,2,1,0:T(8,128)(2,1)S(1)}, bf16[4,33,16,128]{3,2,1,0:T(8,128)(2,1)S(1)}, u32[]{:S(2)}, u32[]{:S(2)}) collective-permute-start(bf16[4,33,16,128]{3,2,1,0:T(8,128)(2,1)S(1)} %pad_maximum_fusion.1._), channel_id=1, source_target_pairs={{0,16},{1,17},{2,18},{3,19},{4,20},{5,21},{6,22},{7,23},{8,24},{9,... | collective-permute-start | bytes 1622024 | tf_op jit(solution)/shard_map/ppermute | solution.py:29
  29.2 0.0 copy-done.2
  29.2 6.8 %rebuild.1.refs_4_ = bf16[32,128,128]{2,1,0:T(8,128)(2,1)} custom-call(s32[32,128]{1,0:T(8,128)} %ids_ref.1, bf16[8192,128]{1,0:T(8,128)(2,1)} %cent_ref.1, f32[32,1,128]{2,1,0:T(1,128)} %bitcast.57, bf16[32,128,128]{2,1,0:T(8,128)(2,1)} %code_ref.1, bf16[4,33,16,128]{3,2,1,0:T(8,128)(2,1)} %copy-done.2), custom_call_target="tpu_custom_call" | custom-call | flops 12000000 | bytes 20000000 | tf_op jit(solution)/shard_map/rebuild/pallas_call | solution.py:71
  36.0 0.0 collective-permute-done.6
  36.0 0.1 collective-permute-start.10
  36.1 0.5 collective-permute-done.7
  36.6 4.7 %collective-permute-start.11 = (bf16[4,33,16,128]{3,2,1,0:T(8,128)(2,1)S(1)}, bf16[4,33,16,128]{3,2,1,0:T(8,128)(2,1)S(1)}, u32[]{:S(2)}, u32[]{:S(2)}) collective-permute-start(bf16[4,33,16,128]{3,2,1,0:T(8,128)(2,1)S(1)} %collective-permute-done.7), channel_id=1, source_target_pairs={{0,16},{1,17},{2,18},{3,19},{4,20},{5,21},{6,22},{7,23},{8,24},{9,... | collective-permute-start | bytes 1622024 | tf_op jit(solution)/shard_map/ppermute | solution.py:29
  41.2 0.0 collective-permute-done.8
  41.2 0.0 collective-permute-start.12
  41.3 0.0 collective-permute-done.9
  41.3 0.1 constant_dynamic-update-slice_fusion.2
  41.4 0.1 constant_dynamic-update-slice_fusion.1
  41.5 0.1 constant_dynamic-update-slice_fusion
  41.5 0.0 copy-start
  41.6 0.0 copy-start.1
  41.6 0.0 collective-permute-done.10
  41.6 1.2 %collective-permute-done.11 = bf16[4,33,16,128]{3,2,1,0:T(8,128)(2,1)S(1)} collective-permute-done((bf16[4,33,16,128]{3,2,1,0:T(8,128)(2,1)S(1)}, bf16[4,33,16,128]{3,2,1,0:T(8,128)(2,1)S(1)}, u32[]{:S(2)}, u32[]{:S(2)}) %collective-permute-start.11) | collective-permute-done | bytes 540704 | tf_op jit(solution)/shard_map/ppermute | solution.py:29
  42.8 0.8 %collective-permute-done.12 = bf16[4,33,16,128]{3,2,1,0:T(8,128)(2,1)S(1)} collective-permute-done((bf16[4,33,16,128]{3,2,1,0:T(8,128)(2,1)S(1)}, bf16[4,33,16,128]{3,2,1,0:T(8,128)(2,1)S(1)}, u32[]{:S(2)}, u32[]{:S(2)}) %collective-permute-start.12) | collective-permute-done | bytes 540704 | tf_op jit(solution)/shard_map/ppermute | solution.py:29
  43.6 0.3 pad_maximum_fusion
  43.9 0.0 copy-done
  43.9 0.0 copy-done.1
  43.9 0.0 copy-start.3
  43.9 6.4 %maxsim_late.1 = f32[128,128]{1,0:T(8,128)} custom-call(s32[5]{0:T(128)S(1)} %stack.50.refs_0_, s32[32]{0:T(128)S(1)} %copy-done.1, bf16[528,16,128]{2,1,0:T(8,128)(2,1)S(1)} %bitcast.42, bf16[528,16,128]{2,1,0:T(8,128)(2,1)S(1)} %bitcast.41, bf16[32,128,128]{2,1,0:T(8,128)(2,1)S(1)} %copy-done), custom_call_target="tpu_custom_call" | custom-call | flops 12000000 | bytes 20000000 | tf_op jit(solution)/shard_map/maxsim_late/pallas_call | solution.py:278
  50.3 8.2 %all-to-all-start = ((f32[128,1,128]{2,1,0:T(1,128)}), f32[128,1,128]{2,1,0:T(1,128)S(1)}, u32[]{:S(2)}, u32[]{:S(2)}) async-start(f32[128,1,128]{2,1,0:T(1,128)} %bitcast.23), calls=%async_computation | async-start | bytes 131072 | tf_op jit(solution)/shard_map/all_to_all | solution.py:379
  58.5 0.0 copy-done.3
  58.5 5.8 %convolution_reduce_fusion = f32[32,8192]{1,0:T(8,128)} fusion(bf16[8192,128]{1,0:T(8,128)(2,1)S(1)} %copy-done.3, bf16[32,32,128]{2,0,1:T(8,128)(2,1)S(1)} %maximum_bitcast_fusion), kind=kOutput, calls=%fused_computation | convolution fusion | flops 2155610112 | bytes 3407872 | tf_op jit(solution)/shard_map/dot_general | solution.py:351
  64.2 3.8 %all-to-all-done = f32[128,1,128]{2,1,0:T(1,128)S(1)} async-done(((f32[128,1,128]{2,1,0:T(1,128)}), f32[128,1,128]{2,1,0:T(1,128)S(1)}, u32[]{:S(2)}, u32[]{:S(2)}) %all-to-all-start) | async-done | bytes 65568 | tf_op jit(solution)/shard_map/all_to_all | solution.py:379
  68.0 0.0 copy-start.4
  68.0 0.6 copy-done.4
  68.6 1.7 %final.1 = f32[8,32]{1,0:T(8,128)} custom-call(s32[8,32]{1,0:T(8,128)} %bitcast.59, f32[128,128]{1,0:T(8,128)} %bitcast.52), custom_call_target="tpu_custom_call" | custom-call | tf_op jit(solution)/shard_map/final/pallas_call | solution.py:340
  (9 shorter events, 0.2 us)
Async XLA Ops:
  2.1 5.6 %collective-permute-start = (bf16[33,4,128]{2,1,0:T(4,128)(2,1)}, bf16[33,4,128]{2,1,0:T(4,128)(2,1)S(1)}, u32[]{:S(2)}, u32[]{:S(2)}) collective-permute-start(bf16[33,4,128]{2,1,0:T(4,128)(2,1)} %pack.1), channel_id=1, source_target_pairs={{0,32},{1,33},{2,34},{3,35},{4,36},{5,37},{6,38},{7,39},{8,40},{9,... | collective-permute-start | bytes 101384 | tf_op jit(solution)/shard_map/ppermute | solution.py:29
  4.1 4.5 %collective-permute-start.1 = (bf16[33,4,128]{2,1,0:T(4,128)(2,1)}, bf16[33,4,128]{2,1,0:T(4,128)(2,1)S(1)}, u32[]{:S(2)}, u32[]{:S(2)}) collective-permute-start(bf16[33,4,128]{2,1,0:T(4,128)(2,1)} %pack.1), channel_id=1, source_target_pairs={{0,64},{1,65},{2,66},{3,67},{4,68},{5,69},{6,70},{7,71},{8,72},{9,... | collective-permute-start | bytes 101384 | tf_op jit(solution)/shard_map/ppermute | solution.py:29
  6.6 3.3 %collective-permute-start.2 = (bf16[33,4,128]{2,1,0:T(4,128)(2,1)}, bf16[33,4,128]{2,1,0:T(4,128)(2,1)S(1)}, u32[]{:S(2)}, u32[]{:S(2)}) collective-permute-start(bf16[33,4,128]{2,1,0:T(4,128)(2,1)} %pack.1), channel_id=1, source_target_pairs={{0,96},{1,97},{2,98},{3,99},{4,100},{5,101},{6,102},{7,103},{8,104... | collective-permute-start | bytes 101384 | tf_op jit(solution)/shard_map/ppermute | solution.py:29
  10.8 6.2 %collective-permute-start.3 = (bf16[33,16,128]{2,1,0:T(8,128)(2,1)S(1)}, bf16[33,16,128]{2,1,0:T(8,128)(2,1)S(1)}, u32[]{:S(2)}, u32[]{:S(2)}) collective-permute-start(bf16[33,16,128]{2,1,0:T(8,128)(2,1)S(1)} %bitcast.43), channel_id=1, source_target_pairs={{0,4},{1,5},{2,6},{3,7},{4,8},{5,9},{6,10},{7,11},{8,12},{9,13},{1... | collective-permute-start | bytes 405512 | tf_op jit(solution)/shard_map/ppermute | solution.py:29
  12.5 7.1 %collective-permute-start.4 = (bf16[33,16,128]{2,1,0:T(8,128)(2,1)S(1)}, bf16[33,16,128]{2,1,0:T(8,128)(2,1)S(1)}, u32[]{:S(2)}, u32[]{:S(2)}) collective-permute-start(bf16[33,16,128]{2,1,0:T(8,128)(2,1)S(1)} %bitcast.44), channel_id=1, source_target_pairs={{0,8},{1,9},{2,10},{3,11},{4,12},{5,13},{6,14},{7,15},{8,0},{9,1},... | collective-permute-start | bytes 405512 | tf_op jit(solution)/shard_map/ppermute | solution.py:29
  15.8 3.9 %collective-permute-start.5 = (bf16[33,16,128]{2,1,0:T(8,128)(2,1)S(1)}, bf16[33,16,128]{2,1,0:T(8,128)(2,1)S(1)}, u32[]{:S(2)}, u32[]{:S(2)}) collective-permute-start(bf16[33,16,128]{2,1,0:T(8,128)(2,1)S(1)} %bitcast.45), channel_id=1, source_target_pairs={{0,12},{1,13},{2,14},{3,15},{4,0},{5,1},{6,2},{7,3},{8,4},{9,5},{1... | collective-permute-start | bytes 405512 | tf_op jit(solution)/shard_map/ppermute | solution.py:29
  19.8 9.4 %copy-start.2 = (bf16[4,33,16,128]{3,2,1,0:T(8,128)(2,1)}, bf16[4,33,16,128]{3,2,1,0:T(8,128)(2,1)S(1)}, u32[]{:S(2)}) copy-start(bf16[4,33,16,128]{3,2,1,0:T(8,128)(2,1)S(1)} %pad_maximum_fusion.1._) | copy-start | bytes 1622020
  19.8 16.2 %collective-permute-start.6 = (bf16[4,33,16,128]{3,2,1,0:T(8,128)(2,1)S(1)}, bf16[4,33,16,128]{3,2,1,0:T(8,128)(2,1)S(1)}, u32[]{:S(2)}, u32[]{:S(2)}) collective-permute-start(bf16[4,33,16,128]{3,2,1,0:T(8,128)(2,1)S(1)} %pad_maximum_fusion.1._), channel_id=1, source_target_pairs={{0,1},{1,2},{2,3},{3,0},{4,5},{5,6},{6,7},{7,4},{8,9},{9,10},{10,1... | collective-permute-start | bytes 1622024 | tf_op jit(solution)/shard_map/ppermute | solution.py:29
  21.4 15.2 %collective-permute-start.7 = (bf16[4,33,16,128]{3,2,1,0:T(8,128)(2,1)S(1)}, bf16[4,33,16,128]{3,2,1,0:T(8,128)(2,1)S(1)}, u32[]{:S(2)}, u32[]{:S(2)}) collective-permute-start(bf16[4,33,16,128]{3,2,1,0:T(8,128)(2,1)S(1)} %pad_maximum_fusion.1._), channel_id=1, source_target_pairs={{0,2},{1,3},{2,0},{3,1},{4,6},{5,7},{6,4},{7,5},{8,10},{9,11},{10,... | collective-permute-start | bytes 1622024 | tf_op jit(solution)/shard_map/ppermute | solution.py:29
  23.8 17.5 %collective-permute-start.8 = (bf16[4,33,16,128]{3,2,1,0:T(8,128)(2,1)S(1)}, bf16[4,33,16,128]{3,2,1,0:T(8,128)(2,1)S(1)}, u32[]{:S(2)}, u32[]{:S(2)}) collective-permute-start(bf16[4,33,16,128]{3,2,1,0:T(8,128)(2,1)S(1)} %pad_maximum_fusion.1._), channel_id=1, source_target_pairs={{0,3},{1,0},{2,1},{3,2},{4,7},{5,4},{6,5},{7,6},{8,11},{9,8},{10,9... | collective-permute-start | bytes 1622024 | tf_op jit(solution)/shard_map/ppermute | solution.py:29
  25.1 16.1 %collective-permute-start.9 = (bf16[4,33,16,128]{3,2,1,0:T(8,128)(2,1)S(1)}, bf16[4,33,16,128]{3,2,1,0:T(8,128)(2,1)S(1)}, u32[]{:S(2)}, u32[]{:S(2)}) collective-permute-start(bf16[4,33,16,128]{3,2,1,0:T(8,128)(2,1)S(1)} %pad_maximum_fusion.1._), channel_id=1, source_target_pairs={{0,16},{1,17},{2,18},{3,19},{4,20},{5,21},{6,22},{7,23},{8,24},{9,... | collective-permute-start | bytes 1622024 | tf_op jit(solution)/shard_map/ppermute | solution.py:29
  36.0 5.6 %collective-permute-start.10 = (bf16[4,33,16,128]{3,2,1,0:T(8,128)(2,1)S(1)}, bf16[4,33,16,128]{3,2,1,0:T(8,128)(2,1)S(1)}, u32[]{:S(2)}, u32[]{:S(2)}) collective-permute-start(bf16[4,33,16,128]{3,2,1,0:T(8,128)(2,1)S(1)} %collective-permute-done.6), channel_id=1, source_target_pairs={{0,16},{1,17},{2,18},{3,19},{4,20},{5,21},{6,22},{7,23},{8,24},{9,... | collective-permute-start | bytes 1622024 | tf_op jit(solution)/shard_map/ppermute | solution.py:29
  36.6 6.2 %collective-permute-start.11 = (bf16[4,33,16,128]{3,2,1,0:T(8,128)(2,1)S(1)}, bf16[4,33,16,128]{3,2,1,0:T(8,128)(2,1)S(1)}, u32[]{:S(2)}, u32[]{:S(2)}) collective-permute-start(bf16[4,33,16,128]{3,2,1,0:T(8,128)(2,1)S(1)} %collective-permute-done.7), channel_id=1, source_target_pairs={{0,16},{1,17},{2,18},{3,19},{4,20},{5,21},{6,22},{7,23},{8,24},{9,... | collective-permute-start | bytes 1622024 | tf_op jit(solution)/shard_map/ppermute | solution.py:29
  41.2 2.3 %collective-permute-start.12 = (bf16[4,33,16,128]{3,2,1,0:T(8,128)(2,1)S(1)}, bf16[4,33,16,128]{3,2,1,0:T(8,128)(2,1)S(1)}, u32[]{:S(2)}, u32[]{:S(2)}) collective-permute-start(bf16[4,33,16,128]{3,2,1,0:T(8,128)(2,1)S(1)} %collective-permute-done.8), channel_id=1, source_target_pairs={{0,16},{1,17},{2,18},{3,19},{4,20},{5,21},{6,22},{7,23},{8,24},{9,... | collective-permute-start | bytes 1622024 | tf_op jit(solution)/shard_map/ppermute | solution.py:29
  41.5 2.3 %copy-start = (bf16[32,128,128]{2,1,0:T(8,128)(2,1)S(1)}, bf16[32,128,128]{2,1,0:T(8,128)(2,1)}, u32[]{:S(2)}) copy-start(bf16[32,128,128]{2,1,0:T(8,128)(2,1)} %rebuild.1.refs_4_) | copy-start | bytes 3145732
  41.6 2.3 %copy-start.1 = (s32[32]{0:T(128)S(1)}, s32[32]{0:T(128)}, u32[]{:S(2)}) copy-start(s32[32]{0:T(128)} %refs_1_.1) | copy-start | bytes 388
  43.9 14.6 %copy-start.3 = (bf16[8192,128]{1,0:T(8,128)(2,1)S(1)}, bf16[8192,128]{1,0:T(8,128)(2,1)}, u32[]{:S(2)}) copy-start(bf16[8192,128]{1,0:T(8,128)(2,1)} %cent_ref.1) | copy-start | bytes 6291460
  50.3 17.7 %all-to-all-start = ((f32[128,1,128]{2,1,0:T(1,128)}), f32[128,1,128]{2,1,0:T(1,128)S(1)}, u32[]{:S(2)}, u32[]{:S(2)}) async-start(f32[128,1,128]{2,1,0:T(1,128)} %bitcast.23), calls=%async_computation | async-start | bytes 131072 | tf_op jit(solution)/shard_map/all_to_all | solution.py:379
  68.0 0.6 copy-start.4

commit v3 on v2

--- a/solution.py
+++ b/solution.py
@@ -92,12 +92,12 @@
 
 REBUILD_STEPS = 4
 CHUNK = 8
-TOGETHER = 8
+TOGETHER = 16
 PLACES = 768
 DUMMY_ROW = DEVICES * CAP
-ALL = [(k, j, 4 * k + j) for k in range(SIDE) for j in range(SIDE)]
-EARLY = [(k, j, 4 * n + j) for n, k in enumerate((0, 1, 3)) for j in (0, 1, 3)]
-LATE = [(2, j, j) for j in range(4)] + [(k, 2, 4 + n) for n, k in enumerate((0, 1, 3))]
+X_STEPS = (0, 1, 2, 3)
+FIRST_STEPS = (0, 1, 2, 3)
+SECOND_STEPS = (0, 1, 3, 2)
 
 
 def as_bf16(mask):
@@ -108,22 +108,20 @@
     return jnp.dot(a.astype(jnp.bfloat16), b, preferred_element_type=jnp.float32)
 
 
-def by_row(row, values):
-    result = jnp.full(row.shape, values[-1], jnp.int32)
+def picked(place, values):
+    result = jnp.full(place.shape, values[-1], jnp.int32)
     for i, value in enumerate(values[:-1]):
-        result = jnp.where(row == i, value, result)
+        result = jnp.where(place == i, value, result)
     return result
 
 
-def request_list(rows, where_ref, own_ref, other_ref, meta):
+def request_list(where_ref, own_ref, other_ref, meta):
     per = PER
     queries = per - 1
     me, my_x, my_core, my_y, my_z = (where_ref[i] for i in range(5))
-    if len(rows) < 16:
-        meta[...] = jnp.full(meta.shape, -1.0, jnp.float32)
     for half, ref in enumerate((own_ref, other_ref)):
-        for i, (_, _, at) in enumerate(rows):
-            meta[pl.ds((half * 16 + i) * 16, 16), :] = ref[at * per + queries].astype(jnp.float32)
+        for i in range(SIDE * SIDE):
+            meta[pl.ds((half * 16 + i) * 16, 16), :] = ref[i * per + queries].astype(jnp.float32)
     square = (DEVICES, 128)
     lane = lax.broadcasted_iota(jnp.int32, square, 1)
     line = lax.broadcasted_iota(jnp.int32, square, 0)
@@ -179,15 +177,11 @@
     u, query, slot, rank = (found[i : i + 1, :] for i in range(4))
     half = u >> 6
     at = (u >> 2) & 15
-    kx = u & 3
-    if len(rows) == 16:
-        straight, turned = at, (at & 3) * 4 + (at >> 2)
-        first, second = at & 3, at >> 2
-    else:
-        places = {(k, j): i for k, j, i in rows}
-        straight = by_row(at, [i for _, _, i in rows])
-        turned = by_row(at, [places[j, k] for k, j, _ in rows])
-        first, second = by_row(at, [j for _, j, _ in rows]), by_row(at, [k for k, _, _ in rows])
+    kx = picked(u & 3, X_STEPS)
+    first, second = picked(at & 3, FIRST_STEPS), picked(at >> 2, SECOND_STEPS)
+    turned_second = picked(at & 3, [SECOND_STEPS.index(step) for step in FIRST_STEPS])
+    turned_first = picked(at >> 2, [FIRST_STEPS.index(step) for step in SECOND_STEPS])
+    straight, turned = at, turned_second * 4 + turned_first
     own_at = jnp.where(half == 0, straight, turned) * per + query - 1
     other_at = jnp.where(half == 0, turned, straight) * per + query - 1
     core = my_core ^ half
@@ -204,27 +198,24 @@
 
 
 def maxsim_kernel(
-    rows, last, where_ref, lengths_ref, own_ref, other_ref, held_ref, best_in, out_ref, meta, table, work, best, sem
+    where_ref, lengths_ref, own_ref, other_ref, held_ref, out_ref, meta, table, work, best, sem
 ):
-    if best is None:
-        best = out_ref
-    elif best_in is not None:
-        best[...] = best_in[...]
-    item, goal, all_chunks = request_list(rows, where_ref, own_ref, other_ref, meta)
-    table[0:1, :] = item
-    table[1:2, :] = goal
-    table[2:3, 0:128] = all_chunks
+    item, goal, all_chunks = request_list(where_ref, own_ref, other_ref, meta)
+    for i in range(PLACES // 128):
+        table[i : i + 1, :] = item[:, i * 128 : i * 128 + 128]
+        table[8 + i : 9 + i, :] = goal[:, i * 128 : i * 128 + 128]
+    table[7:8, :] = all_chunks
     copy = pltpu.make_async_copy(table, work, sem)
     copy.start()
     copy.wait()
-    total = work[2, 0]
+    total = work[7, 0]
     slots_id = lax.broadcasted_iota(jnp.int32, (128, CHUNK * 32), 0)
     group = lax.broadcasted_iota(jnp.int32, (1, 128), 1) >> 5
 
-    def one(chunk):
+    def one(step, chunk):
         tokens = []
         for i in range(CHUNK):
-            item = work[0, chunk * CHUNK + i]
+            item = work[step, chunk * CHUNK + i]
             if i == 0:
                 block = item & 31
             tokens.append(own_ref[(item >> 5) & 1023])
@@ -239,81 +230,66 @@
         return jnp.max(kept, axis=0, keepdims=True)
 
     def steps(step, carry):
-        done = [one(step * TOGETHER + i) for i in range(TOGETHER)]
+        done = [one(step, i) for i in range(TOGETHER)]
         for i, value in enumerate(done):
             for j in range(CHUNK):
                 part = value[:, j // 4 * 128 : j // 4 * 128 + 128]
-                dest = work[1, (step * TOGETHER + i) * CHUNK + j]
+                dest = work[8 + step, i * CHUNK + j]
                 best[pl.ds(dest, 1), :] = jnp.where(group == j % 4, part, 0.0)
         return carry
 
     lax.fori_loop(0, (total + TOGETHER - 1) // TOGETHER, steps, 0)
-    if last:
-        lane = lax.broadcasted_iota(jnp.int32, (DEVICES, 128), 1)
-        result = jnp.zeros((DEVICES, 128), jnp.float32)
-        for rank in range(CAP):
-            value = jnp.sum(best[pl.ds(rank * DEVICES, DEVICES), :], axis=1, keepdims=True)
-            result = jnp.where(lane == rank, value * (1.0 / 32.0), result)
-        out_ref[...] = result
-
-
-def maxsim(where, lengths, own, other, held, rows=ALL, last=True, best=None):
-    def body(*refs):
-        refs = list(refs)
-        if best is None:
-            refs.insert(5, None)
-        if not last:
-            refs.insert(-1, None)
-        maxsim_kernel(rows, last, *refs)
-
-    buffer = (DEVICES * CAP + 8, 128)
-    scratch = [
-        VMEM((DEVICES * 4, 128), jnp.float32),
-        VMEM((8, PLACES), jnp.int32),
-        SMEM((8, PLACES), jnp.int32),
-    ]
-    if last:
-        scratch.append(VMEM(buffer, jnp.float32))
-    operands = (where, lengths, own, other, held) + (() if best is None else (best,))
+    lane = lax.broadcasted_iota(jnp.int32, (DEVICES, 128), 1)
+    result = jnp.zeros((DEVICES, 128), jnp.float32)
+    for rank in range(CAP):
+        value = jnp.sum(best[pl.ds(rank * DEVICES, DEVICES), :], axis=1, keepdims=True)
+        result = jnp.where(lane == rank, value * (1.0 / 32.0), result)
+    out_ref[...] = result
+
+
+def maxsim(where, lengths, own, other, held):
     return pl.pallas_call(
-        body,
-        out_shape=jax.ShapeDtypeStruct((DEVICES, 128) if last else buffer, jnp.float32),
-        in_specs=[pl.BlockSpec(memory_space=SMEM)] * 2
-        + [pl.BlockSpec(memory_space=VMEM)] * (len(operands) - 2),
+        maxsim_kernel,
+        out_shape=jax.ShapeDtypeStruct((DEVICES, 128), jnp.float32),
+        in_specs=[pl.BlockSpec(memory_space=SMEM)] * 2 + [pl.BlockSpec(memory_space=VMEM)] * 3,
         out_specs=pl.BlockSpec(memory_space=VMEM),
-        scratch_shapes=scratch + [pltpu.SemaphoreType.DMA],
+        scratch_shapes=[
+            VMEM((DEVICES * 4, 128), jnp.float32),
+            VMEM((16, 128), jnp.int32),
+            SMEM((16, 128), jnp.int32),
+            VMEM((DEVICES * CAP + 8, 128), jnp.float32),
+            pltpu.SemaphoreType.DMA,
+        ],
         compiler_params=pltpu.CompilerParams(vmem_limit_bytes=32 << 20),
         cost_estimate=pl.CostEstimate(flops=12000000, bytes_accessed=20000000, transcendentals=0),
-        name="maxsim_late" if last else "maxsim_early",
-    )(*operands)
-
-
-def pack_kernel(query_ref, owner_ref, slot_ref, out_ref):
+        name="maxsim",
+    )(where, lengths, own, other, held)
+
+
+def pack_kernel(query_ref, ask_ref, out_ref):
     queries = query_ref.shape[0]
     out_ref[:queries] = query_ref[...]
     lane = lax.broadcasted_iota(jnp.int32, (1, 128), 1) >> 5
+    wide = jnp.concatenate([ask_ref[...]] * 4, axis=1)
     rows = []
-    for ref in (owner_ref, slot_ref):
-        wide = ref[...].astype(jnp.float32)
-        wide = jnp.concatenate([wide] * 4, axis=1)
-        for part in range(2):
-            row = jnp.zeros((1, 128), jnp.float32)
-            for i in range(4):
-                c = part * 4 + i
-                row = jnp.where(lane == i, wide[c : c + 1, :], row)
-            rows.append(row)
+    for part in range(4):
+        row = wide[4 * part : 4 * part + 1, :]
+        for i in range(1, 4):
+            row = jnp.where(lane == i, wide[4 * part + i : 4 * part + i + 1, :], row)
+        rows.append(row)
     out_ref[queries] = jnp.concatenate(rows, axis=0).astype(jnp.bfloat16)
 
 
-def pack(queries, owners, slots):
+def pack(queries, asks):
     rows, tokens, width = queries.shape
     return pl.pallas_call(
         pack_kernel,
         out_shape=jax.ShapeDtypeStruct((rows + 1, tokens, width), jnp.bfloat16),
-        in_specs=[pl.BlockSpec(memory_space=VMEM)] * 3,
+        in_specs=[pl.BlockSpec(memory_space=VMEM)] * 2,
         out_specs=pl.BlockSpec(memory_space=VMEM),
+        compiler_params=pltpu.CompilerParams(vmem_limit_bytes=4 << 20),
         name="pack",
-    )(queries, owners, slots)
+    )(queries, asks)
 
 
 def final_kernel(owner_ref, back_ref, out_ref):
@@ -342,6 +318,7 @@
         out_shape=jax.ShapeDtypeStruct(owners.shape, jnp.float32),
         in_specs=[pl.BlockSpec(memory_space=VMEM)] * 2,
         out_specs=pl.BlockSpec(memory_space=VMEM),
+        compiler_params=pltpu.CompilerParams(vmem_limit_bytes=4 << 20),
         name="final",
     )(owners, back)
 
@@ -360,14 +337,20 @@
 def per_device(queries, centroids, codes, scales, centroid_ids, lengths, owners, slots):
     query_rows = queries.shape[0]
     owner, slot = owners[0].T, slots[0].T
-    first = pack(queries, owner, slot)
-    by_x = jnp.stack([first] + [moved(first, along_x(k)) for k in range(1, SIDE)], axis=1)
+    asks = jnp.concatenate([owner, slot], axis=0).astype(jnp.float32)
+    first = pack(queries, asks)
+    by_x = jnp.stack([first if k == 0 else moved(first, along_x(k)) for k in X_STEPS], axis=1)
     by_x = by_x.reshape(query_rows + 1, SIDE * 4, 128)
-    second = jnp.stack([by_x] + [moved(by_x, along_first(k)) for k in range(1, SIDE)], axis=0)
-    pieces = [second] + [moved(second, along_second(k)) for k in range(1, SIDE)]
+    second = jnp.stack(
+        [by_x if k == 0 else moved(by_x, along_first(k)) for k in FIRST_STEPS], axis=0
+    )
+    pieces = [second if k == 0 else moved(second, along_second(k)) for k in SECOND_STEPS]
     peers = [moved(piece, other_core) for piece in pieces]
     own = jnp.concatenate(pieces, axis=0).reshape(-1, SIDE * 4, 128)
-    other = jnp.concatenate(peers, axis=0).reshape(-1, SIDE * 4, 128)
+    other = jnp.zeros((SIDE * SIDE, query_rows + 1, SIDE * 4, 128), queries.dtype)
+    for i, piece in enumerate(peers):
+        other = lax.dynamic_update_slice(other, piece, (i * SIDE, 0, 0, 0))
+    other = other.reshape(-1, SIDE * 4, 128)
 
     lists, score = lax.axis_index("lists"), lax.axis_index("score")
     where = jnp.stack(

time: 70.2 us -> 66.6 us (0.949)
  Pallas kernels: 16.4 us -> 12.9 us
  starting transfers between devices: 33.6 us -> 32.8 us
  local copies, waits for them, and re-layouts: 1.18 us -> 1.93 us
    pallas_call x1, Pallas kernels: 1.48 us -> 0.08 us  [pack(): pl.pallas_call(pack_kernel, out_shape=jax.ShapeDtypeStruct((rows + 1, tok...]
    pallas_call x1, Pallas kernels: 6.4 us -> 5.16 us  [maxsim(): pl.pallas_call(maxsim_kernel, out_shape=jax.ShapeDtypeStruct((DEVICES, 12...]
    pallas_call x1, Pallas kernels: 1.71 us -> 0.85 us  [final(): pl.pallas_call(final_kernel, out_shape=jax.ShapeDtypeStruct(owners.shape,...]
    another operation x2, other arithmetic: 0.95 us -> 0.19 us  [the longest x1 0.12 us: per_device(): jnp.stack([first if k == 0 else moved(first, along_x(k)) for k in X_STEPS...]
    convert_element_type x0 -> x1, other arithmetic: none -> 0.71 us  [per_device(): asks = jnp.concatenate([owner, slot], axis=0).astype(jnp.float32)]
  transfers between devices with their start and end apart: 14 -> 14, of which waited for: 8 -> 6; matrix products, arithmetic and copies ran while one was open for 9% -> 10% of each run, Pallas kernels for 10% -> 10%
where the time goes in v3:
time: 66.6 us; the launch traced here: 66.1 us
  starting transfers between devices  32.8 us (49%)
  Pallas kernels  12.9 us (19%)
  waiting for transfers between devices  11 us (17%)
  matrix products  5.77 us (9%)
  local copies, waits for them, and re-layouts  1.93 us (3%)
  other arithmetic  0.92 us (1%)
  between operations  0.87 us (1%)
    ppermute x13, starting transfers between devices, moved(): return lax.ppermute(value, AXES, pairs)  25.1 us
    all_to_all x1, starting transfers between devices, per_device(): lax.all_to_all(outgoing, AXES, split_axis=0, concat_axis=0, tiled=True)  7.65 us
    ppermute x13, waiting for transfers between devices, moved(): return lax.ppermute(value, AXES, pairs)  7.21 us
    pallas_call x1, Pallas kernels, rebuild(): pl.pallas_call(rebuild_kernel, grid=(REBUILD_STEPS,), out_shape=jax.Shape...  6.78 us
    dot_general x1, matrix products, relevance_of(): lax.dot_general(tokens.reshape(token_count * query_rows, width), centroid...  5.77 us
    pallas_call x1, Pallas kernels, maxsim(): pl.pallas_call(maxsim_kernel, out_shape=jax.ShapeDtypeStruct((DEVICES, 12...  5.16 us
    all_to_all x1, waiting for transfers between devices, per_device(): lax.all_to_all(outgoing, AXES, split_axis=0, concat_axis=0, tiled=True)  3.79 us
  transfers between devices with their start and end apart: 14, of which 6 were waited for; matrix products, arithmetic and copies ran while one was open for 10% of the time, Pallas kernels for 10%

profile of v3, /device:TPU:1, one launch (start us, length us, event | category | flops | bytes accessed | tf_op | source)
XLA Modules:
  0.0 66.1 jit_solution(2614692396049246141)
XLA Ops:
  0.6 0.7 %add_convert_fusion.ask_ref = f32[16,32]{1,0:T(8,128)S(1)} fusion(s32[8,32]{1,0:T(8,128)} %bitcast.61, s32[8,32]{1,0:T(8,128)} %bitcast.45), kind=kLoop, calls=%fused_computation.14 | loop fusion | flops 1024 | bytes 4096 | tf_op jit(solution)/shard_map/convert_element_type | solution.py:340
  1.3 0.0 copy-start.1
  1.3 0.8 %copy-done.1 = bf16[32,4,128]{2,1,0:T(4,128)(2,1)S(1)} copy-done((bf16[32,4,128]{2,1,0:T(4,128)(2,1)S(1)}, bf16[32,4,128]{2,1,0:T(4,128)(2,1)}, u32[]{:S(2)}) %copy-start.1) | copy-done | bytes 32792
  2.1 0.1 pack.1
  2.2 3.4 %collective-permute-start.2 = (bf16[33,4,128]{2,1,0:T(4,128)(2,1)S(1)}, bf16[33,4,128]{2,1,0:T(4,128)(2,1)S(1)}, u32[]{:S(2)}, u32[]{:S(2)}) collective-permute-start(bf16[33,4,128]{2,1,0:T(4,128)(2,1)S(1)} %pack.1), channel_id=1, source_target_pairs={{0,96},{1,97},{2,98},{3,99},{4,100},{5,101},{6,102},{7,103},{8,104... | collective-permute-start | bytes 101384 | tf_op jit(solution)/shard_map/ppermute | solution.py:29
  5.6 0.5 collective-permute-start.1
  6.1 0.6 collective-permute-start
  6.7 0.0 collective-permute-done.2
  6.7 3.2 %collective-permute-done.1 = bf16[33,4,128]{2,1,0:T(4,128)(2,1)S(1)} collective-permute-done((bf16[33,4,128]{2,1,0:T(4,128)(2,1)S(1)}, bf16[33,4,128]{2,1,0:T(4,128)(2,1)S(1)}, u32[]{:S(2)}, u32[]{:S(2)}) %collective-permute-start.1) | collective-permute-done | bytes 33824 | tf_op jit(solution)/shard_map/ppermute | solution.py:29
  9.8 0.4 collective-permute-done
  10.2 0.1 pad_maximum_fusion.1
  10.4 1.7 %collective-permute-start.3 = (bf16[33,16,128]{2,1,0:T(8,128)(2,1)S(1)}, bf16[33,16,128]{2,1,0:T(8,128)(2,1)S(1)}, u32[]{:S(2)}, u32[]{:S(2)}) collective-permute-start(bf16[33,16,128]{2,1,0:T(8,128)(2,1)S(1)} %bitcast.47), channel_id=1, source_target_pairs={{0,4},{1,5},{2,6},{3,7},{4,8},{5,9},{6,10},{7,11},{8,12},{9,13},{1... | collective-permute-start | bytes 405512 | tf_op jit(solution)/shard_map/ppermute | solution.py:29
  12.1 3.3 %collective-permute-start.4 = (bf16[33,16,128]{2,1,0:T(8,128)(2,1)S(1)}, bf16[33,16,128]{2,1,0:T(8,128)(2,1)S(1)}, u32[]{:S(2)}, u32[]{:S(2)}) collective-permute-start(bf16[33,16,128]{2,1,0:T(8,128)(2,1)S(1)} %bitcast.48), channel_id=1, source_target_pairs={{0,8},{1,9},{2,10},{3,11},{4,12},{5,13},{6,14},{7,15},{8,0},{9,1},... | collective-permute-start | bytes 405512 | tf_op jit(solution)/shard_map/ppermute | solution.py:29
  15.4 0.7 %collective-permute-start.5 = (bf16[33,16,128]{2,1,0:T(8,128)(2,1)S(1)}, bf16[33,16,128]{2,1,0:T(8,128)(2,1)S(1)}, u32[]{:S(2)}, u32[]{:S(2)}) collective-permute-start(bf16[33,16,128]{2,1,0:T(8,128)(2,1)S(1)} %bitcast.49), channel_id=1, source_target_pairs={{0,12},{1,13},{2,14},{3,15},{4,0},{5,1},{6,2},{7,3},{8,4},{9,5},{1... | collective-permute-start | bytes 405512 | tf_op jit(solution)/shard_map/ppermute | solution.py:29
  16.1 0.1 stack.50.where_ref
  16.3 0.3 collective-permute-done.3
  16.6 2.6 %collective-permute-done.4 = bf16[33,16,128]{2,1,0:T(8,128)(2,1)S(1)} collective-permute-done((bf16[33,16,128]{2,1,0:T(8,128)(2,1)S(1)}, bf16[33,16,128]{2,1,0:T(8,128)(2,1)S(1)}, u32[]{:S(2)}, u32[]{:S(2)}) %collective-permute-start.4) | collective-permute-done | bytes 135200 | tf_op jit(solution)/shard_map/ppermute | solution.py:29
  19.2 0.0 collective-permute-done.5
  19.2 0.1 pad_maximum_fusion._
  19.3 0.0 copy-start.4
  19.3 1.7 %collective-permute-start.6 = (bf16[4,33,16,128]{3,2,1,0:T(8,128)(2,1)S(1)}, bf16[4,33,16,128]{3,2,1,0:T(8,128)(2,1)S(1)}, u32[]{:S(2)}, u32[]{:S(2)}) collective-permute-start(bf16[4,33,16,128]{3,2,1,0:T(8,128)(2,1)S(1)} %pad_maximum_fusion._), channel_id=1, source_target_pairs={{0,1},{1,2},{2,3},{3,0},{4,5},{5,6},{6,7},{7,4},{8,9},{9,10},{10,1... | collective-permute-start | bytes 1622024 | tf_op jit(solution)/shard_map/ppermute | solution.py:29
  21.0 1.2 %collective-permute-start.7 = (bf16[4,33,16,128]{3,2,1,0:T(8,128)(2,1)S(1)}, bf16[4,33,16,128]{3,2,1,0:T(8,128)(2,1)S(1)}, u32[]{:S(2)}, u32[]{:S(2)}) collective-permute-start(bf16[4,33,16,128]{3,2,1,0:T(8,128)(2,1)S(1)} %pad_maximum_fusion._), channel_id=1, source_target_pairs={{0,3},{1,0},{2,1},{3,2},{4,7},{5,4},{6,5},{7,6},{8,11},{9,8},{10,9... | collective-permute-start | bytes 1622024 | tf_op jit(solution)/shard_map/ppermute | solution.py:29
  22.2 1.9 %collective-permute-start.8 = (bf16[4,33,16,128]{3,2,1,0:T(8,128)(2,1)S(1)}, bf16[4,33,16,128]{3,2,1,0:T(8,128)(2,1)S(1)}, u32[]{:S(2)}, u32[]{:S(2)}) collective-permute-start(bf16[4,33,16,128]{3,2,1,0:T(8,128)(2,1)S(1)} %pad_maximum_fusion._), channel_id=1, source_target_pairs={{0,2},{1,3},{2,0},{3,1},{4,6},{5,7},{6,4},{7,5},{8,10},{9,11},{10,... | collective-permute-start | bytes 1622024 | tf_op jit(solution)/shard_map/ppermute | solution.py:29
  24.1 4.2 %collective-permute-start.9 = (bf16[4,33,16,128]{3,2,1,0:T(8,128)(2,1)S(1)}, bf16[4,33,16,128]{3,2,1,0:T(8,128)(2,1)S(1)}, u32[]{:S(2)}, u32[]{:S(2)}) collective-permute-start(bf16[4,33,16,128]{3,2,1,0:T(8,128)(2,1)S(1)} %pad_maximum_fusion._), channel_id=1, source_target_pairs={{0,16},{1,17},{2,18},{3,19},{4,20},{5,21},{6,22},{7,23},{8,24},{9,... | collective-permute-start | bytes 1622024 | tf_op jit(solution)/shard_map/ppermute | solution.py:29
  28.3 0.0 copy-done.4
  28.3 6.8 %rebuild.1.held_ref = bf16[32,128,128]{2,1,0:T(8,128)(2,1)} custom-call(s32[32,128]{1,0:T(8,128)} %ids_ref.1, bf16[8192,128]{1,0:T(8,128)(2,1)} %cent_ref.1, f32[32,1,128]{2,1,0:T(1,128)} %bitcast.59, bf16[32,128,128]{2,1,0:T(8,128)(2,1)} %code_ref.1, bf16[4,33,16,128]{3,2,1,0:T(8,128)(2,1)} %copy-done.4), custom_call_target="tpu_custom_call" | custom-call | flops 12000000 | bytes 20000000 | tf_op jit(solution)/shard_map/rebuild/pallas_call | solution.py:71
  35.1 0.0 collective-permute-done.6
  35.1 0.1 collective-permute-start.10
  35.2 0.0 collective-permute-done.7
  35.2 4.1 %collective-permute-start.11 = (bf16[4,33,16,128]{3,2,1,0:T(8,128)(2,1)S(1)}, bf16[4,33,16,128]{3,2,1,0:T(8,128)(2,1)S(1)}, u32[]{:S(2)}, u32[]{:S(2)}) collective-permute-start(bf16[4,33,16,128]{3,2,1,0:T(8,128)(2,1)S(1)} %collective-permute-done.7), channel_id=1, source_target_pairs={{0,16},{1,17},{2,18},{3,19},{4,20},{5,21},{6,22},{7,23},{8,24},{9,... | collective-permute-start | bytes 1622024 | tf_op jit(solution)/shard_map/ppermute | solution.py:29
  39.3 0.0 collective-permute-done.8
  39.3 1.8 %collective-permute-start.12 = (bf16[4,33,16,128]{3,2,1,0:T(8,128)(2,1)S(1)}, bf16[4,33,16,128]{3,2,1,0:T(8,128)(2,1)S(1)}, u32[]{:S(2)}, u32[]{:S(2)}) collective-permute-start(bf16[4,33,16,128]{3,2,1,0:T(8,128)(2,1)S(1)} %collective-permute-done.8), channel_id=1, source_target_pairs={{0,16},{1,17},{2,18},{3,19},{4,20},{5,21},{6,22},{7,23},{8,24},{9,... | collective-permute-start | bytes 1622024 | tf_op jit(solution)/shard_map/ppermute | solution.py:29
  41.1 0.1 constant_dynamic-update-slice_fusion.2
  41.2 0.0 collective-permute-done.9
  41.3 0.3 dynamic_update_slice.12
  41.6 0.1 constant_dynamic-update-slice_fusion.1
  41.6 0.0 copy-start
  41.7 0.0 copy-start.3
  41.7 0.1 constant_dynamic-update-slice_fusion
  41.7 0.0 collective-permute-done.10
  41.8 0.1 constant_dynamic-update-slice_fusion.9
  41.8 0.0 collective-permute-done.11
  41.8 0.1 constant_dynamic-update-slice_fusion.8
  41.9 0.8 %collective-permute-done.12 = bf16[4,33,16,128]{3,2,1,0:T(8,128)(2,1)S(1)} collective-permute-done((bf16[4,33,16,128]{3,2,1,0:T(8,128)(2,1)S(1)}, bf16[4,33,16,128]{3,2,1,0:T(8,128)(2,1)S(1)}, u32[]{:S(2)}, u32[]{:S(2)}) %collective-permute-start.12) | collective-permute-done | bytes 540704 | tf_op jit(solution)/shard_map/ppermute | solution.py:29
  42.7 0.1 constant_dynamic-update-slice_fusion.7
  42.8 0.1 copy-done
  42.9 0.0 copy-done.3
  42.9 0.0 copy-start.5
  42.9 5.2 %maxsim.1 = f32[128,128]{1,0:T(8,128)} custom-call(s32[5]{0:T(128)S(1)} %stack.50.where_ref, s32[32]{0:T(128)S(1)} %copy-done.3, bf16[528,16,128]{2,1,0:T(8,128)(2,1)S(1)} %bitcast.42, bf16[528,16,128]{2,1,0:T(8,128)(2,1)S(1)} %bitcast.41, bf16[32,128,128]{2,1,0:T(8,128)(2,1)S(1)} %copy-done), custom_call_target="tpu_custom_call" | custom-call | flops 12000000 | bytes 20000000 | tf_op jit(solution)/shard_map/maxsim/pallas_call | solution.py:251
  48.0 7.7 %all-to-all-start = ((f32[128,1,128]{2,1,0:T(1,128)}), f32[128,1,128]{2,1,0:T(1,128)S(1)}, u32[]{:S(2)}, u32[]{:S(2)}) async-start(f32[128,1,128]{2,1,0:T(1,128)} %bitcast.23), calls=%async_computation | async-start | bytes 131072 | tf_op jit(solution)/shard_map/all_to_all | solution.py:362
  55.7 0.0 copy-done.5
  55.7 0.0 copy-start.2
  55.7 5.8 %convolution_reduce_fusion = f32[32,8192]{1,0:T(8,128)} fusion(bf16[8192,128]{1,0:T(8,128)(2,1)S(1)} %copy-done.5, bf16[32,32,128]{2,0,1:T(8,128)(2,1)S(1)} %maximum_bitcast_fusion), kind=kOutput, calls=%fused_computation | convolution fusion | flops 2155610112 | bytes 3407872 | tf_op jit(solution)/shard_map/dot_general | solution.py:328
  61.5 3.8 %all-to-all-done = f32[128,1,128]{2,1,0:T(1,128)S(1)} async-done(((f32[128,1,128]{2,1,0:T(1,128)}), f32[128,1,128]{2,1,0:T(1,128)S(1)}, u32[]{:S(2)}, u32[]{:S(2)}) %all-to-all-start) | async-done | bytes 65568 | tf_op jit(solution)/shard_map/all_to_all | solution.py:362
  65.3 0.0 copy-done.2
  65.3 0.9 %final.1 = f32[8,32]{1,0:T(8,128)} custom-call(s32[8,32]{1,0:T(8,128)S(1)} %bitcast.46, f32[128,128]{1,0:T(8,128)S(1)} %bitcast.43), custom_call_target="tpu_custom_call" | custom-call | tf_op jit(solution)/shard_map/final/pallas_call | solution.py:316
  (9 shorter events, 0.2 us)
Async XLA Ops:
  1.3 0.8 %copy-start.1 = (bf16[32,4,128]{2,1,0:T(4,128)(2,1)S(1)}, bf16[32,4,128]{2,1,0:T(4,128)(2,1)}, u32[]{:S(2)}) copy-start(bf16[32,4,128]{2,1,0:T(4,128)(2,1)} %query_ref.1) | copy-start | bytes 98308
  2.2 4.5 %collective-permute-start.2 = (bf16[33,4,128]{2,1,0:T(4,128)(2,1)S(1)}, bf16[33,4,128]{2,1,0:T(4,128)(2,1)S(1)}, u32[]{:S(2)}, u32[]{:S(2)}) collective-permute-start(bf16[33,4,128]{2,1,0:T(4,128)(2,1)S(1)} %pack.1), channel_id=1, source_target_pairs={{0,96},{1,97},{2,98},{3,99},{4,100},{5,101},{6,102},{7,103},{8,104... | collective-permute-start | bytes 101384 | tf_op jit(solution)/shard_map/ppermute | solution.py:29
  5.6 4.3 %collective-permute-start.1 = (bf16[33,4,128]{2,1,0:T(4,128)(2,1)S(1)}, bf16[33,4,128]{2,1,0:T(4,128)(2,1)S(1)}, u32[]{:S(2)}, u32[]{:S(2)}) collective-permute-start(bf16[33,4,128]{2,1,0:T(4,128)(2,1)S(1)} %pack.1), channel_id=1, source_target_pairs={{0,64},{1,65},{2,66},{3,67},{4,68},{5,69},{6,70},{7,71},{8,72},{9,... | collective-permute-start | bytes 101384 | tf_op jit(solution)/shard_map/ppermute | solution.py:29
  6.1 4.1 %collective-permute-start = (bf16[33,4,128]{2,1,0:T(4,128)(2,1)S(1)}, bf16[33,4,128]{2,1,0:T(4,128)(2,1)S(1)}, u32[]{:S(2)}, u32[]{:S(2)}) collective-permute-start(bf16[33,4,128]{2,1,0:T(4,128)(2,1)S(1)} %pack.1), channel_id=1, source_target_pairs={{0,32},{1,33},{2,34},{3,35},{4,36},{5,37},{6,38},{7,39},{8,40},{9,... | collective-permute-start | bytes 101384 | tf_op jit(solution)/shard_map/ppermute | solution.py:29
  10.4 6.2 %collective-permute-start.3 = (bf16[33,16,128]{2,1,0:T(8,128)(2,1)S(1)}, bf16[33,16,128]{2,1,0:T(8,128)(2,1)S(1)}, u32[]{:S(2)}, u32[]{:S(2)}) collective-permute-start(bf16[33,16,128]{2,1,0:T(8,128)(2,1)S(1)} %bitcast.47), channel_id=1, source_target_pairs={{0,4},{1,5},{2,6},{3,7},{4,8},{5,9},{6,10},{7,11},{8,12},{9,13},{1... | collective-permute-start | bytes 405512 | tf_op jit(solution)/shard_map/ppermute | solution.py:29
  12.1 7.1 %collective-permute-start.4 = (bf16[33,16,128]{2,1,0:T(8,128)(2,1)S(1)}, bf16[33,16,128]{2,1,0:T(8,128)(2,1)S(1)}, u32[]{:S(2)}, u32[]{:S(2)}) collective-permute-start(bf16[33,16,128]{2,1,0:T(8,128)(2,1)S(1)} %bitcast.48), channel_id=1, source_target_pairs={{0,8},{1,9},{2,10},{3,11},{4,12},{5,13},{6,14},{7,15},{8,0},{9,1},... | collective-permute-start | bytes 405512 | tf_op jit(solution)/shard_map/ppermute | solution.py:29
  15.4 3.9 %collective-permute-start.5 = (bf16[33,16,128]{2,1,0:T(8,128)(2,1)S(1)}, bf16[33,16,128]{2,1,0:T(8,128)(2,1)S(1)}, u32[]{:S(2)}, u32[]{:S(2)}) collective-permute-start(bf16[33,16,128]{2,1,0:T(8,128)(2,1)S(1)} %bitcast.49), channel_id=1, source_target_pairs={{0,12},{1,13},{2,14},{3,15},{4,0},{5,1},{6,2},{7,3},{8,4},{9,5},{1... | collective-permute-start | bytes 405512 | tf_op jit(solution)/shard_map/ppermute | solution.py:29
  19.3 8.9 %copy-start.4 = (bf16[4,33,16,128]{3,2,1,0:T(8,128)(2,1)}, bf16[4,33,16,128]{3,2,1,0:T(8,128)(2,1)S(1)}, u32[]{:S(2)}) copy-start(bf16[4,33,16,128]{3,2,1,0:T(8,128)(2,1)S(1)} %pad_maximum_fusion._) | copy-start | bytes 1622020
  19.3 15.8 %collective-permute-start.6 = (bf16[4,33,16,128]{3,2,1,0:T(8,128)(2,1)S(1)}, bf16[4,33,16,128]{3,2,1,0:T(8,128)(2,1)S(1)}, u32[]{:S(2)}, u32[]{:S(2)}) collective-permute-start(bf16[4,33,16,128]{3,2,1,0:T(8,128)(2,1)S(1)} %pad_maximum_fusion._), channel_id=1, source_target_pairs={{0,1},{1,2},{2,3},{3,0},{4,5},{5,6},{6,7},{7,4},{8,9},{9,10},{10,1... | collective-permute-start | bytes 1622024 | tf_op jit(solution)/shard_map/ppermute | solution.py:29
  21.0 14.2 %collective-permute-start.7 = (bf16[4,33,16,128]{3,2,1,0:T(8,128)(2,1)S(1)}, bf16[4,33,16,128]{3,2,1,0:T(8,128)(2,1)S(1)}, u32[]{:S(2)}, u32[]{:S(2)}) collective-permute-start(bf16[4,33,16,128]{3,2,1,0:T(8,128)(2,1)S(1)} %pad_maximum_fusion._), channel_id=1, source_target_pairs={{0,3},{1,0},{2,1},{3,2},{4,7},{5,4},{6,5},{7,6},{8,11},{9,8},{10,9... | collective-permute-start | bytes 1622024 | tf_op jit(solution)/shard_map/ppermute | solution.py:29
  22.2 17.1 %collective-permute-start.8 = (bf16[4,33,16,128]{3,2,1,0:T(8,128)(2,1)S(1)}, bf16[4,33,16,128]{3,2,1,0:T(8,128)(2,1)S(1)}, u32[]{:S(2)}, u32[]{:S(2)}) collective-permute-start(bf16[4,33,16,128]{3,2,1,0:T(8,128)(2,1)S(1)} %pad_maximum_fusion._), channel_id=1, source_target_pairs={{0,2},{1,3},{2,0},{3,1},{4,6},{5,7},{6,4},{7,5},{8,10},{9,11},{10,... | collective-permute-start | bytes 1622024 | tf_op jit(solution)/shard_map/ppermute | solution.py:29
  24.1 17.1 %collective-permute-start.9 = (bf16[4,33,16,128]{3,2,1,0:T(8,128)(2,1)S(1)}, bf16[4,33,16,128]{3,2,1,0:T(8,128)(2,1)S(1)}, u32[]{:S(2)}, u32[]{:S(2)}) collective-permute-start(bf16[4,33,16,128]{3,2,1,0:T(8,128)(2,1)S(1)} %pad_maximum_fusion._), channel_id=1, source_target_pairs={{0,16},{1,17},{2,18},{3,19},{4,20},{5,21},{6,22},{7,23},{8,24},{9,... | collective-permute-start | bytes 1622024 | tf_op jit(solution)/shard_map/ppermute | solution.py:29
  35.1 6.6 %collective-permute-start.10 = (bf16[4,33,16,128]{3,2,1,0:T(8,128)(2,1)S(1)}, bf16[4,33,16,128]{3,2,1,0:T(8,128)(2,1)S(1)}, u32[]{:S(2)}, u32[]{:S(2)}) collective-permute-start(bf16[4,33,16,128]{3,2,1,0:T(8,128)(2,1)S(1)} %collective-permute-done.6), channel_id=1, source_target_pairs={{0,16},{1,17},{2,18},{3,19},{4,20},{5,21},{6,22},{7,23},{8,24},{9,... | collective-permute-start | bytes 1622024 | tf_op jit(solution)/shard_map/ppermute | solution.py:29
  35.2 6.6 %collective-permute-start.11 = (bf16[4,33,16,128]{3,2,1,0:T(8,128)(2,1)S(1)}, bf16[4,33,16,128]{3,2,1,0:T(8,128)(2,1)S(1)}, u32[]{:S(2)}, u32[]{:S(2)}) collective-permute-start(bf16[4,33,16,128]{3,2,1,0:T(8,128)(2,1)S(1)} %collective-permute-done.7), channel_id=1, source_target_pairs={{0,16},{1,17},{2,18},{3,19},{4,20},{5,21},{6,22},{7,23},{8,24},{9,... | collective-permute-start | bytes 1622024 | tf_op jit(solution)/shard_map/ppermute | solution.py:29
  39.3 3.4 %collective-permute-start.12 = (bf16[4,33,16,128]{3,2,1,0:T(8,128)(2,1)S(1)}, bf16[4,33,16,128]{3,2,1,0:T(8,128)(2,1)S(1)}, u32[]{:S(2)}, u32[]{:S(2)}) collective-permute-start(bf16[4,33,16,128]{3,2,1,0:T(8,128)(2,1)S(1)} %collective-permute-done.8), channel_id=1, source_target_pairs={{0,16},{1,17},{2,18},{3,19},{4,20},{5,21},{6,22},{7,23},{8,24},{9,... | collective-permute-start | bytes 1622024 | tf_op jit(solution)/shard_map/ppermute | solution.py:29
  41.6 1.2 %copy-start = (bf16[32,128,128]{2,1,0:T(8,128)(2,1)S(1)}, bf16[32,128,128]{2,1,0:T(8,128)(2,1)}, u32[]{:S(2)}) copy-start(bf16[32,128,128]{2,1,0:T(8,128)(2,1)} %rebuild.1.held_ref) | copy-start | bytes 3145732
  41.7 1.2 %copy-start.3 = (s32[32]{0:T(128)S(1)}, s32[32]{0:T(128)}, u32[]{:S(2)}) copy-start(s32[32]{0:T(128)} %lengths_ref.1) | copy-start | bytes 388
  42.9 12.8 %copy-start.5 = (bf16[8192,128]{1,0:T(8,128)(2,1)S(1)}, bf16[8192,128]{1,0:T(8,128)(2,1)}, u32[]{:S(2)}) copy-start(bf16[8192,128]{1,0:T(8,128)(2,1)} %cent_ref.1) | copy-start | bytes 6291460
  48.0 17.2 %all-to-all-start = ((f32[128,1,128]{2,1,0:T(1,128)}), f32[128,1,128]{2,1,0:T(1,128)S(1)}, u32[]{:S(2)}, u32[]{:S(2)}) async-start(f32[128,1,128]{2,1,0:T(1,128)} %bitcast.23), calls=%async_computation | async-start | bytes 131072 | tf_op jit(solution)/shard_map/all_to_all | solution.py:362
  55.7 9.6 %copy-start.2 = (s32[1,32,8]{1,2,0:T(8,128)S(1)}, s32[1,32,8]{1,2,0:T(8,128)}, u32[]{:S(2)}) copy-start(s32[1,32,8]{1,2,0:T(8,128)} %param.14) | copy-start | bytes 3076

commit v4 on v3

--- a/solution.py
+++ b/solution.py
@@ -356,7 +356,7 @@
     where = jnp.stack(
         [lists * 16 + score, lists // 2, lists % 2, score // SIDE, score % SIDE]
     ).astype(jnp.int32)
-    held = rebuild(codes, scales, centroid_ids, centroids, second)
+    held = rebuild(codes, scales, centroid_ids, centroids, second[1, 0])
     totals = maxsim(where, lengths, own, other, held)
     outgoing = totals.reshape(DEVICES, 1, 128)
     back = lax.all_to_all(outgoing, AXES, split_axis=0, concat_axis=0, tiled=True)

time: 66.6 us -> 65.7 us (0.986)
  starting transfers between devices: 32.8 us -> 31.2 us
    all_to_all x1, starting transfers between devices: 7.65 us -> 6.57 us  [per_device(): lax.all_to_all(outgoing, AXES, split_axis=0, concat_axis=0, tiled=True)]
  transfers between devices with their start and end apart: 14 -> 14, of which waited for: 6 -> 6; matrix products, arithmetic and copies ran while one was open for 10% -> 11% of each run, Pallas kernels for 10% -> 10%
where the time goes in v4:
time: 65.7 us; the launch traced here: 65 us
  starting transfers between devices  31.2 us (47%)
  Pallas kernels  12.8 us (19%)
  waiting for transfers between devices  11 us (17%)
  matrix products  5.77 us (9%)
  local copies, waits for them, and re-layouts  2.52 us (4%)
  other arithmetic  0.92 us (1%)
  between operations  0.85 us (1%)
    ppermute x13, starting transfers between devices, moved(): return lax.ppermute(value, AXES, pairs)  24.6 us
    ppermute x13, waiting for transfers between devices, moved(): return lax.ppermute(value, AXES, pairs)  7.21 us
    pallas_call x1, Pallas kernels, rebuild(): pl.pallas_call(rebuild_kernel, grid=(REBUILD_STEPS,), out_shape=jax.Shape...  6.75 us
    all_to_all x1, starting transfers between devices, per_device(): lax.all_to_all(outgoing, AXES, split_axis=0, concat_axis=0, tiled=True)  6.57 us
    dot_general x1, matrix products, relevance_of(): lax.dot_general(tokens.reshape(token_count * query_rows, width), centroid...  5.77 us
    pallas_call x1, Pallas kernels, maxsim(): pl.pallas_call(maxsim_kernel, out_shape=jax.ShapeDtypeStruct((DEVICES, 12...  5.15 us
    all_to_all x1, waiting for transfers between devices, per_device(): lax.all_to_all(outgoing, AXES, split_axis=0, concat_axis=0, tiled=True)  3.77 us
  transfers between devices with their start and end apart: 14, of which 6 were waited for; matrix products, arithmetic and copies ran while one was open for 11% of the time, Pallas kernels for 10%

profile of v4, /device:TPU:1, one launch (start us, length us, event | category | flops | bytes accessed | tf_op | source)
XLA Modules:
  0.0 65.0 jit_solution(1507123667449223974)
XLA Ops:
  0.6 0.7 %add_convert_fusion.ask_ref = f32[16,32]{1,0:T(8,128)S(1)} fusion(s32[8,32]{1,0:T(8,128)} %bitcast.64, s32[8,32]{1,0:T(8,128)} %bitcast.47), kind=kLoop, calls=%fused_computation.14 | loop fusion | flops 1024 | bytes 4096 | tf_op jit(solution)/shard_map/convert_element_type | solution.py:340
  1.3 0.0 copy-start.1
  1.3 0.8 %copy-done.1 = bf16[32,4,128]{2,1,0:T(4,128)(2,1)S(1)} copy-done((bf16[32,4,128]{2,1,0:T(4,128)(2,1)S(1)}, bf16[32,4,128]{2,1,0:T(4,128)(2,1)}, u32[]{:S(2)}) %copy-start.1) | copy-done | bytes 32792
  2.1 0.1 pack.1
  2.2 3.4 %collective-permute-start.2 = (bf16[33,4,128]{2,1,0:T(4,128)(2,1)S(1)}, bf16[33,4,128]{2,1,0:T(4,128)(2,1)S(1)}, u32[]{:S(2)}, u32[]{:S(2)}) collective-permute-start(bf16[33,4,128]{2,1,0:T(4,128)(2,1)S(1)} %pack.1), channel_id=1, source_target_pairs={{0,96},{1,97},{2,98},{3,99},{4,100},{5,101},{6,102},{7,103},{8,104... | collective-permute-start | bytes 101384 | tf_op jit(solution)/shard_map/ppermute | solution.py:29
  5.6 0.5 collective-permute-start.1
  6.1 0.6 collective-permute-start
  6.7 0.0 collective-permute-done.2
  6.7 3.2 %collective-permute-done.1 = bf16[33,4,128]{2,1,0:T(4,128)(2,1)S(1)} collective-permute-done((bf16[33,4,128]{2,1,0:T(4,128)(2,1)S(1)}, bf16[33,4,128]{2,1,0:T(4,128)(2,1)S(1)}, u32[]{:S(2)}, u32[]{:S(2)}) %collective-permute-start.1) | collective-permute-done | bytes 33824 | tf_op jit(solution)/shard_map/ppermute | solution.py:29
  9.8 0.4 collective-permute-done
  10.2 0.1 pad_maximum_fusion.1
  10.4 1.7 %collective-permute-start.3 = (bf16[33,16,128]{2,1,0:T(8,128)(2,1)S(1)}, bf16[33,16,128]{2,1,0:T(8,128)(2,1)S(1)}, u32[]{:S(2)}, u32[]{:S(2)}) collective-permute-start(bf16[33,16,128]{2,1,0:T(8,128)(2,1)S(1)} %bitcast.49), channel_id=1, source_target_pairs={{0,4},{1,5},{2,6},{3,7},{4,8},{5,9},{6,10},{7,11},{8,12},{9,13},{1... | collective-permute-start | bytes 405512 | tf_op jit(solution)/shard_map/ppermute | solution.py:29
  12.1 3.3 %collective-permute-start.4 = (bf16[33,16,128]{2,1,0:T(8,128)(2,1)S(1)}, bf16[33,16,128]{2,1,0:T(8,128)(2,1)S(1)}, u32[]{:S(2)}, u32[]{:S(2)}) collective-permute-start(bf16[33,16,128]{2,1,0:T(8,128)(2,1)S(1)} %bitcast.50), channel_id=1, source_target_pairs={{0,8},{1,9},{2,10},{3,11},{4,12},{5,13},{6,14},{7,15},{8,0},{9,1},... | collective-permute-start | bytes 405512 | tf_op jit(solution)/shard_map/ppermute | solution.py:29
  15.4 0.7 %collective-permute-start.5 = (bf16[33,16,128]{2,1,0:T(8,128)(2,1)S(1)}, bf16[33,16,128]{2,1,0:T(8,128)(2,1)S(1)}, u32[]{:S(2)}, u32[]{:S(2)}) collective-permute-start(bf16[33,16,128]{2,1,0:T(8,128)(2,1)S(1)} %bitcast.51), channel_id=1, source_target_pairs={{0,12},{1,13},{2,14},{3,15},{4,0},{5,1},{6,2},{7,3},{8,4},{9,5},{1... | collective-permute-start | bytes 405512 | tf_op jit(solution)/shard_map/ppermute | solution.py:29
  16.1 0.1 stack.50.where_ref
  16.3 0.3 collective-permute-done.3
  16.6 2.6 %collective-permute-done.4 = bf16[33,16,128]{2,1,0:T(8,128)(2,1)S(1)} collective-permute-done((bf16[33,16,128]{2,1,0:T(8,128)(2,1)S(1)}, bf16[33,16,128]{2,1,0:T(8,128)(2,1)S(1)}, u32[]{:S(2)}, u32[]{:S(2)}) %collective-permute-start.4) | collective-permute-done | bytes 135200 | tf_op jit(solution)/shard_map/ppermute | solution.py:29
  19.2 0.0 collective-permute-done.5
  19.2 0.1 pad_maximum_fusion
  19.3 1.7 %collective-permute-start.6 = (bf16[4,33,16,128]{3,2,1,0:T(8,128)(2,1)S(1)}, bf16[4,33,16,128]{3,2,1,0:T(8,128)(2,1)S(1)}, u32[]{:S(2)}, u32[]{:S(2)}) collective-permute-start(bf16[4,33,16,128]{3,2,1,0:T(8,128)(2,1)S(1)} %pad_maximum_fusion), channel_id=1, source_target_pairs={{0,1},{1,2},{2,3},{3,0},{4,5},{5,6},{6,7},{7,4},{8,9},{9,10},{10,1... | collective-permute-start | bytes 1622024 | tf_op jit(solution)/shard_map/ppermute | solution.py:29
  21.0 1.2 %collective-permute-start.7 = (bf16[4,33,16,128]{3,2,1,0:T(8,128)(2,1)S(1)}, bf16[4,33,16,128]{3,2,1,0:T(8,128)(2,1)S(1)}, u32[]{:S(2)}, u32[]{:S(2)}) collective-permute-start(bf16[4,33,16,128]{3,2,1,0:T(8,128)(2,1)S(1)} %pad_maximum_fusion), channel_id=1, source_target_pairs={{0,3},{1,0},{2,1},{3,2},{4,7},{5,4},{6,5},{7,6},{8,11},{9,8},{10,9... | collective-permute-start | bytes 1622024 | tf_op jit(solution)/shard_map/ppermute | solution.py:29
  22.2 1.9 %collective-permute-start.8 = (bf16[4,33,16,128]{3,2,1,0:T(8,128)(2,1)S(1)}, bf16[4,33,16,128]{3,2,1,0:T(8,128)(2,1)S(1)}, u32[]{:S(2)}, u32[]{:S(2)}) collective-permute-start(bf16[4,33,16,128]{3,2,1,0:T(8,128)(2,1)S(1)} %pad_maximum_fusion), channel_id=1, source_target_pairs={{0,2},{1,3},{2,0},{3,1},{4,6},{5,7},{6,4},{7,5},{8,10},{9,11},{10,... | collective-permute-start | bytes 1622024 | tf_op jit(solution)/shard_map/ppermute | solution.py:29
  24.1 4.2 %collective-permute-start.9 = (bf16[4,33,16,128]{3,2,1,0:T(8,128)(2,1)S(1)}, bf16[4,33,16,128]{3,2,1,0:T(8,128)(2,1)S(1)}, u32[]{:S(2)}, u32[]{:S(2)}) collective-permute-start(bf16[4,33,16,128]{3,2,1,0:T(8,128)(2,1)S(1)} %pad_maximum_fusion), channel_id=1, source_target_pairs={{0,16},{1,17},{2,18},{3,19},{4,20},{5,21},{6,22},{7,23},{8,24},{9,... | collective-permute-start | bytes 1622024 | tf_op jit(solution)/shard_map/ppermute | solution.py:29
  28.3 0.6 slice_bitcast_fusion.1._
  28.9 6.8 %rebuild.1.held_ref = bf16[32,128,128]{2,1,0:T(8,128)(2,1)} custom-call(s32[32,128]{1,0:T(8,128)} %ids_ref.1, bf16[8192,128]{1,0:T(8,128)(2,1)} %cent_ref.1, f32[32,1,128]{2,1,0:T(1,128)} %bitcast.62, bf16[32,128,128]{2,1,0:T(8,128)(2,1)} %code_ref.1, bf16[16,128]{1,0:T(8,128)(2,1)} %slice_bitcast_fusion.1._), custom_call_target="tpu_custom_call" | custom-call | flops 12000000 | bytes 20000000 | tf_op jit(solution)/shard_map/rebuild/pallas_call | solution.py:71
  35.7 0.0 collective-permute-done.6
  35.7 0.1 collective-permute-start.10
  35.8 0.0 collective-permute-done.7
  35.8 3.6 %collective-permute-start.11 = (bf16[4,33,16,128]{3,2,1,0:T(8,128)(2,1)S(1)}, bf16[4,33,16,128]{3,2,1,0:T(8,128)(2,1)S(1)}, u32[]{:S(2)}, u32[]{:S(2)}) collective-permute-start(bf16[4,33,16,128]{3,2,1,0:T(8,128)(2,1)S(1)} %collective-permute-done.7), channel_id=1, source_target_pairs={{0,16},{1,17},{2,18},{3,19},{4,20},{5,21},{6,22},{7,23},{8,24},{9,... | collective-permute-start | bytes 1622024 | tf_op jit(solution)/shard_map/ppermute | solution.py:29
  39.3 0.0 collective-permute-done.8
  39.3 1.8 %collective-permute-start.12 = (bf16[4,33,16,128]{3,2,1,0:T(8,128)(2,1)S(1)}, bf16[4,33,16,128]{3,2,1,0:T(8,128)(2,1)S(1)}, u32[]{:S(2)}, u32[]{:S(2)}) collective-permute-start(bf16[4,33,16,128]{3,2,1,0:T(8,128)(2,1)S(1)} %collective-permute-done.8), channel_id=1, source_target_pairs={{0,16},{1,17},{2,18},{3,19},{4,20},{5,21},{6,22},{7,23},{8,24},{9,... | collective-permute-start | bytes 1622024 | tf_op jit(solution)/shard_map/ppermute | solution.py:29
  41.1 0.1 constant_dynamic-update-slice_fusion.2
  41.2 0.0 collective-permute-done.9
  41.3 0.3 dynamic_update_slice.12
  41.6 0.1 constant_dynamic-update-slice_fusion.1
  41.6 0.0 copy-start
  41.7 0.0 copy-start.3
  41.7 0.1 constant_dynamic-update-slice_fusion
  41.7 0.0 collective-permute-done.10
  41.8 0.1 constant_dynamic-update-slice_fusion.9
  41.8 0.0 collective-permute-done.11
  41.8 0.1 constant_dynamic-update-slice_fusion.8
  41.9 0.8 %collective-permute-done.12 = bf16[4,33,16,128]{3,2,1,0:T(8,128)(2,1)S(1)} collective-permute-done((bf16[4,33,16,128]{3,2,1,0:T(8,128)(2,1)S(1)}, bf16[4,33,16,128]{3,2,1,0:T(8,128)(2,1)S(1)}, u32[]{:S(2)}, u32[]{:S(2)}) %collective-permute-start.12) | collective-permute-done | bytes 540704 | tf_op jit(solution)/shard_map/ppermute | solution.py:29
  42.7 0.1 constant_dynamic-update-slice_fusion.7
  42.8 0.1 copy-done
  42.9 0.0 copy-done.3
  42.9 0.0 copy-start.4
  42.9 5.2 %maxsim.1 = f32[128,128]{1,0:T(8,128)} custom-call(s32[5]{0:T(128)S(1)} %stack.50.where_ref, s32[32]{0:T(128)S(1)} %copy-done.3, bf16[528,16,128]{2,1,0:T(8,128)(2,1)S(1)} %bitcast.44, bf16[528,16,128]{2,1,0:T(8,128)(2,1)S(1)} %bitcast.43, bf16[32,128,128]{2,1,0:T(8,128)(2,1)S(1)} %copy-done), custom_call_target="tpu_custom_call" | custom-call | flops 12000000 | bytes 20000000 | tf_op jit(solution)/shard_map/maxsim/pallas_call | solution.py:251
  48.0 6.6 %all-to-all-start = ((f32[128,1,128]{2,1,0:T(1,128)}), f32[128,1,128]{2,1,0:T(1,128)S(1)}, u32[]{:S(2)}, u32[]{:S(2)}) async-start(f32[128,1,128]{2,1,0:T(1,128)} %bitcast.24), calls=%async_computation | async-start | bytes 131072 | tf_op jit(solution)/shard_map/all_to_all | solution.py:362
  54.6 0.0 copy-done.4
  54.6 0.0 copy-start.2
  54.6 5.8 %convolution_reduce_fusion = f32[32,8192]{1,0:T(8,128)} fusion(bf16[8192,128]{1,0:T(8,128)(2,1)S(1)} %copy-done.4, bf16[32,32,128]{2,0,1:T(8,128)(2,1)S(1)} %maximum_bitcast_fusion), kind=kOutput, calls=%fused_computation | convolution fusion | flops 2155610112 | bytes 3407872 | tf_op jit(solution)/shard_map/dot_general | solution.py:328
  60.4 3.8 %all-to-all-done = f32[128,1,128]{2,1,0:T(1,128)S(1)} async-done(((f32[128,1,128]{2,1,0:T(1,128)}), f32[128,1,128]{2,1,0:T(1,128)S(1)}, u32[]{:S(2)}, u32[]{:S(2)}) %all-to-all-start) | async-done | bytes 65568 | tf_op jit(solution)/shard_map/all_to_all | solution.py:362
  64.2 0.0 copy-done.2
  64.2 0.9 %final.1 = f32[8,32]{1,0:T(8,128)} custom-call(s32[8,32]{1,0:T(8,128)S(1)} %bitcast.48, f32[128,128]{1,0:T(8,128)S(1)} %bitcast.45), custom_call_target="tpu_custom_call" | custom-call | tf_op jit(solution)/shard_map/final/pallas_call | solution.py:316
  (9 shorter events, 0.2 us)
Async XLA Ops:
  1.3 0.8 %copy-start.1 = (bf16[32,4,128]{2,1,0:T(4,128)(2,1)S(1)}, bf16[32,4,128]{2,1,0:T(4,128)(2,1)}, u32[]{:S(2)}) copy-start(bf16[32,4,128]{2,1,0:T(4,128)(2,1)} %query_ref.1) | copy-start | bytes 98308
  2.2 4.5 %collective-permute-start.2 = (bf16[33,4,128]{2,1,0:T(4,128)(2,1)S(1)}, bf16[33,4,128]{2,1,0:T(4,128)(2,1)S(1)}, u32[]{:S(2)}, u32[]{:S(2)}) collective-permute-start(bf16[33,4,128]{2,1,0:T(4,128)(2,1)S(1)} %pack.1), channel_id=1, source_target_pairs={{0,96},{1,97},{2,98},{3,99},{4,100},{5,101},{6,102},{7,103},{8,104... | collective-permute-start | bytes 101384 | tf_op jit(solution)/shard_map/ppermute | solution.py:29
  5.6 4.3 %collective-permute-start.1 = (bf16[33,4,128]{2,1,0:T(4,128)(2,1)S(1)}, bf16[33,4,128]{2,1,0:T(4,128)(2,1)S(1)}, u32[]{:S(2)}, u32[]{:S(2)}) collective-permute-start(bf16[33,4,128]{2,1,0:T(4,128)(2,1)S(1)} %pack.1), channel_id=1, source_target_pairs={{0,64},{1,65},{2,66},{3,67},{4,68},{5,69},{6,70},{7,71},{8,72},{9,... | collective-permute-start | bytes 101384 | tf_op jit(solution)/shard_map/ppermute | solution.py:29
  6.1 4.1 %collective-permute-start = (bf16[33,4,128]{2,1,0:T(4,128)(2,1)S(1)}, bf16[33,4,128]{2,1,0:T(4,128)(2,1)S(1)}, u32[]{:S(2)}, u32[]{:S(2)}) collective-permute-start(bf16[33,4,128]{2,1,0:T(4,128)(2,1)S(1)} %pack.1), channel_id=1, source_target_pairs={{0,32},{1,33},{2,34},{3,35},{4,36},{5,37},{6,38},{7,39},{8,40},{9,... | collective-permute-start | bytes 101384 | tf_op jit(solution)/shard_map/ppermute | solution.py:29
  10.4 6.2 %collective-permute-start.3 = (bf16[33,16,128]{2,1,0:T(8,128)(2,1)S(1)}, bf16[33,16,128]{2,1,0:T(8,128)(2,1)S(1)}, u32[]{:S(2)}, u32[]{:S(2)}) collective-permute-start(bf16[33,16,128]{2,1,0:T(8,128)(2,1)S(1)} %bitcast.49), channel_id=1, source_target_pairs={{0,4},{1,5},{2,6},{3,7},{4,8},{5,9},{6,10},{7,11},{8,12},{9,13},{1... | collective-permute-start | bytes 405512 | tf_op jit(solution)/shard_map/ppermute | solution.py:29
  12.1 7.1 %collective-permute-start.4 = (bf16[33,16,128]{2,1,0:T(8,128)(2,1)S(1)}, bf16[33,16,128]{2,1,0:T(8,128)(2,1)S(1)}, u32[]{:S(2)}, u32[]{:S(2)}) collective-permute-start(bf16[33,16,128]{2,1,0:T(8,128)(2,1)S(1)} %bitcast.50), channel_id=1, source_target_pairs={{0,8},{1,9},{2,10},{3,11},{4,12},{5,13},{6,14},{7,15},{8,0},{9,1},... | collective-permute-start | bytes 405512 | tf_op jit(solution)/shard_map/ppermute | solution.py:29
  15.4 3.9 %collective-permute-start.5 = (bf16[33,16,128]{2,1,0:T(8,128)(2,1)S(1)}, bf16[33,16,128]{2,1,0:T(8,128)(2,1)S(1)}, u32[]{:S(2)}, u32[]{:S(2)}) collective-permute-start(bf16[33,16,128]{2,1,0:T(8,128)(2,1)S(1)} %bitcast.51), channel_id=1, source_target_pairs={{0,12},{1,13},{2,14},{3,15},{4,0},{5,1},{6,2},{7,3},{8,4},{9,5},{1... | collective-permute-start | bytes 405512 | tf_op jit(solution)/shard_map/ppermute | solution.py:29
  19.3 16.3 %collective-permute-start.6 = (bf16[4,33,16,128]{3,2,1,0:T(8,128)(2,1)S(1)}, bf16[4,33,16,128]{3,2,1,0:T(8,128)(2,1)S(1)}, u32[]{:S(2)}, u32[]{:S(2)}) collective-permute-start(bf16[4,33,16,128]{3,2,1,0:T(8,128)(2,1)S(1)} %pad_maximum_fusion), channel_id=1, source_target_pairs={{0,1},{1,2},{2,3},{3,0},{4,5},{5,6},{6,7},{7,4},{8,9},{9,10},{10,1... | collective-permute-start | bytes 1622024 | tf_op jit(solution)/shard_map/ppermute | solution.py:29
  21.0 14.8 %collective-permute-start.7 = (bf16[4,33,16,128]{3,2,1,0:T(8,128)(2,1)S(1)}, bf16[4,33,16,128]{3,2,1,0:T(8,128)(2,1)S(1)}, u32[]{:S(2)}, u32[]{:S(2)}) collective-permute-start(bf16[4,33,16,128]{3,2,1,0:T(8,128)(2,1)S(1)} %pad_maximum_fusion), channel_id=1, source_target_pairs={{0,3},{1,0},{2,1},{3,2},{4,7},{5,4},{6,5},{7,6},{8,11},{9,8},{10,9... | collective-permute-start | bytes 1622024 | tf_op jit(solution)/shard_map/ppermute | solution.py:29
  22.2 17.1 %collective-permute-start.8 = (bf16[4,33,16,128]{3,2,1,0:T(8,128)(2,1)S(1)}, bf16[4,33,16,128]{3,2,1,0:T(8,128)(2,1)S(1)}, u32[]{:S(2)}, u32[]{:S(2)}) collective-permute-start(bf16[4,33,16,128]{3,2,1,0:T(8,128)(2,1)S(1)} %pad_maximum_fusion), channel_id=1, source_target_pairs={{0,2},{1,3},{2,0},{3,1},{4,6},{5,7},{6,4},{7,5},{8,10},{9,11},{10,... | collective-permute-start | bytes 1622024 | tf_op jit(solution)/shard_map/ppermute | solution.py:29
  24.1 17.1 %collective-permute-start.9 = (bf16[4,33,16,128]{3,2,1,0:T(8,128)(2,1)S(1)}, bf16[4,33,16,128]{3,2,1,0:T(8,128)(2,1)S(1)}, u32[]{:S(2)}, u32[]{:S(2)}) collective-permute-start(bf16[4,33,16,128]{3,2,1,0:T(8,128)(2,1)S(1)} %pad_maximum_fusion), channel_id=1, source_target_pairs={{0,16},{1,17},{2,18},{3,19},{4,20},{5,21},{6,22},{7,23},{8,24},{9,... | collective-permute-start | bytes 1622024 | tf_op jit(solution)/shard_map/ppermute | solution.py:29
  35.7 6.1 %collective-permute-start.10 = (bf16[4,33,16,128]{3,2,1,0:T(8,128)(2,1)S(1)}, bf16[4,33,16,128]{3,2,1,0:T(8,128)(2,1)S(1)}, u32[]{:S(2)}, u32[]{:S(2)}) collective-permute-start(bf16[4,33,16,128]{3,2,1,0:T(8,128)(2,1)S(1)} %collective-permute-done.6), channel_id=1, source_target_pairs={{0,16},{1,17},{2,18},{3,19},{4,20},{5,21},{6,22},{7,23},{8,24},{9,... | collective-permute-start | bytes 1622024 | tf_op jit(solution)/shard_map/ppermute | solution.py:29
  35.8 6.1 %collective-permute-start.11 = (bf16[4,33,16,128]{3,2,1,0:T(8,128)(2,1)S(1)}, bf16[4,33,16,128]{3,2,1,0:T(8,128)(2,1)S(1)}, u32[]{:S(2)}, u32[]{:S(2)}) collective-permute-start(bf16[4,33,16,128]{3,2,1,0:T(8,128)(2,1)S(1)} %collective-permute-done.7), channel_id=1, source_target_pairs={{0,16},{1,17},{2,18},{3,19},{4,20},{5,21},{6,22},{7,23},{8,24},{9,... | collective-permute-start | bytes 1622024 | tf_op jit(solution)/shard_map/ppermute | solution.py:29
  39.3 3.4 %collective-permute-start.12 = (bf16[4,33,16,128]{3,2,1,0:T(8,128)(2,1)S(1)}, bf16[4,33,16,128]{3,2,1,0:T(8,128)(2,1)S(1)}, u32[]{:S(2)}, u32[]{:S(2)}) collective-permute-start(bf16[4,33,16,128]{3,2,1,0:T(8,128)(2,1)S(1)} %collective-permute-done.8), channel_id=1, source_target_pairs={{0,16},{1,17},{2,18},{3,19},{4,20},{5,21},{6,22},{7,23},{8,24},{9,... | collective-permute-start | bytes 1622024 | tf_op jit(solution)/shard_map/ppermute | solution.py:29
  41.6 1.2 %copy-start = (bf16[32,128,128]{2,1,0:T(8,128)(2,1)S(1)}, bf16[32,128,128]{2,1,0:T(8,128)(2,1)}, u32[]{:S(2)}) copy-start(bf16[32,128,128]{2,1,0:T(8,128)(2,1)} %rebuild.1.held_ref) | copy-start | bytes 3145732
  41.7 1.2 %copy-start.3 = (s32[32]{0:T(128)S(1)}, s32[32]{0:T(128)}, u32[]{:S(2)}) copy-start(s32[32]{0:T(128)} %lengths_ref.1) | copy-start | bytes 388
  42.9 11.7 %copy-start.4 = (bf16[8192,128]{1,0:T(8,128)(2,1)S(1)}, bf16[8192,128]{1,0:T(8,128)(2,1)}, u32[]{:S(2)}) copy-start(bf16[8192,128]{1,0:T(8,128)(2,1)} %cent_ref.1) | copy-start | bytes 6291460
  48.0 16.1 %all-to-all-start = ((f32[128,1,128]{2,1,0:T(1,128)}), f32[128,1,128]{2,1,0:T(1,128)S(1)}, u32[]{:S(2)}, u32[]{:S(2)}) async-start(f32[128,1,128]{2,1,0:T(1,128)} %bitcast.24), calls=%async_computation | async-start | bytes 131072 | tf_op jit(solution)/shard_map/all_to_all | solution.py:362
  54.6 9.6 %copy-start.2 = (s32[1,32,8]{1,2,0:T(8,128)S(1)}, s32[1,32,8]{1,2,0:T(8,128)}, u32[]{:S(2)}) copy-start(s32[1,32,8]{1,2,0:T(8,128)} %param.14) | copy-start | bytes 3076

commit v5 on v4

--- a/solution.py
+++ b/solution.py
@@ -198,7 +198,7 @@
 
 
 def maxsim_kernel(
-    where_ref, lengths_ref, own_ref, other_ref, held_ref, out_ref, meta, table, work, best, sem
+    where_ref, own_ref, other_ref, held_ref, out_ref, meta, table, work, best, sem
 ):
     item, goal, all_chunks = request_list(where_ref, own_ref, other_ref, meta)
     for i in range(PLACES // 128):
@@ -226,7 +226,7 @@
             (((1,), (1,)), ((), ())),
             preferred_element_type=jnp.float32,
         )
-        kept = jnp.where(slots_id < lengths_ref[block], inner, -1e30)
+        kept = jnp.where(slots_id < where_ref[5 + block], inner, -1e30)
         return jnp.max(kept, axis=0, keepdims=True)
 
     def steps(step, carry):
@@ -251,7 +251,7 @@
     return pl.pallas_call(
         maxsim_kernel,
         out_shape=jax.ShapeDtypeStruct((DEVICES, 128), jnp.float32),
-        in_specs=[pl.BlockSpec(memory_space=SMEM)] * 2 + [pl.BlockSpec(memory_space=VMEM)] * 3,
+        in_specs=[pl.BlockSpec(memory_space=SMEM)] + [pl.BlockSpec(memory_space=VMEM)] * 3,
         out_specs=pl.BlockSpec(memory_space=VMEM),
         scratch_shapes=[
             VMEM((DEVICES * 4, 128), jnp.float32),
@@ -263,7 +263,7 @@
         compiler_params=pltpu.CompilerParams(vmem_limit_bytes=32 << 20),
         cost_estimate=pl.CostEstimate(flops=12000000, bytes_accessed=20000000, transcendentals=0),
         name="maxsim",
-    )(where, lengths, own, other, held)
+    )(jnp.concatenate([where, lengths]), own, other, held)
 
 
 def pack_kernel(query_ref, ask_ref, out_ref):

time: 65.7 us -> 65.5 us (level)
  waiting for transfers between devices: 11 us -> 10.3 us
    concatenate x0 -> x1, local copies, waits for them, and re-layouts: none -> 0.73 us  [maxsim(): jnp.concatenate([where, lengths])]
  transfers between devices with their start and end apart: 14 -> 14, of which waited for: 6 -> 5; matrix products, arithmetic and copies ran while one was open for 11% -> 12% of each run, Pallas kernels for 10% -> 10%
where the time goes in v5:
time: 65.5 us; the launch traced here: 65 us
  starting transfers between devices  31.1 us (47%)
  Pallas kernels  12.8 us (20%)
  waiting for transfers between devices  10.3 us (16%)
  matrix products  5.77 us (9%)
  local copies, waits for them, and re-layouts  3.16 us (5%)
  other arithmetic  0.92 us (1%)
  between operations  0.85 us (1%)
    ppermute x13, starting transfers between devices, moved(): return lax.ppermute(value, AXES, pairs)  24.6 us
    pallas_call x1, Pallas kernels, rebuild(): pl.pallas_call(rebuild_kernel, grid=(REBUILD_STEPS,), out_shape=jax.Shape...  6.76 us
    all_to_all x1, starting transfers between devices, per_device(): lax.all_to_all(outgoing, AXES, split_axis=0, concat_axis=0, tiled=True)  6.56 us
    ppermute x13, waiting for transfers between devices, moved(): return lax.ppermute(value, AXES, pairs)  6.56 us
    dot_general x1, matrix products, relevance_of(): lax.dot_general(tokens.reshape(token_count * query_rows, width), centroid...  5.77 us
    pallas_call x1, Pallas kernels, maxsim(): pl.pallas_call(maxsim_kernel, out_shape=jax.ShapeDtypeStruct((DEVICES, 12...  5.15 us
    all_to_all x1, waiting for transfers between devices, per_device(): lax.all_to_all(outgoing, AXES, split_axis=0, concat_axis=0, tiled=True)  3.77 us
  transfers between devices with their start and end apart: 14, of which 5 were waited for; matrix products, arithmetic and copies ran while one was open for 12% of the time, Pallas kernels for 10%

profile of v5, /device:TPU:1, one launch (start us, length us, event | category | flops | bytes accessed | tf_op | source)
XLA Modules:
  0.0 65.0 jit_solution(14470149029615436790)
XLA Ops:
  0.6 0.7 %add_convert_fusion.ask_ref = f32[16,32]{1,0:T(8,128)S(1)} fusion(s32[8,32]{1,0:T(8,128)} %bitcast.64, s32[8,32]{1,0:T(8,128)} %bitcast.47), kind=kLoop, calls=%fused_computation.14 | loop fusion | flops 1024 | bytes 4096 | tf_op jit(solution)/shard_map/convert_element_type | solution.py:340
  1.3 0.0 copy-start.1
  1.3 0.8 %copy-done.1 = bf16[32,4,128]{2,1,0:T(4,128)(2,1)S(1)} copy-done((bf16[32,4,128]{2,1,0:T(4,128)(2,1)S(1)}, bf16[32,4,128]{2,1,0:T(4,128)(2,1)}, u32[]{:S(2)}) %copy-start.1) | copy-done | bytes 32792
  2.1 0.1 pack.1
  2.2 3.4 %collective-permute-start.2 = (bf16[33,4,128]{2,1,0:T(4,128)(2,1)S(1)}, bf16[33,4,128]{2,1,0:T(4,128)(2,1)S(1)}, u32[]{:S(2)}, u32[]{:S(2)}) collective-permute-start(bf16[33,4,128]{2,1,0:T(4,128)(2,1)S(1)} %pack.1), channel_id=1, source_target_pairs={{0,96},{1,97},{2,98},{3,99},{4,100},{5,101},{6,102},{7,103},{8,104... | collective-permute-start | bytes 101384 | tf_op jit(solution)/shard_map/ppermute | solution.py:29
  5.6 0.5 collective-permute-start.1
  6.1 0.6 collective-permute-start
  6.7 0.0 collective-permute-done.2
  6.7 3.2 %collective-permute-done.1 = bf16[33,4,128]{2,1,0:T(4,128)(2,1)S(1)} collective-permute-done((bf16[33,4,128]{2,1,0:T(4,128)(2,1)S(1)}, bf16[33,4,128]{2,1,0:T(4,128)(2,1)S(1)}, u32[]{:S(2)}, u32[]{:S(2)}) %collective-permute-start.1) | collective-permute-done | bytes 33824 | tf_op jit(solution)/shard_map/ppermute | solution.py:29
  9.8 0.4 collective-permute-done
  10.2 0.1 pad_maximum_fusion.1
  10.4 1.7 %collective-permute-start.3 = (bf16[33,16,128]{2,1,0:T(8,128)(2,1)S(1)}, bf16[33,16,128]{2,1,0:T(8,128)(2,1)S(1)}, u32[]{:S(2)}, u32[]{:S(2)}) collective-permute-start(bf16[33,16,128]{2,1,0:T(8,128)(2,1)S(1)} %bitcast.49), channel_id=1, source_target_pairs={{0,4},{1,5},{2,6},{3,7},{4,8},{5,9},{6,10},{7,11},{8,12},{9,13},{1... | collective-permute-start | bytes 405512 | tf_op jit(solution)/shard_map/ppermute | solution.py:29
  12.1 3.3 %collective-permute-start.4 = (bf16[33,16,128]{2,1,0:T(8,128)(2,1)S(1)}, bf16[33,16,128]{2,1,0:T(8,128)(2,1)S(1)}, u32[]{:S(2)}, u32[]{:S(2)}) collective-permute-start(bf16[33,16,128]{2,1,0:T(8,128)(2,1)S(1)} %bitcast.50), channel_id=1, source_target_pairs={{0,8},{1,9},{2,10},{3,11},{4,12},{5,13},{6,14},{7,15},{8,0},{9,1},... | collective-permute-start | bytes 405512 | tf_op jit(solution)/shard_map/ppermute | solution.py:29
  15.4 0.7 %collective-permute-start.5 = (bf16[33,16,128]{2,1,0:T(8,128)(2,1)S(1)}, bf16[33,16,128]{2,1,0:T(8,128)(2,1)S(1)}, u32[]{:S(2)}, u32[]{:S(2)}) collective-permute-start(bf16[33,16,128]{2,1,0:T(8,128)(2,1)S(1)} %bitcast.51), channel_id=1, source_target_pairs={{0,12},{1,13},{2,14},{3,15},{4,0},{5,1},{6,2},{7,3},{8,4},{9,5},{1... | collective-permute-start | bytes 405512 | tf_op jit(solution)/shard_map/ppermute | solution.py:29
  16.1 0.7 %concatenate.13.where_ref = s32[37]{0:T(128)S(1)} concatenate(s32[1]{0:T(128)} %bitcast.2, s32[1]{0:T(128)} %bitcast.3, s32[1]{0:T(128)} %bitcast.4, s32[1]{0:T(128)} %bitcast.5, s32[1]{0:T(128)} %bitcast.6, s32[32]{0:T(128)} %param.13), dimensions={0} | concatenate | bytes 296 | tf_op jit(solution)/shard_map/concatenate | solution.py:266
  17.0 0.0 collective-permute-done.3
  17.0 2.2 %collective-permute-done.4 = bf16[33,16,128]{2,1,0:T(8,128)(2,1)S(1)} collective-permute-done((bf16[33,16,128]{2,1,0:T(8,128)(2,1)S(1)}, bf16[33,16,128]{2,1,0:T(8,128)(2,1)S(1)}, u32[]{:S(2)}, u32[]{:S(2)}) %collective-permute-start.4) | collective-permute-done | bytes 135200 | tf_op jit(solution)/shard_map/ppermute | solution.py:29
  19.2 0.0 collective-permute-done.5
  19.2 0.1 pad_maximum_fusion
  19.3 1.7 %collective-permute-start.6 = (bf16[4,33,16,128]{3,2,1,0:T(8,128)(2,1)S(1)}, bf16[4,33,16,128]{3,2,1,0:T(8,128)(2,1)S(1)}, u32[]{:S(2)}, u32[]{:S(2)}) collective-permute-start(bf16[4,33,16,128]{3,2,1,0:T(8,128)(2,1)S(1)} %pad_maximum_fusion), channel_id=1, source_target_pairs={{0,1},{1,2},{2,3},{3,0},{4,5},{5,6},{6,7},{7,4},{8,9},{9,10},{10,1... | collective-permute-start | bytes 1622024 | tf_op jit(solution)/shard_map/ppermute | solution.py:29
  21.0 1.2 %collective-permute-start.7 = (bf16[4,33,16,128]{3,2,1,0:T(8,128)(2,1)S(1)}, bf16[4,33,16,128]{3,2,1,0:T(8,128)(2,1)S(1)}, u32[]{:S(2)}, u32[]{:S(2)}) collective-permute-start(bf16[4,33,16,128]{3,2,1,0:T(8,128)(2,1)S(1)} %pad_maximum_fusion), channel_id=1, source_target_pairs={{0,3},{1,0},{2,1},{3,2},{4,7},{5,4},{6,5},{7,6},{8,11},{9,8},{10,9... | collective-permute-start | bytes 1622024 | tf_op jit(solution)/shard_map/ppermute | solution.py:29
  22.2 1.9 %collective-permute-start.8 = (bf16[4,33,16,128]{3,2,1,0:T(8,128)(2,1)S(1)}, bf16[4,33,16,128]{3,2,1,0:T(8,128)(2,1)S(1)}, u32[]{:S(2)}, u32[]{:S(2)}) collective-permute-start(bf16[4,33,16,128]{3,2,1,0:T(8,128)(2,1)S(1)} %pad_maximum_fusion), channel_id=1, source_target_pairs={{0,2},{1,3},{2,0},{3,1},{4,6},{5,7},{6,4},{7,5},{8,10},{9,11},{10,... | collective-permute-start | bytes 1622024 | tf_op jit(solution)/shard_map/ppermute | solution.py:29
  24.1 4.2 %collective-permute-start.9 = (bf16[4,33,16,128]{3,2,1,0:T(8,128)(2,1)S(1)}, bf16[4,33,16,128]{3,2,1,0:T(8,128)(2,1)S(1)}, u32[]{:S(2)}, u32[]{:S(2)}) collective-permute-start(bf16[4,33,16,128]{3,2,1,0:T(8,128)(2,1)S(1)} %pad_maximum_fusion), channel_id=1, source_target_pairs={{0,16},{1,17},{2,18},{3,19},{4,20},{5,21},{6,22},{7,23},{8,24},{9,... | collective-permute-start | bytes 1622024 | tf_op jit(solution)/shard_map/ppermute | solution.py:29
  28.3 0.6 slice_bitcast_fusion.1._
  28.9 6.8 %rebuild.1.held_ref = bf16[32,128,128]{2,1,0:T(8,128)(2,1)} custom-call(s32[32,128]{1,0:T(8,128)} %ids_ref.1, bf16[8192,128]{1,0:T(8,128)(2,1)} %cent_ref.1, f32[32,1,128]{2,1,0:T(1,128)} %bitcast.62, bf16[32,128,128]{2,1,0:T(8,128)(2,1)} %code_ref.1, bf16[16,128]{1,0:T(8,128)(2,1)} %slice_bitcast_fusion.1._), custom_call_target="tpu_custom_call" | custom-call | flops 12000000 | bytes 20000000 | tf_op jit(solution)/shard_map/rebuild/pallas_call | solution.py:71
  35.7 0.0 collective-permute-done.6
  35.7 0.1 collective-permute-start.10
  35.8 0.0 collective-permute-done.7
  35.8 3.6 %collective-permute-start.11 = (bf16[4,33,16,128]{3,2,1,0:T(8,128)(2,1)S(1)}, bf16[4,33,16,128]{3,2,1,0:T(8,128)(2,1)S(1)}, u32[]{:S(2)}, u32[]{:S(2)}) collective-permute-start(bf16[4,33,16,128]{3,2,1,0:T(8,128)(2,1)S(1)} %collective-permute-done.7), channel_id=1, source_target_pairs={{0,16},{1,17},{2,18},{3,19},{4,20},{5,21},{6,22},{7,23},{8,24},{9,... | collective-permute-start | bytes 1622024 | tf_op jit(solution)/shard_map/ppermute | solution.py:29
  39.3 0.0 collective-permute-done.8
  39.3 1.8 %collective-permute-start.12 = (bf16[4,33,16,128]{3,2,1,0:T(8,128)(2,1)S(1)}, bf16[4,33,16,128]{3,2,1,0:T(8,128)(2,1)S(1)}, u32[]{:S(2)}, u32[]{:S(2)}) collective-permute-start(bf16[4,33,16,128]{3,2,1,0:T(8,128)(2,1)S(1)} %collective-permute-done.8), channel_id=1, source_target_pairs={{0,16},{1,17},{2,18},{3,19},{4,20},{5,21},{6,22},{7,23},{8,24},{9,... | collective-permute-start | bytes 1622024 | tf_op jit(solution)/shard_map/ppermute | solution.py:29
  41.1 0.1 constant_dynamic-update-slice_fusion.2
  41.2 0.0 collective-permute-done.9
  41.3 0.3 dynamic_update_slice.12
  41.6 0.1 constant_dynamic-update-slice_fusion.1
  41.6 0.0 copy-start
  41.7 0.1 constant_dynamic-update-slice_fusion
  41.7 0.0 collective-permute-done.10
  41.7 0.1 constant_dynamic-update-slice_fusion.9
  41.8 0.0 collective-permute-done.11
  41.8 0.1 constant_dynamic-update-slice_fusion.8
  41.9 0.8 %collective-permute-done.12 = bf16[4,33,16,128]{3,2,1,0:T(8,128)(2,1)S(1)} collective-permute-done((bf16[4,33,16,128]{3,2,1,0:T(8,128)(2,1)S(1)}, bf16[4,33,16,128]{3,2,1,0:T(8,128)(2,1)S(1)}, u32[]{:S(2)}, u32[]{:S(2)}) %collective-permute-start.12) | collective-permute-done | bytes 540704 | tf_op jit(solution)/shard_map/ppermute | solution.py:29
  42.7 0.1 constant_dynamic-update-slice_fusion.7
  42.8 0.1 copy-done
  42.9 0.0 copy-start.3
  42.9 5.1 %maxsim.1 = f32[128,128]{1,0:T(8,128)} custom-call(s32[37]{0:T(128)S(1)} %concatenate.13.where_ref, bf16[528,16,128]{2,1,0:T(8,128)(2,1)S(1)} %bitcast.44, bf16[528,16,128]{2,1,0:T(8,128)(2,1)S(1)} %bitcast.43, bf16[32,128,128]{2,1,0:T(8,128)(2,1)S(1)} %copy-done), custom_call_target="tpu_custom_call" | custom-call | flops 12000000 | bytes 20000000 | tf_op jit(solution)/shard_map/maxsim/pallas_call | solution.py:251
  48.0 6.6 %all-to-all-start = ((f32[128,1,128]{2,1,0:T(1,128)}), f32[128,1,128]{2,1,0:T(1,128)S(1)}, u32[]{:S(2)}, u32[]{:S(2)}) async-start(f32[128,1,128]{2,1,0:T(1,128)} %bitcast.24), calls=%async_computation | async-start | bytes 131072 | tf_op jit(solution)/shard_map/all_to_all | solution.py:362
  54.6 0.0 copy-done.3
  54.6 0.0 copy-start.2
  54.6 5.8 %convolution_reduce_fusion = f32[32,8192]{1,0:T(8,128)} fusion(bf16[8192,128]{1,0:T(8,128)(2,1)S(1)} %copy-done.3, bf16[32,32,128]{2,0,1:T(8,128)(2,1)S(1)} %maximum_bitcast_fusion), kind=kOutput, calls=%fused_computation | convolution fusion | flops 2155610112 | bytes 3407872 | tf_op jit(solution)/shard_map/dot_general | solution.py:328
  60.4 3.8 %all-to-all-done = f32[128,1,128]{2,1,0:T(1,128)S(1)} async-done(((f32[128,1,128]{2,1,0:T(1,128)}), f32[128,1,128]{2,1,0:T(1,128)S(1)}, u32[]{:S(2)}, u32[]{:S(2)}) %all-to-all-start) | async-done | bytes 65568 | tf_op jit(solution)/shard_map/all_to_all | solution.py:362
  64.2 0.0 copy-done.2
  64.2 0.9 %final.1 = f32[8,32]{1,0:T(8,128)} custom-call(s32[8,32]{1,0:T(8,128)S(1)} %bitcast.48, f32[128,128]{1,0:T(8,128)S(1)} %bitcast.45), custom_call_target="tpu_custom_call" | custom-call | tf_op jit(solution)/shard_map/final/pallas_call | solution.py:316
  (9 shorter events, 0.2 us)
Async XLA Ops:
  1.3 0.8 %copy-start.1 = (bf16[32,4,128]{2,1,0:T(4,128)(2,1)S(1)}, bf16[32,4,128]{2,1,0:T(4,128)(2,1)}, u32[]{:S(2)}) copy-start(bf16[32,4,128]{2,1,0:T(4,128)(2,1)} %query_ref.1) | copy-start | bytes 98308
  2.2 4.5 %collective-permute-start.2 = (bf16[33,4,128]{2,1,0:T(4,128)(2,1)S(1)}, bf16[33,4,128]{2,1,0:T(4,128)(2,1)S(1)}, u32[]{:S(2)}, u32[]{:S(2)}) collective-permute-start(bf16[33,4,128]{2,1,0:T(4,128)(2,1)S(1)} %pack.1), channel_id=1, source_target_pairs={{0,96},{1,97},{2,98},{3,99},{4,100},{5,101},{6,102},{7,103},{8,104... | collective-permute-start | bytes 101384 | tf_op jit(solution)/shard_map/ppermute | solution.py:29
  5.6 4.3 %collective-permute-start.1 = (bf16[33,4,128]{2,1,0:T(4,128)(2,1)S(1)}, bf16[33,4,128]{2,1,0:T(4,128)(2,1)S(1)}, u32[]{:S(2)}, u32[]{:S(2)}) collective-permute-start(bf16[33,4,128]{2,1,0:T(4,128)(2,1)S(1)} %pack.1), channel_id=1, source_target_pairs={{0,64},{1,65},{2,66},{3,67},{4,68},{5,69},{6,70},{7,71},{8,72},{9,... | collective-permute-start | bytes 101384 | tf_op jit(solution)/shard_map/ppermute | solution.py:29
  6.1 4.1 %collective-permute-start = (bf16[33,4,128]{2,1,0:T(4,128)(2,1)S(1)}, bf16[33,4,128]{2,1,0:T(4,128)(2,1)S(1)}, u32[]{:S(2)}, u32[]{:S(2)}) collective-permute-start(bf16[33,4,128]{2,1,0:T(4,128)(2,1)S(1)} %pack.1), channel_id=1, source_target_pairs={{0,32},{1,33},{2,34},{3,35},{4,36},{5,37},{6,38},{7,39},{8,40},{9,... | collective-permute-start | bytes 101384 | tf_op jit(solution)/shard_map/ppermute | solution.py:29
  10.4 6.6 %collective-permute-start.3 = (bf16[33,16,128]{2,1,0:T(8,128)(2,1)S(1)}, bf16[33,16,128]{2,1,0:T(8,128)(2,1)S(1)}, u32[]{:S(2)}, u32[]{:S(2)}) collective-permute-start(bf16[33,16,128]{2,1,0:T(8,128)(2,1)S(1)} %bitcast.49), channel_id=1, source_target_pairs={{0,4},{1,5},{2,6},{3,7},{4,8},{5,9},{6,10},{7,11},{8,12},{9,13},{1... | collective-permute-start | bytes 405512 | tf_op jit(solution)/shard_map/ppermute | solution.py:29
  12.1 7.1 %collective-permute-start.4 = (bf16[33,16,128]{2,1,0:T(8,128)(2,1)S(1)}, bf16[33,16,128]{2,1,0:T(8,128)(2,1)S(1)}, u32[]{:S(2)}, u32[]{:S(2)}) collective-permute-start(bf16[33,16,128]{2,1,0:T(8,128)(2,1)S(1)} %bitcast.50), channel_id=1, source_target_pairs={{0,8},{1,9},{2,10},{3,11},{4,12},{5,13},{6,14},{7,15},{8,0},{9,1},... | collective-permute-start | bytes 405512 | tf_op jit(solution)/shard_map/ppermute | solution.py:29
  15.4 3.9 %collective-permute-start.5 = (bf16[33,16,128]{2,1,0:T(8,128)(2,1)S(1)}, bf16[33,16,128]{2,1,0:T(8,128)(2,1)S(1)}, u32[]{:S(2)}, u32[]{:S(2)}) collective-permute-start(bf16[33,16,128]{2,1,0:T(8,128)(2,1)S(1)} %bitcast.51), channel_id=1, source_target_pairs={{0,12},{1,13},{2,14},{3,15},{4,0},{5,1},{6,2},{7,3},{8,4},{9,5},{1... | collective-permute-start | bytes 405512 | tf_op jit(solution)/shard_map/ppermute | solution.py:29
  19.3 16.3 %collective-permute-start.6 = (bf16[4,33,16,128]{3,2,1,0:T(8,128)(2,1)S(1)}, bf16[4,33,16,128]{3,2,1,0:T(8,128)(2,1)S(1)}, u32[]{:S(2)}, u32[]{:S(2)}) collective-permute-start(bf16[4,33,16,128]{3,2,1,0:T(8,128)(2,1)S(1)} %pad_maximum_fusion), channel_id=1, source_target_pairs={{0,1},{1,2},{2,3},{3,0},{4,5},{5,6},{6,7},{7,4},{8,9},{9,10},{10,1... | collective-permute-start | bytes 1622024 | tf_op jit(solution)/shard_map/ppermute | solution.py:29
  21.0 14.8 %collective-permute-start.7 = (bf16[4,33,16,128]{3,2,1,0:T(8,128)(2,1)S(1)}, bf16[4,33,16,128]{3,2,1,0:T(8,128)(2,1)S(1)}, u32[]{:S(2)}, u32[]{:S(2)}) collective-permute-start(bf16[4,33,16,128]{3,2,1,0:T(8,128)(2,1)S(1)} %pad_maximum_fusion), channel_id=1, source_target_pairs={{0,3},{1,0},{2,1},{3,2},{4,7},{5,4},{6,5},{7,6},{8,11},{9,8},{10,9... | collective-permute-start | bytes 1622024 | tf_op jit(solution)/shard_map/ppermute | solution.py:29
  22.2 17.1 %collective-permute-start.8 = (bf16[4,33,16,128]{3,2,1,0:T(8,128)(2,1)S(1)}, bf16[4,33,16,128]{3,2,1,0:T(8,128)(2,1)S(1)}, u32[]{:S(2)}, u32[]{:S(2)}) collective-permute-start(bf16[4,33,16,128]{3,2,1,0:T(8,128)(2,1)S(1)} %pad_maximum_fusion), channel_id=1, source_target_pairs={{0,2},{1,3},{2,0},{3,1},{4,6},{5,7},{6,4},{7,5},{8,10},{9,11},{10,... | collective-permute-start | bytes 1622024 | tf_op jit(solution)/shard_map/ppermute | solution.py:29
  24.1 17.1 %collective-permute-start.9 = (bf16[4,33,16,128]{3,2,1,0:T(8,128)(2,1)S(1)}, bf16[4,33,16,128]{3,2,1,0:T(8,128)(2,1)S(1)}, u32[]{:S(2)}, u32[]{:S(2)}) collective-permute-start(bf16[4,33,16,128]{3,2,1,0:T(8,128)(2,1)S(1)} %pad_maximum_fusion), channel_id=1, source_target_pairs={{0,16},{1,17},{2,18},{3,19},{4,20},{5,21},{6,22},{7,23},{8,24},{9,... | collective-permute-start | bytes 1622024 | tf_op jit(solution)/shard_map/ppermute | solution.py:29
  35.7 6.1 %collective-permute-start.10 = (bf16[4,33,16,128]{3,2,1,0:T(8,128)(2,1)S(1)}, bf16[4,33,16,128]{3,2,1,0:T(8,128)(2,1)S(1)}, u32[]{:S(2)}, u32[]{:S(2)}) collective-permute-start(bf16[4,33,16,128]{3,2,1,0:T(8,128)(2,1)S(1)} %collective-permute-done.6), channel_id=1, source_target_pairs={{0,16},{1,17},{2,18},{3,19},{4,20},{5,21},{6,22},{7,23},{8,24},{9,... | collective-permute-start | bytes 1622024 | tf_op jit(solution)/shard_map/ppermute | solution.py:29
  35.8 6.1 %collective-permute-start.11 = (bf16[4,33,16,128]{3,2,1,0:T(8,128)(2,1)S(1)}, bf16[4,33,16,128]{3,2,1,0:T(8,128)(2,1)S(1)}, u32[]{:S(2)}, u32[]{:S(2)}) collective-permute-start(bf16[4,33,16,128]{3,2,1,0:T(8,128)(2,1)S(1)} %collective-permute-done.7), channel_id=1, source_target_pairs={{0,16},{1,17},{2,18},{3,19},{4,20},{5,21},{6,22},{7,23},{8,24},{9,... | collective-permute-start | bytes 1622024 | tf_op jit(solution)/shard_map/ppermute | solution.py:29
  39.3 3.4 %collective-permute-start.12 = (bf16[4,33,16,128]{3,2,1,0:T(8,128)(2,1)S(1)}, bf16[4,33,16,128]{3,2,1,0:T(8,128)(2,1)S(1)}, u32[]{:S(2)}, u32[]{:S(2)}) collective-permute-start(bf16[4,33,16,128]{3,2,1,0:T(8,128)(2,1)S(1)} %collective-permute-done.8), channel_id=1, source_target_pairs={{0,16},{1,17},{2,18},{3,19},{4,20},{5,21},{6,22},{7,23},{8,24},{9,... | collective-permute-start | bytes 1622024 | tf_op jit(solution)/shard_map/ppermute | solution.py:29
  41.6 1.2 %copy-start = (bf16[32,128,128]{2,1,0:T(8,128)(2,1)S(1)}, bf16[32,128,128]{2,1,0:T(8,128)(2,1)}, u32[]{:S(2)}) copy-start(bf16[32,128,128]{2,1,0:T(8,128)(2,1)} %rebuild.1.held_ref) | copy-start | bytes 3145732
  42.9 11.7 %copy-start.3 = (bf16[8192,128]{1,0:T(8,128)(2,1)S(1)}, bf16[8192,128]{1,0:T(8,128)(2,1)}, u32[]{:S(2)}) copy-start(bf16[8192,128]{1,0:T(8,128)(2,1)} %cent_ref.1) | copy-start | bytes 6291460
  48.0 16.1 %all-to-all-start = ((f32[128,1,128]{2,1,0:T(1,128)}), f32[128,1,128]{2,1,0:T(1,128)S(1)}, u32[]{:S(2)}, u32[]{:S(2)}) async-start(f32[128,1,128]{2,1,0:T(1,128)} %bitcast.24), calls=%async_computation | async-start | bytes 131072 | tf_op jit(solution)/shard_map/all_to_all | solution.py:362
  54.6 9.6 %copy-start.2 = (s32[1,32,8]{1,2,0:T(8,128)S(1)}, s32[1,32,8]{1,2,0:T(8,128)}, u32[]{:S(2)}) copy-start(s32[1,32,8]{1,2,0:T(8,128)} %param.14) | copy-start | bytes 3076
